TPU v7x, 32 devices: a whole 2x2x4 slice. The times are simulated.
32 devices in a mesh: freq: 4 (over z), layer: 2 (over x), lat: 4 (over y, core).
Axes of the slice: x: 2, y: 2, z: 4, core: 2. Of those that a mesh axis runs over, the one named last changes fastest.
Arguments:
- source: float32 [2, 4, 2, 2, 512, 512], P(None, 'freq', None, 'layer', 'lat'), may hold values from -6 to 6
- contrast: float32 [2, 4, 2, 512, 512], P(None, 'freq', 'layer', 'lat'), may hold values from -0.5 to 0.5
- green: float32 [2, 4, 2, 2, 512, 512], P(None, 'freq', None, 'layer', 'lat'), may hold values from -0.6 to 0.6
- efield: float32 [2, 4, 2, 2, 512, 512], P(None, 'freq', None, 'layer', 'lat'), may hold values from -6 to 6
- cell_class: int32 [2, 512, 512], P('layer', 'lat'), may hold values from 0 to 7
Outputs:
- cell_gradient: float32 [2, 512, 512], P('layer', 'lat')
- class_gradient: float32 [2, 8], P('layer')
All inputs are finite; a program needn't handle non-finite values.
Results may differ from a plain program's by a relative error of at most 0.0001.
Values sent between devices are 32-bit elements; how exact they have to be, the bound alone decides.
No kernel may reach another device: no remote copies, remote signals or barrier semaphores. Data moves between devices by JAX's collectives and lax.ppermute only.
A program may use at most 64 MiB of HBM per device.

v0:
```python
import functools
import math

import jax
import jax.numpy as jnp
import ml_dtypes
import numpy as np
from jax import lax
from jax.experimental import pallas as pl
from jax.experimental.pallas import tpu as pltpu
from jax.sharding import PartitionSpec as P

NXY = 512
ITERS = 2
CLASSES = 8


highest = lax.Precision.HIGHEST


def tables(length):
    index = jnp.arange(length, dtype=jnp.int32)
    phase = index[:, None] * index[None, :] % length
    angle = phase.astype(jnp.float32) * (2.0 * math.pi / length)
    factor = 1.0 / math.sqrt(length)
    return (jnp.cos(angle) * factor, jnp.sin(angle) * factor)


def forward(field, cosine, sine):
    first = jnp.einsum("zfplxy,yk->zfplkx", field, cosine, precision=highest)
    second = jnp.einsum("zfplxy,yk->zfplkx", field, sine, precision=highest)
    partial_spec = jnp.stack([first[0] + second[1], first[1] - second[0]])
    turned = lax.all_to_all(partial_spec, "lat", split_axis=4, concat_axis=5, tiled=True)
    first = jnp.einsum("zfplkx,xq->zfplkq", turned, cosine, precision=highest)
    second = jnp.einsum("zfplkx,xq->zfplkq", turned, sine, precision=highest)
    return jnp.stack([first[0] + second[1], first[1] - second[0]])


def inverse(mixed, cosine, sine):
    first = jnp.einsum("lzfpkq,qx->zfplkx", mixed, cosine, precision=highest)
    second = jnp.einsum("lzfpkq,qx->zfplkx", mixed, sine, precision=highest)
    half_back = jnp.stack([first[0] - second[1], first[1] + second[0]])
    turned = lax.all_to_all(half_back, "lat", split_axis=5, concat_axis=4, tiled=True)
    first = jnp.einsum("zfplkx,ky->zfplxy", turned, cosine, precision=highest)
    second = jnp.einsum("zfplkx,ky->zfplxy", turned, sine, precision=highest)
    return jnp.stack([first[0] - second[1], first[1] + second[0]])


def couple_product(left, right):
    return jnp.einsum("foiyx,fpiyx->ofpyx", left, right, precision=highest)


def couple(kernel, spectra):
    real_part = couple_product(kernel[0], spectra[0]) - couple_product(kernel[1], spectra[1])
    imag_part = couple_product(kernel[0], spectra[1]) + couple_product(kernel[1], spectra[0])
    return jnp.stack([real_part, imag_part], axis=1)


def cmul(factor, field):
    return jnp.stack(
        [factor[0] * field[0] - factor[1] * field[1], factor[0] * field[1] + factor[1] * field[0]]
    )


def plain_device(source, contrast, green, efield, cell_class):
    cosine, sine = tables(source.shape[5])
    factor = contrast[:, :, None]
    field = source
    for step in range(ITERS):
        spectra = forward(cmul(factor, field), cosine, sine)
        mixed = lax.psum_scatter(couple(green, spectra), "layer", scatter_dimension=0, tiled=True)
        field = source + cmul(factor, inverse(mixed, cosine, sine))
    cell_terms = jnp.sum(efield[0] * field[0] - efield[1] * field[1], axis=(0, 1))
    cell = lax.psum(cell_terms, "freq")
    onehot = (cell_class[None] == jnp.arange(CLASSES, dtype=jnp.int32)[:, None, None, None]).astype(
        jnp.float32
    )
    local_sums = jnp.einsum("clxy,lxy->lc", onehot, cell_terms, precision=highest) / float(NXY)
    classes = lax.psum(local_sums, ("freq", "lat"))
    return (cell, classes)


VMEM_BYTES = 40 * 1024 * 1024
FIRST_VMEM_BYTES = 62 * 1024 * 1024
FINE = 16


def small_tables(length):
    index = np.arange(length)

    def waves(first):
        angle = (first[:, None] * index[None, :] % length) * (2.0 * np.pi / length)
        return np.stack([np.cos(angle), np.sin(angle)])

    both = [waves(index[::FINE]) / math.sqrt(length), waves(index[:FINE])]
    return np.concatenate(both, axis=1).astype(np.float32)


def halves(value):
    high = value.astype(jnp.bfloat16)
    return high, (value - high.astype(jnp.float32)).astype(jnp.bfloat16)


def product(left_high, left_low, right_high, right_low):
    def dot(left, right):
        return jnp.dot(left, right, preferred_element_type=jnp.float32)

    return dot(left_high, right_high) + (dot(left_high, right_low) + dot(left_low, right_high))


def along_y(real, imag, high_ref, low_ref, where, sign):
    rows = real.shape[0]
    high, low = halves(jnp.concatenate([real, imag], axis=0))
    got = product(high, low, high_ref[where], low_ref[where])
    width = got.shape[1] // 2
    out_real = got[:rows, :width] - sign * got[rows:, width:]
    out_imag = got[rows:, :width] + sign * got[:rows, width:]
    return out_real, out_imag


def along_x(high_ref, low_ref, where, high, low, sign):
    got = product(high_ref[where], low_ref[where], high, low)
    rows, width = got.shape[0] // 2, got.shape[1] // 2
    out_real = got[:rows, :width] - sign * got[rows:, width:]
    out_imag = got[:rows, width:] + sign * got[rows:, :width]
    return out_real, out_imag


def call(body, outs, args, specs, flops, scratch=(), after=(), vmem=VMEM_BYTES):
    sizes = sum(math.prod(o.shape) * 4 for o in outs)
    taken, tied = len(args), len(after)

    def ordered(*refs):
        body(*refs[:taken], *refs[taken + tied :])

    return pl.pallas_call(
        ordered,
        grid=(1,),
        out_shape=outs,
        in_specs=list(specs) + [pl.BlockSpec(memory_space=pl.ANY)] * tied,
        out_specs=[whole(o.shape) for o in outs],
        scratch_shapes=list(scratch),
        compiler_params=pltpu.CompilerParams(vmem_limit_bytes=vmem),
        cost_estimate=pl.CostEstimate(flops=flops, bytes_accessed=2 * sizes, transcendentals=0),
    )(*args, *after)


def whole(shape):
    return pl.BlockSpec(tuple(shape), lambda step: (0,) * len(shape))


def pick(shape, pol):
    return pl.BlockSpec((shape[0], 1) + tuple(shape[2:]), lambda step: (0, pol, 0, 0))


def f32(*shape):
    return jax.ShapeDtypeStruct(shape, jnp.float32)


def send(blocks, axis, size):
    got = [blocks[0]] + [None] * (size - 1)
    for d in sorted(range(1, size), key=lambda d: (d < 2, d)):
        got[d] = lax.ppermute(blocks[d], axis, [(i, i ^ d) for i in range(size)])
    return got


def make_tables(small, col_high, col_low, row_high=None, row_low=None):
    blocks, length, width = col_high.shape
    width = width // 2
    steps = length // FINE
    f_real, f_imag = small[0, steps:], small[1, steps:]
    for a in range(steps):
        c_real, c_imag = small[0, a : a + 1], small[1, a : a + 1]
        pair = (c_real * f_real - c_imag * f_imag, c_real * f_imag + c_imag * f_real)
        block, first = a * FINE // width, a * FINE % width
        for z, part in enumerate(pair):
            for value, row, col in zip(halves(part), (row_high, row_low), (col_high, col_low)):
                if row is not None:
                    row[block, z * width + first : z * width + first + FINE] = value
                for k in range(blocks):
                    spot = slice(a * FINE, (a + 1) * FINE)
                    col[k, spot, z * width : (z + 1) * width] = value[:, k * width : (k + 1) * width]


def forward_blocks(real, imag, high_ref, low_ref, out_refs):
    me = lax.axis_index("lat")
    for d, out in enumerate(out_refs):
        out[0], out[1] = along_y(real, imag, high_ref, low_ref, me ^ d, -1)


def weighted(contrast, real, imag):
    m_real, m_imag = contrast[0], contrast[1]
    return m_real * real - m_imag * imag, m_real * imag + m_imag * real


def first_body(lat, source, contrast, small, *refs):
    outs, (field, factor, waves, high, low, sems) = refs[:lat], refs[lat:]
    copies = [
        pltpu.make_async_copy(small, waves, sems.at[0]),
        pltpu.make_async_copy(source.at[:, 0], field, sems.at[1]),
        pltpu.make_async_copy(contrast, factor, sems.at[2]),
    ]
    for copy in copies:
        copy.start()
    copies[0].wait()
    make_tables(waves, high, low)
    copies[1].wait()
    copies[2].wait()
    real, imag = weighted(factor, field[0], field[1])
    forward_blocks(real, imag, high, low, outs)


def start_body(lat, source, contrast, high_ref, low_ref, *outs):
    real, imag = weighted(contrast, source[0, 0], source[1, 0])
    forward_blocks(real, imag, high_ref, low_ref, outs)


def turn_body(green, out):
    for z in range(green.shape[0]):
        for o in range(green.shape[1]):
            out[z, o] = green[z, o].T


def couple_body(lat, layers, *refs):
    parts, (green, high_ref, low_ref), rest = refs[:lat], refs[lat : lat + 3], refs[lat + 3 :]
    outs, (high, low) = rest[:layers], rest[layers:]
    me, layer = lax.axis_index("lat"), lax.axis_index("layer")
    rows, width = parts[0].shape[1:]
    for d, part in enumerate(parts):
        at = pl.ds(pl.multiple_of((me ^ d) * rows, rows), rows)
        for z in range(2):
            high[at, z * width : (z + 1) * width], low[at, z * width : (z + 1) * width] = halves(part[z])
    right_high, right_low = high[...], low[...]
    for k in range(high_ref.shape[0]):
        real, imag = along_x(high_ref, low_ref, k, right_high, right_low, -1)
        at = slice(k * rows, (k + 1) * rows)
        for e, out in enumerate(outs):
            g_real, g_imag = green[0, layer ^ e, at], green[1, layer ^ e, at]
            out[0, at] = g_real * real - g_imag * imag
            out[1, at] = g_real * imag + g_imag * real


def back_body(lat, layers, *refs):
    parts, (high_ref, low_ref), outs = refs[:layers], refs[layers : layers + 2], refs[layers + 2 :]
    me = lax.axis_index("lat")
    mixed = [sum((part[z] for part in parts[1:]), parts[0][z]) for z in range(2)]
    high, low = halves(jnp.concatenate(mixed, axis=1))
    for d, out in enumerate(outs):
        out[0], out[1] = along_x(high_ref, low_ref, me ^ d, high, low, +1)


def gather_lanes(parts, field):
    me = lax.axis_index("lat")
    width = parts[0].shape[2]
    for d, part in enumerate(parts):
        at = pl.ds(pl.multiple_of((me ^ d) * width, width), width)
        for z in range(2):
            field[z, :, at] = part[z]


def update(parts, source, contrast, high_ref, low_ref, field):
    gather_lanes(parts, field)
    back_real, back_imag = field[0], field[1]
    width = parts[0].shape[2]
    for k in range(high_ref.shape[0]):
        real, imag = along_y(back_real, back_imag, high_ref, low_ref, k, +1)
        at = slice(k * width, (k + 1) * width)
        m_real, m_imag = contrast[0, :, at], contrast[1, :, at]
        field[0, :, at] = source[0, 0, :, at] + (m_real * real - m_imag * imag)
        field[1, :, at] = source[1, 0, :, at] + (m_real * imag + m_imag * real)


def again_body(lat, *refs):
    parts, (source, contrast, high_ref, low_ref), rest = refs[:lat], refs[lat : lat + 4], refs[lat + 4 :]
    outs, field = rest[:-1], rest[-1]
    update(parts, source, contrast, high_ref, low_ref, field)
    real, imag = weighted(contrast, field[0], field[1])
    forward_blocks(real, imag, high_ref, low_ref, outs)


def terms_of(parts, source, contrast, efield, high_ref, low_ref, field):
    update(parts, source, contrast, high_ref, low_ref, field)
    return efield[0, 0] * field[0] - efield[1, 0] * field[1]


def end_body(lat, *refs):
    parts, (source, contrast, efield, high_ref, low_ref), rest = refs[:lat], refs[lat : lat + 5], refs[lat + 5 :]
    before, out, field = (rest[0] if len(rest) == 3 else None), rest[-2], rest[-1]
    terms = terms_of(parts, source, contrast, efield, high_ref, low_ref, field)
    out[...] = terms if before is None else before[...] + terms


def deal_body(lat, *refs):
    parts, (source, contrast, efield, high_ref, low_ref), rest = refs[:lat], refs[lat : lat + 5], refs[lat + 5 :]
    before, kinds, gone, kept, table, field, cell = rest
    cell[...] = before[...] + terms_of(parts, source, contrast, efield, high_ref, low_ref, field)
    bit = lax.axis_index("freq") & 1
    width = table.shape[1]
    rows = cell.shape[0] // 2
    for which, out in ((1 - bit, gone), (bit, kept)):
        block = cell[pl.ds(pl.multiple_of(which * rows, rows), rows)]
        for k in range(block.shape[1] // width):
            out[k * rows : (k + 1) * rows] = block[:, k * width : (k + 1) * width]
    lines = []
    for c in range(CLASSES):
        chosen = jnp.where(kinds[...] == c, cell[...], 0.0)
        lines.append(jnp.full((1, width), jnp.sum(chosen), jnp.float32))
    table[...] = jnp.concatenate(lines, axis=0)


def keep_body(one, two, *refs):
    tables, out = refs[:-1], refs[-1]
    rows = one.shape[0]
    out[:rows] = one[...] + two[...]
    out[rows:] = sum((table[...] for table in tables[1:]), tables[0][...])


def add_body(one, two, out):
    out[...] = one[...] + two[...]


def place_body(own, other, cell, classes):
    bit = lax.axis_index("freq") & 1
    width = own.shape[1]
    count = cell.shape[1] // width
    rows = cell.shape[0] // 2
    for which, ref in ((bit, own), (1 - bit, other)):
        at = pl.ds(pl.multiple_of(which * rows, rows), rows)
        for k in range(count):
            cell[at, k * width : (k + 1) * width] = ref[k * rows : (k + 1) * rows]
    total = own[count * rows :] + other[count * rows :]
    row = lax.broadcasted_iota(jnp.int32, total.shape, 0)
    lane = lax.broadcasted_iota(jnp.int32, total.shape, 1)
    line = jnp.sum(jnp.where(row == lane, total, 0.0), axis=0, keepdims=True)
    classes[...] = line[:, :CLASSES] / float(NXY)


def fast_device(sizes, source, contrast, green, efield, cell_class):
    freqs, layers, lat = sizes["freq"], sizes["layer"], sizes["lat"]
    pols, rows, length = source.shape[2], source.shape[4], source.shape[5]
    source = source.reshape(2, pols, rows, length)
    efield = efield.reshape(2, pols, rows, length)
    contrast = contrast.reshape(2, rows, length)
    green = green.reshape(2, layers, rows, length)
    kinds = cell_class.reshape(rows, length)
    col_shape, row_shape = (lat, length, 2 * rows), (lat, 2 * rows, length)
    table_specs, row_specs = [whole(col_shape)] * 2, [whole(row_shape)] * 2
    block = f32(2, rows, rows)
    spectrum = f32(2, length, rows)
    held = pltpu.VMEM((length, 2 * rows), jnp.bfloat16)
    full = pltpu.VMEM((2, rows, length), jnp.float32)
    stage_flops = 24 * rows * length * length
    last = pols - 1
    order = []

    def kernel(body, outs, args, specs, flops=stage_flops, scratch=(), vmem=VMEM_BYTES):
        got = call(body, outs, args, specs, flops, scratch, tuple(order[-1:]), vmem)
        order.append(got[0])
        return got

    small = jnp.asarray(small_tables(length))

    def first():
        specs = [pl.BlockSpec(memory_space=pltpu.HBM)] * 3
        scratch = [
            full,
            full,
            pltpu.VMEM(small.shape, jnp.float32),
            pltpu.VMEM(col_shape, jnp.bfloat16),
            pltpu.VMEM(col_shape, jnp.bfloat16),
            pltpu.SemaphoreType.DMA((3,)),
        ]
        body = functools.partial(first_body, lat)
        args = (source, contrast, small)
        return send(kernel(body, [block] * lat, args, specs, scratch=scratch, vmem=FIRST_VMEM_BYTES), "lat", lat)

    def start(p):
        specs = [pick(source.shape, p), whole(contrast.shape)] + table_specs
        return send(kernel(functools.partial(start_body, lat), [block] * lat, (source, contrast, *col), specs), "lat", lat)

    def couple(parts):
        body = functools.partial(couple_body, lat, layers)
        specs = [whole(block.shape)] * lat + [whole(turned.shape)] + row_specs
        got = kernel(body, [spectrum] * layers, (*parts, turned, *row), specs, scratch=[held, held])
        return send(got, "layer", layers)

    def back(parts):
        body = functools.partial(back_body, lat, layers)
        specs = [whole(spectrum.shape)] * layers + row_specs
        return send(kernel(body, [block] * lat, (*parts, *row), specs), "lat", lat)

    def field_specs(p):
        return [whole(block.shape)] * lat + [pick(source.shape, p), whole(contrast.shape)]

    def again(p, parts):
        args = (*parts, source, contrast, *col)
        specs = field_specs(p) + table_specs
        got = kernel(functools.partial(again_body, lat), [block] * lat, args, specs, 2 * stage_flops, [full])
        return send(got, "lat", lat)

    def end(p, parts, cells):
        more = () if cells is None else (cells,)
        specs = field_specs(p) + [pick(efield.shape, p)] + table_specs + [whole((rows, length))] * len(more)
        args = (*parts, source, contrast, efield, *col, *more)
        return kernel(functools.partial(end_body, lat), [f32(rows, length)], args, specs, scratch=[full])[0]

    def deal(parts, cells):
        specs = field_specs(last) + [pick(efield.shape, last)] + table_specs + [whole((rows, length))] * 2
        args = (*parts, source, contrast, efield, *col, cells, kinds)
        outs = [f32(rows // 2 * (length // 128), 128)] * 2 + [f32(CLASSES, 128)]
        scratch = [full, pltpu.VMEM((rows, length), jnp.float32)]
        return kernel(functools.partial(deal_body, lat), outs, args, specs, scratch=scratch)

    def across(value, d):
        return lax.ppermute(value, "freq", [(i, i ^ d) for i in range(freqs)])

    def simple(body, shape, args):
        return kernel(body, [f32(*shape)], tuple(args), [whole(arg.shape) for arg in args], 1 << 16)[0]

    chains = [first()]
    tables = kernel(
        make_tables,
        [jax.ShapeDtypeStruct(shape, jnp.bfloat16) for shape in (col_shape,) * 2 + (row_shape,) * 2],
        (small,),
        [whole(small.shape)],
        1 << 20,
    )
    col, row = tuple(tables[:2]), tuple(tables[2:])
    chains += [start(p) for p in range(1, pols)]
    turned = kernel(turn_body, [f32(2, layers, length, rows)], (green,), [whole(green.shape)], 1 << 20)[0]
    chains = [couple(chain) for chain in chains]
    for step in range(ITERS - 1):
        turns = [None] * pols
        for p in range(pols):
            turns[p] = back(chains[p])
            if p > 0:
                chains[p - 1] = couple(turns[p - 1])
            turns[p] = again(p, turns[p])
        chains[last] = couple(turns[last])
    cells = jnp.zeros((rows, length), jnp.float32) if last == 0 else None
    for p in range(last):
        cells = end(p, back(chains[p]), cells)
    gone, kept, found = deal(back(chains[last]), cells)
    came = across(gone, 1)
    found = send([found] * lat, "lat", lat)
    kept = simple(keep_body, (kept.shape[0] + CLASSES, 128), [kept, came, *found])
    d = 2
    while d < freqs:
        kept = simple(add_body, kept.shape, [kept, across(kept, d)])
        d *= 2
    both = (kept, across(kept, 1))
    outs = [f32(rows, length), f32(1, CLASSES)]
    cell, classes = kernel(place_body, outs, both, [whole(part.shape) for part in both], 1 << 16)
    return cell.reshape(1, rows, length), classes


def solution(mesh):
    whole_lanes = (
        NXY % (mesh.shape["lat"] * 128) == 0
        and NXY % (mesh.shape["lat"] * 128) == 0
        and mesh.shape["freq"] > 1
        and all(mesh.shape[name] & (mesh.shape[name] - 1) == 0 for name in mesh.axis_names)
    )
    per_device = functools.partial(fast_device, dict(mesh.shape)) if whole_lanes else plain_device

    placed = (
        P(None, "freq", None, "layer", "lat", None),
        P(None, "freq", "layer", "lat", None),
        P(None, "freq", None, "layer", "lat", None),
        P(None, "freq", None, "layer", "lat", None),
        P("layer", "lat", None),
    )
    return jax.shard_map(
        per_device,
        mesh=mesh,
        in_specs=placed,
        out_specs=(P("layer", "lat", None), P("layer", None)),
        check_vma=False,
    )
```

profile of v0, /device:TPU:0, one launch (start us, length us, event | category | flops | bytes accessed | tf_op | source)
XLA Modules:
  0.0 112.6 jit_solution(7090862534733023357)
XLA Ops:
  0.7 3.4 %shard_map.77 = (f32[2,128,128]{2,1,0:T(8,128)}, f32[2,128,128]{2,1,0:T(8,128)}, f32[2,128,128]{2,1,0:T(8,128)}, f32[2,128,128]{2,1,0:T(8,128)}) custom-call(f32[2,2,128,512]{3,2,1,0:T(8,128)} %bitcast.6, f32[2,128,512]{2,1,0:T(8,128)} %bitcast.12, f32[2,48,512]{2,1,0:T(8,128)} %constant.2.clone.refs_2_.refs_0_), custom_call_target="tpu_custom_call" | custom-call | flops 805306368 | bytes 1048576 | tf_op jit(solution)/shard_map/pallas_call | solution.py:136
  4.6 2.6 %collective-permute-start.4 = (f32[2,128,128]{2,1,0:T(8,128)}, f32[2,128,128]{2,1,0:T(8,128)S(1)}, u32[]{:S(2)}, u32[]{:S(2)}) collective-permute-start(f32[2,128,128]{2,1,0:T(8,128)} %get-tuple-element.61), channel_id=1, source_target_pairs={{0,2},{1,3},{2,0},{3,1},{4,6},{5,7},{6,4},{7,5},{8,10},{9,11},{10,... | collective-permute-start | bytes 393224 | tf_op jit(solution)/shard_map/ppermute | solution.py:163
  11.7 2.3 %collective-permute-done.5.refs_3_ = f32[2,128,128]{2,1,0:T(8,128)S(1)} collective-permute-done((f32[2,128,128]{2,1,0:T(8,128)}, f32[2,128,128]{2,1,0:T(8,128)S(1)}, u32[]{:S(2)}, u32[]{:S(2)}) %collective-permute-start.5) | collective-permute-done | bytes 131104 | tf_op jit(solution)/shard_map/ppermute | solution.py:163
  15.1 1.6 %collective-permute-start.7 = (f32[2,512,128]{2,1,0:T(8,128)S(1)}, f32[2,512,128]{2,1,0:T(8,128)S(1)}, u32[]{:S(2)}, u32[]{:S(2)}) collective-permute-start(f32[2,512,128]{2,1,0:T(8,128)S(1)} %get-tuple-element.66), channel_id=1, source_target_pairs={{0,4},{4,0},{1,5},{5,1},{2,6},{6,2},{3,7},{7,3},{8,12},{12,8},{9,1... | collective-permute-start | bytes 1572872 | tf_op jit(solution)/shard_map/ppermute | solution.py:163
  16.7 1.5 %collective-permute-start.1 = (f32[2,128,128]{2,1,0:T(8,128)S(1)}, f32[2,128,128]{2,1,0:T(8,128)S(1)}, u32[]{:S(2)}, u32[]{:S(2)}) collective-permute-start(f32[2,128,128]{2,1,0:T(8,128)S(1)} %get-tuple-element.56), channel_id=1, source_target_pairs={{0,2},{1,3},{2,0},{3,1},{4,6},{5,7},{6,4},{7,5},{8,10},{9,11},{10,... | collective-permute-start | bytes 393224 | tf_op jit(solution)/shard_map/ppermute | solution.py:163
  18.6 4.4 %collective-permute-done.1.refs_2_ = f32[2,128,128]{2,1,0:T(8,128)S(1)} collective-permute-done((f32[2,128,128]{2,1,0:T(8,128)S(1)}, f32[2,128,128]{2,1,0:T(8,128)S(1)}, u32[]{:S(2)}, u32[]{:S(2)}) %collective-permute-start.1) | collective-permute-done | bytes 131104 | tf_op jit(solution)/shard_map/ppermute | solution.py:163
  23.0 2.0 %collective-permute-done.2.refs_3_ = f32[2,128,128]{2,1,0:T(8,128)S(1)} collective-permute-done((f32[2,128,128]{2,1,0:T(8,128)S(1)}, f32[2,128,128]{2,1,0:T(8,128)S(1)}, u32[]{:S(2)}, u32[]{:S(2)}) %collective-permute-start.2) | collective-permute-done | bytes 131104 | tf_op jit(solution)/shard_map/ppermute | solution.py:163
  26.7 2.4 %collective-permute-done.7.refs_1_ = f32[2,512,128]{2,1,0:T(8,128)S(1)} collective-permute-done((f32[2,512,128]{2,1,0:T(8,128)S(1)}, f32[2,512,128]{2,1,0:T(8,128)S(1)}, u32[]{:S(2)}, u32[]{:S(2)}) %collective-permute-start.7) | collective-permute-done | bytes 524320 | tf_op jit(solution)/shard_map/ppermute | solution.py:163
  30.2 1.8 %collective-permute-start.9 = (f32[2,128,128]{2,1,0:T(8,128)S(1)}, f32[2,128,128]{2,1,0:T(8,128)S(1)}, u32[]{:S(2)}, u32[]{:S(2)}) collective-permute-start(f32[2,128,128]{2,1,0:T(8,128)S(1)} %get-tuple-element.69), channel_id=1, source_target_pairs={{0,2},{1,3},{2,0},{3,1},{4,6},{5,7},{6,4},{7,5},{8,10},{9,11},{10,... | collective-permute-start | bytes 393224 | tf_op jit(solution)/shard_map/ppermute | solution.py:163
  32.0 4.5 %collective-permute-done.9.refs_2_ = f32[2,128,128]{2,1,0:T(8,128)S(1)} collective-permute-done((f32[2,128,128]{2,1,0:T(8,128)S(1)}, f32[2,128,128]{2,1,0:T(8,128)S(1)}, u32[]{:S(2)}, u32[]{:S(2)}) %collective-permute-start.9) | collective-permute-done | bytes 131104 | tf_op jit(solution)/shard_map/ppermute | solution.py:163
  36.5 1.9 %collective-permute-done.10.refs_3_ = f32[2,128,128]{2,1,0:T(8,128)S(1)} collective-permute-done((f32[2,128,128]{2,1,0:T(8,128)S(1)}, f32[2,128,128]{2,1,0:T(8,128)S(1)}, u32[]{:S(2)}, u32[]{:S(2)}) %collective-permute-start.10) | collective-permute-done | bytes 131104 | tf_op jit(solution)/shard_map/ppermute | solution.py:163
  38.4 1.9 %shard_map.84 = (f32[2,128,128]{2,1,0:T(8,128)S(1)}, f32[2,128,128]{2,1,0:T(8,128)S(1)}, f32[2,128,128]{2,1,0:T(8,128)S(1)}, f32[2,128,128]{2,1,0:T(8,128)S(1)}) custom-call(f32[2,128,128]{2,1,0:T(8,128)S(1)} %get-tuple-element.67.refs_0_.refs_8_, f32[2,128,128]{2,1,0:T(8,128)S(1)} %collective-permute-done.8.refs_1_, ...), custom_call_target="tpu_custom_call" | custom-call | flops 1610612736 | bytes 1048576 | tf_op jit(solution)/shard_map/pallas_call | solution.py:136
  41.0 1.7 %collective-permute-start.15 = (f32[2,128,128]{2,1,0:T(8,128)S(1)}, f32[2,128,128]{2,1,0:T(8,128)S(1)}, u32[]{:S(2)}, u32[]{:S(2)}) collective-permute-start(f32[2,128,128]{2,1,0:T(8,128)S(1)} %get-tuple-element.77), channel_id=1, source_target_pairs={{0,2},{1,3},{2,0},{3,1},{4,6},{5,7},{6,4},{7,5},{8,10},{9,11},{10,... | collective-permute-start | bytes 393224 | tf_op jit(solution)/shard_map/ppermute | solution.py:163
  44.2 1.7 %collective-permute-start.12 = (f32[2,128,128]{2,1,0:T(8,128)S(1)}, f32[2,128,128]{2,1,0:T(8,128)S(1)}, u32[]{:S(2)}, u32[]{:S(2)}) collective-permute-start(f32[2,128,128]{2,1,0:T(8,128)S(1)} %get-tuple-element.74), channel_id=1, source_target_pairs={{0,2},{1,3},{2,0},{3,1},{4,6},{5,7},{6,4},{7,5},{8,10},{9,11},{10,... | collective-permute-start | bytes 393224 | tf_op jit(solution)/shard_map/ppermute | solution.py:163
  47.2 2.2 %collective-permute-done.16.refs_3_ = f32[2,128,128]{2,1,0:T(8,128)S(1)} collective-permute-done((f32[2,128,128]{2,1,0:T(8,128)S(1)}, f32[2,128,128]{2,1,0:T(8,128)S(1)}, u32[]{:S(2)}, u32[]{:S(2)}) %collective-permute-start.16) | collective-permute-done | bytes 131104 | tf_op jit(solution)/shard_map/ppermute | solution.py:163
  50.5 2.2 %collective-permute-start.21 = (f32[2,512,128]{2,1,0:T(8,128)S(1)}, f32[2,512,128]{2,1,0:T(8,128)S(1)}, u32[]{:S(2)}, u32[]{:S(2)}) collective-permute-start(f32[2,512,128]{2,1,0:T(8,128)S(1)} %get-tuple-element.86), channel_id=1, source_target_pairs={{0,4},{4,0},{1,5},{5,1},{2,6},{6,2},{3,7},{7,3},{8,12},{12,8},{9,1... | collective-permute-start | bytes 1572872 | tf_op jit(solution)/shard_map/ppermute | solution.py:163
  54.2 1.9 %shard_map.87 = (f32[2,128,128]{2,1,0:T(8,128)S(1)}, f32[2,128,128]{2,1,0:T(8,128)S(1)}, f32[2,128,128]{2,1,0:T(8,128)S(1)}, f32[2,128,128]{2,1,0:T(8,128)S(1)}) custom-call(f32[2,128,128]{2,1,0:T(8,128)S(1)} %get-tuple-element.72.refs_7_.refs_0_, f32[2,128,128]{2,1,0:T(8,128)S(1)} %collective-permute-done.11.refs_1_, ...), custom_call_target="tpu_custom_call" | custom-call | flops 1610612736 | bytes 1048576 | tf_op jit(solution)/shard_map/pallas_call | solution.py:136
  57.1 1.7 %collective-permute-start.18 = (f32[2,128,128]{2,1,0:T(8,128)S(1)}, f32[2,128,128]{2,1,0:T(8,128)S(1)}, u32[]{:S(2)}, u32[]{:S(2)}) collective-permute-start(f32[2,128,128]{2,1,0:T(8,128)S(1)} %get-tuple-element.82), channel_id=1, source_target_pairs={{0,2},{1,3},{2,0},{3,1},{4,6},{5,7},{6,4},{7,5},{8,10},{9,11},{10,... | collective-permute-start | bytes 393224 | tf_op jit(solution)/shard_map/ppermute | solution.py:163
  58.8 4.5 %collective-permute-done.18.refs_2_ = f32[2,128,128]{2,1,0:T(8,128)S(1)} collective-permute-done((f32[2,128,128]{2,1,0:T(8,128)S(1)}, f32[2,128,128]{2,1,0:T(8,128)S(1)}, u32[]{:S(2)}, u32[]{:S(2)}) %collective-permute-start.18) | collective-permute-done | bytes 131104 | tf_op jit(solution)/shard_map/ppermute | solution.py:163
  65.7 2.3 %collective-permute-start.20 = (f32[2,512,128]{2,1,0:T(8,128)S(1)}, f32[2,512,128]{2,1,0:T(8,128)S(1)}, u32[]{:S(2)}, u32[]{:S(2)}) collective-permute-start(f32[2,512,128]{2,1,0:T(8,128)S(1)} %get-tuple-element.85), channel_id=1, source_target_pairs={{0,4},{4,0},{1,5},{5,1},{2,6},{6,2},{3,7},{7,3},{8,12},{12,8},{9,1... | collective-permute-start | bytes 1572872 | tf_op jit(solution)/shard_map/ppermute | solution.py:163
  69.6 1.5 %collective-permute-start.23 = (f32[2,128,128]{2,1,0:T(8,128)S(1)}, f32[2,128,128]{2,1,0:T(8,128)S(1)}, u32[]{:S(2)}, u32[]{:S(2)}) collective-permute-start(f32[2,128,128]{2,1,0:T(8,128)S(1)} %get-tuple-element.89), channel_id=1, source_target_pairs={{0,2},{1,3},{2,0},{3,1},{4,6},{5,7},{6,4},{7,5},{8,10},{9,11},{10,... | collective-permute-start | bytes 393224 | tf_op jit(solution)/shard_map/ppermute | solution.py:163
  71.2 4.8 %collective-permute-done.23.refs_2_ = f32[2,128,128]{2,1,0:T(8,128)S(1)} collective-permute-done((f32[2,128,128]{2,1,0:T(8,128)S(1)}, f32[2,128,128]{2,1,0:T(8,128)S(1)}, u32[]{:S(2)}, u32[]{:S(2)}) %collective-permute-start.23) | collective-permute-done | bytes 131104 | tf_op jit(solution)/shard_map/ppermute | solution.py:163
  78.2 2.6 %collective-permute-done.20.refs_1_ = f32[2,512,128]{2,1,0:T(8,128)S(1)} collective-permute-done((f32[2,512,128]{2,1,0:T(8,128)S(1)}, f32[2,512,128]{2,1,0:T(8,128)S(1)}, u32[]{:S(2)}, u32[]{:S(2)}) %collective-permute-start.20) | collective-permute-done | bytes 524320 | tf_op jit(solution)/shard_map/ppermute | solution.py:163
  81.9 1.5 %collective-permute-start.26 = (f32[2,128,128]{2,1,0:T(8,128)S(1)}, f32[2,128,128]{2,1,0:T(8,128)S(1)}, u32[]{:S(2)}, u32[]{:S(2)}) collective-permute-start(f32[2,128,128]{2,1,0:T(8,128)S(1)} %get-tuple-element.93), channel_id=1, source_target_pairs={{0,2},{1,3},{2,0},{3,1},{4,6},{5,7},{6,4},{7,5},{8,10},{9,11},{10,... | collective-permute-start | bytes 393224 | tf_op jit(solution)/shard_map/ppermute | solution.py:163
  83.7 4.6 %collective-permute-done.26.refs_2_ = f32[2,128,128]{2,1,0:T(8,128)S(1)} collective-permute-done((f32[2,128,128]{2,1,0:T(8,128)S(1)}, f32[2,128,128]{2,1,0:T(8,128)S(1)}, u32[]{:S(2)}, u32[]{:S(2)}) %collective-permute-start.26) | collective-permute-done | bytes 131104 | tf_op jit(solution)/shard_map/ppermute | solution.py:163
  88.2 1.7 %collective-permute-done.27.refs_3_ = f32[2,128,128]{2,1,0:T(8,128)S(1)} collective-permute-done((f32[2,128,128]{2,1,0:T(8,128)S(1)}, f32[2,128,128]{2,1,0:T(8,128)S(1)}, u32[]{:S(2)}, u32[]{:S(2)}) %collective-permute-start.27) | collective-permute-done | bytes 131104 | tf_op jit(solution)/shard_map/ppermute | solution.py:163
  90.0 1.5 %shard_map.92 = (f32[256,128]{1,0:T(8,128)S(1)}, f32[256,128]{1,0:T(8,128)S(1)}, f32[8,128]{1,0:T(8,128)S(1)}) custom-call(f32[2,128,128]{2,1,0:T(8,128)S(1)} %get-tuple-element.91.refs_0_.refs_11_, f32[2,128,128]{2,1,0:T(8,128)S(1)} %collective-permute-done.25.refs_1_, f32[2,128,128]{2,1,0:T(8,128)S(1)} %collective-permute-done.26.refs_2_, ...), custom_call_target="tpu_custom_call" | custom-call | flops 805306368 | bytes 532480 | tf_op jit(solution)/shard_map/pallas_call | solution.py:136
  91.5 1.7 %collective-permute-start.28 = (f32[256,128]{1,0:T(8,128)S(1)}, f32[256,128]{1,0:T(8,128)S(1)}, u32[]{:S(2)}, u32[]{:S(2)}) collective-permute-start(f32[256,128]{1,0:T(8,128)S(1)} %get-tuple-element.96.refs_6_), channel_id=1, source_target_pairs={{0,8},{8,0},{16,24},{24,16},{1,9},{9,1},{17,25},{25,17},{2,10},{10... | collective-permute-start | bytes 393224 | tf_op jit(solution)/shard_map/ppermute | solution.py:415
  96.2 1.8 %collective-permute-done.30.refs_4_ = f32[8,128]{1,0:T(8,128)S(1)} collective-permute-done((f32[8,128]{1,0:T(8,128)S(1)}, f32[8,128]{1,0:T(8,128)S(1)}, u32[]{:S(2)}, u32[]{:S(2)}) %collective-permute-start.30) | collective-permute-done | bytes 4128 | tf_op jit(solution)/shard_map/ppermute | solution.py:163
  98.0 2.7 %collective-permute-start.32 = (f32[264,128]{1,0:T(8,128)S(1)}, f32[264,128]{1,0:T(8,128)S(1)}, u32[]{:S(2)}, u32[]{:S(2)}) collective-permute-start(f32[264,128]{1,0:T(8,128)S(1)} %shard_map.93.refs_0_.refs_2_), channel_id=1, source_target_pairs={{0,16},{8,24},{16,0},{24,8},{1,17},{9,25},{17,1},{25,9},{2,18},{10... | collective-permute-start | bytes 405512 | tf_op jit(solution)/shard_map/ppermute | solution.py:415
  100.6 6.2 %collective-permute-done.32.refs_1_ = f32[264,128]{1,0:T(8,128)S(1)} collective-permute-done((f32[264,128]{1,0:T(8,128)S(1)}, f32[264,128]{1,0:T(8,128)S(1)}, u32[]{:S(2)}, u32[]{:S(2)}) %collective-permute-start.32) | collective-permute-done | bytes 135200 | tf_op jit(solution)/shard_map/ppermute | solution.py:415
  107.1 4.8 %collective-permute-done.33.refs_1_ = f32[264,128]{1,0:T(8,128)S(1)} collective-permute-done((f32[264,128]{1,0:T(8,128)S(1)}, f32[264,128]{1,0:T(8,128)S(1)}, u32[]{:S(2)}, u32[]{:S(2)}) %collective-permute-start.33) | collective-permute-done | bytes 135200 | tf_op jit(solution)/shard_map/ppermute | solution.py:415
  (71 shorter events, 27.8 us)
Async XLA Ops:
  4.0 6.3 %collective-permute-start.3 = (f32[2,128,128]{2,1,0:T(8,128)}, f32[2,128,128]{2,1,0:T(8,128)S(1)}, u32[]{:S(2)}, u32[]{:S(2)}) collective-permute-start(f32[2,128,128]{2,1,0:T(8,128)} %get-tuple-element.60), channel_id=1, source_target_pairs={{0,1},{1,0},{2,3},{3,2},{4,5},{5,4},{6,7},{7,6},{8,9},{9,8},{10,11... | collective-permute-start | bytes 393224 | tf_op jit(solution)/shard_map/ppermute | solution.py:163
  4.6 7.2 %collective-permute-start.4 = (f32[2,128,128]{2,1,0:T(8,128)}, f32[2,128,128]{2,1,0:T(8,128)S(1)}, u32[]{:S(2)}, u32[]{:S(2)}) collective-permute-start(f32[2,128,128]{2,1,0:T(8,128)} %get-tuple-element.61), channel_id=1, source_target_pairs={{0,2},{1,3},{2,0},{3,1},{4,6},{5,7},{6,4},{7,5},{8,10},{9,11},{10,... | collective-permute-start | bytes 393224 | tf_op jit(solution)/shard_map/ppermute | solution.py:163
  7.1 6.8 %collective-permute-start.5 = (f32[2,128,128]{2,1,0:T(8,128)}, f32[2,128,128]{2,1,0:T(8,128)S(1)}, u32[]{:S(2)}, u32[]{:S(2)}) collective-permute-start(f32[2,128,128]{2,1,0:T(8,128)} %get-tuple-element.62), channel_id=1, source_target_pairs={{0,3},{1,2},{2,1},{3,0},{4,7},{5,6},{6,5},{7,4},{8,11},{9,10},{10,... | collective-permute-start | bytes 393224 | tf_op jit(solution)/shard_map/ppermute | solution.py:163
  15.1 14.0 %collective-permute-start.7 = (f32[2,512,128]{2,1,0:T(8,128)S(1)}, f32[2,512,128]{2,1,0:T(8,128)S(1)}, u32[]{:S(2)}, u32[]{:S(2)}) collective-permute-start(f32[2,512,128]{2,1,0:T(8,128)S(1)} %get-tuple-element.66), channel_id=1, source_target_pairs={{0,4},{4,0},{1,5},{5,1},{2,6},{6,2},{3,7},{7,3},{8,12},{12,8},{9,1... | collective-permute-start | bytes 1572872 | tf_op jit(solution)/shard_map/ppermute | solution.py:163
  16.7 6.3 %collective-permute-start.1 = (f32[2,128,128]{2,1,0:T(8,128)S(1)}, f32[2,128,128]{2,1,0:T(8,128)S(1)}, u32[]{:S(2)}, u32[]{:S(2)}) collective-permute-start(f32[2,128,128]{2,1,0:T(8,128)S(1)} %get-tuple-element.56), channel_id=1, source_target_pairs={{0,2},{1,3},{2,0},{3,1},{4,6},{5,7},{6,4},{7,5},{8,10},{9,11},{10,... | collective-permute-start | bytes 393224 | tf_op jit(solution)/shard_map/ppermute | solution.py:163
  18.2 6.8 %collective-permute-start.2 = (f32[2,128,128]{2,1,0:T(8,128)S(1)}, f32[2,128,128]{2,1,0:T(8,128)S(1)}, u32[]{:S(2)}, u32[]{:S(2)}) collective-permute-start(f32[2,128,128]{2,1,0:T(8,128)S(1)} %get-tuple-element.57), channel_id=1, source_target_pairs={{0,3},{1,2},{2,1},{3,0},{4,7},{5,6},{6,5},{7,4},{8,11},{9,10},{10,... | collective-permute-start | bytes 393224 | tf_op jit(solution)/shard_map/ppermute | solution.py:163
  26.1 16.6 %collective-permute-start.6 = (f32[2,512,128]{2,1,0:T(8,128)S(1)}, f32[2,512,128]{2,1,0:T(8,128)S(1)}, u32[]{:S(2)}, u32[]{:S(2)}) collective-permute-start(f32[2,512,128]{2,1,0:T(8,128)S(1)} %get-tuple-element.65), channel_id=1, source_target_pairs={{0,4},{4,0},{1,5},{5,1},{2,6},{6,2},{3,7},{7,3},{8,12},{12,8},{9,1... | collective-permute-start | bytes 1572872 | tf_op jit(solution)/shard_map/ppermute | solution.py:163
  30.1 2.0 %collective-permute-start.8 = (f32[2,128,128]{2,1,0:T(8,128)S(1)}, f32[2,128,128]{2,1,0:T(8,128)S(1)}, u32[]{:S(2)}, u32[]{:S(2)}) collective-permute-start(f32[2,128,128]{2,1,0:T(8,128)S(1)} %get-tuple-element.68), channel_id=1, source_target_pairs={{0,1},{1,0},{2,3},{3,2},{4,5},{5,4},{6,7},{7,6},{8,9},{9,8},{10,11... | collective-permute-start | bytes 393224 | tf_op jit(solution)/shard_map/ppermute | solution.py:163
  30.2 6.4 %collective-permute-start.9 = (f32[2,128,128]{2,1,0:T(8,128)S(1)}, f32[2,128,128]{2,1,0:T(8,128)S(1)}, u32[]{:S(2)}, u32[]{:S(2)}) collective-permute-start(f32[2,128,128]{2,1,0:T(8,128)S(1)} %get-tuple-element.69), channel_id=1, source_target_pairs={{0,2},{1,3},{2,0},{3,1},{4,6},{5,7},{6,4},{7,5},{8,10},{9,11},{10,... | collective-permute-start | bytes 393224 | tf_op jit(solution)/shard_map/ppermute | solution.py:163
  32.0 6.5 %collective-permute-start.10 = (f32[2,128,128]{2,1,0:T(8,128)S(1)}, f32[2,128,128]{2,1,0:T(8,128)S(1)}, u32[]{:S(2)}, u32[]{:S(2)}) collective-permute-start(f32[2,128,128]{2,1,0:T(8,128)S(1)} %get-tuple-element.70), channel_id=1, source_target_pairs={{0,3},{1,2},{2,1},{3,0},{4,7},{5,6},{6,5},{7,4},{8,11},{9,10},{10,... | collective-permute-start | bytes 393224 | tf_op jit(solution)/shard_map/ppermute | solution.py:163
  40.4 5.6 %collective-permute-start.14 = (f32[2,128,128]{2,1,0:T(8,128)S(1)}, f32[2,128,128]{2,1,0:T(8,128)S(1)}, u32[]{:S(2)}, u32[]{:S(2)}) collective-permute-start(f32[2,128,128]{2,1,0:T(8,128)S(1)} %get-tuple-element.76), channel_id=1, source_target_pairs={{0,1},{1,0},{2,3},{3,2},{4,5},{5,4},{6,7},{7,6},{8,9},{9,8},{10,11... | collective-permute-start | bytes 393224 | tf_op jit(solution)/shard_map/ppermute | solution.py:163
  41.0 6.2 %collective-permute-start.15 = (f32[2,128,128]{2,1,0:T(8,128)S(1)}, f32[2,128,128]{2,1,0:T(8,128)S(1)}, u32[]{:S(2)}, u32[]{:S(2)}) collective-permute-start(f32[2,128,128]{2,1,0:T(8,128)S(1)} %get-tuple-element.77), channel_id=1, source_target_pairs={{0,2},{1,3},{2,0},{3,1},{4,6},{5,7},{6,4},{7,5},{8,10},{9,11},{10,... | collective-permute-start | bytes 393224 | tf_op jit(solution)/shard_map/ppermute | solution.py:163
  42.8 6.7 %collective-permute-start.16 = (f32[2,128,128]{2,1,0:T(8,128)S(1)}, f32[2,128,128]{2,1,0:T(8,128)S(1)}, u32[]{:S(2)}, u32[]{:S(2)}) collective-permute-start(f32[2,128,128]{2,1,0:T(8,128)S(1)} %get-tuple-element.78), channel_id=1, source_target_pairs={{0,3},{1,2},{2,1},{3,0},{4,7},{5,6},{6,5},{7,4},{8,11},{9,10},{10,... | collective-permute-start | bytes 393224 | tf_op jit(solution)/shard_map/ppermute | solution.py:163
  43.7 9.0 %collective-permute-start.11 = (f32[2,128,128]{2,1,0:T(8,128)S(1)}, f32[2,128,128]{2,1,0:T(8,128)S(1)}, u32[]{:S(2)}, u32[]{:S(2)}) collective-permute-start(f32[2,128,128]{2,1,0:T(8,128)S(1)} %get-tuple-element.73), channel_id=1, source_target_pairs={{0,1},{1,0},{2,3},{3,2},{4,5},{5,4},{6,7},{7,6},{8,9},{9,8},{10,11... | collective-permute-start | bytes 393224 | tf_op jit(solution)/shard_map/ppermute | solution.py:163
  44.2 8.6 %collective-permute-start.12 = (f32[2,128,128]{2,1,0:T(8,128)S(1)}, f32[2,128,128]{2,1,0:T(8,128)S(1)}, u32[]{:S(2)}, u32[]{:S(2)}) collective-permute-start(f32[2,128,128]{2,1,0:T(8,128)S(1)} %get-tuple-element.74), channel_id=1, source_target_pairs={{0,2},{1,3},{2,0},{3,1},{4,6},{5,7},{6,4},{7,5},{8,10},{9,11},{10,... | collective-permute-start | bytes 393224 | tf_op jit(solution)/shard_map/ppermute | solution.py:163
  46.0 8.2 %collective-permute-start.13 = (f32[2,128,128]{2,1,0:T(8,128)S(1)}, f32[2,128,128]{2,1,0:T(8,128)S(1)}, u32[]{:S(2)}, u32[]{:S(2)}) collective-permute-start(f32[2,128,128]{2,1,0:T(8,128)S(1)} %get-tuple-element.75), channel_id=1, source_target_pairs={{0,3},{1,2},{2,1},{3,0},{4,7},{5,6},{6,5},{7,4},{8,11},{9,10},{10,... | collective-permute-start | bytes 393224 | tf_op jit(solution)/shard_map/ppermute | solution.py:163
  50.5 17.5 %collective-permute-start.21 = (f32[2,512,128]{2,1,0:T(8,128)S(1)}, f32[2,512,128]{2,1,0:T(8,128)S(1)}, u32[]{:S(2)}, u32[]{:S(2)}) collective-permute-start(f32[2,512,128]{2,1,0:T(8,128)S(1)} %get-tuple-element.86), channel_id=1, source_target_pairs={{0,4},{4,0},{1,5},{5,1},{2,6},{6,2},{3,7},{7,3},{8,12},{12,8},{9,1... | collective-permute-start | bytes 1572872 | tf_op jit(solution)/shard_map/ppermute | solution.py:163
  56.1 2.7 %collective-permute-start.17 = (f32[2,128,128]{2,1,0:T(8,128)S(1)}, f32[2,128,128]{2,1,0:T(8,128)S(1)}, u32[]{:S(2)}, u32[]{:S(2)}) collective-permute-start(f32[2,128,128]{2,1,0:T(8,128)S(1)} %get-tuple-element.81), channel_id=1, source_target_pairs={{0,1},{1,0},{2,3},{3,2},{4,5},{5,4},{6,7},{7,6},{8,9},{9,8},{10,11... | collective-permute-start | bytes 393224 | tf_op jit(solution)/shard_map/ppermute | solution.py:163
  57.1 6.2 %collective-permute-start.18 = (f32[2,128,128]{2,1,0:T(8,128)S(1)}, f32[2,128,128]{2,1,0:T(8,128)S(1)}, u32[]{:S(2)}, u32[]{:S(2)}) collective-permute-start(f32[2,128,128]{2,1,0:T(8,128)S(1)} %get-tuple-element.82), channel_id=1, source_target_pairs={{0,2},{1,3},{2,0},{3,1},{4,6},{5,7},{6,4},{7,5},{8,10},{9,11},{10,... | collective-permute-start | bytes 393224 | tf_op jit(solution)/shard_map/ppermute | solution.py:163
  58.8 5.8 %collective-permute-start.19 = (f32[2,128,128]{2,1,0:T(8,128)S(1)}, f32[2,128,128]{2,1,0:T(8,128)S(1)}, u32[]{:S(2)}, u32[]{:S(2)}) collective-permute-start(f32[2,128,128]{2,1,0:T(8,128)S(1)} %get-tuple-element.83), channel_id=1, source_target_pairs={{0,3},{1,2},{2,1},{3,0},{4,7},{5,6},{6,5},{7,4},{8,11},{9,10},{10,... | collective-permute-start | bytes 393224 | tf_op jit(solution)/shard_map/ppermute | solution.py:163
  65.7 15.0 %collective-permute-start.20 = (f32[2,512,128]{2,1,0:T(8,128)S(1)}, f32[2,512,128]{2,1,0:T(8,128)S(1)}, u32[]{:S(2)}, u32[]{:S(2)}) collective-permute-start(f32[2,512,128]{2,1,0:T(8,128)S(1)} %get-tuple-element.85), channel_id=1, source_target_pairs={{0,4},{4,0},{1,5},{5,1},{2,6},{6,2},{3,7},{7,3},{8,12},{12,8},{9,1... | collective-permute-start | bytes 1572872 | tf_op jit(solution)/shard_map/ppermute | solution.py:163
  69.2 2.0 %collective-permute-start.22 = (f32[2,128,128]{2,1,0:T(8,128)S(1)}, f32[2,128,128]{2,1,0:T(8,128)S(1)}, u32[]{:S(2)}, u32[]{:S(2)}) collective-permute-start(f32[2,128,128]{2,1,0:T(8,128)S(1)} %get-tuple-element.88), channel_id=1, source_target_pairs={{0,1},{1,0},{2,3},{3,2},{4,5},{5,4},{6,7},{7,6},{8,9},{9,8},{10,11... | collective-permute-start | bytes 393224 | tf_op jit(solution)/shard_map/ppermute | solution.py:163
  69.6 6.4 %collective-permute-start.23 = (f32[2,128,128]{2,1,0:T(8,128)S(1)}, f32[2,128,128]{2,1,0:T(8,128)S(1)}, u32[]{:S(2)}, u32[]{:S(2)}) collective-permute-start(f32[2,128,128]{2,1,0:T(8,128)S(1)} %get-tuple-element.89), channel_id=1, source_target_pairs={{0,2},{1,3},{2,0},{3,1},{4,6},{5,7},{6,4},{7,5},{8,10},{9,11},{10,... | collective-permute-start | bytes 393224 | tf_op jit(solution)/shard_map/ppermute | solution.py:163
  71.2 5.9 %collective-permute-start.24 = (f32[2,128,128]{2,1,0:T(8,128)S(1)}, f32[2,128,128]{2,1,0:T(8,128)S(1)}, u32[]{:S(2)}, u32[]{:S(2)}) collective-permute-start(f32[2,128,128]{2,1,0:T(8,128)S(1)} %get-tuple-element.90), channel_id=1, source_target_pairs={{0,3},{1,2},{2,1},{3,0},{4,7},{5,6},{6,5},{7,4},{8,11},{9,10},{10,... | collective-permute-start | bytes 393224 | tf_op jit(solution)/shard_map/ppermute | solution.py:163
  81.9 6.3 %collective-permute-start.26 = (f32[2,128,128]{2,1,0:T(8,128)S(1)}, f32[2,128,128]{2,1,0:T(8,128)S(1)}, u32[]{:S(2)}, u32[]{:S(2)}) collective-permute-start(f32[2,128,128]{2,1,0:T(8,128)S(1)} %get-tuple-element.93), channel_id=1, source_target_pairs={{0,2},{1,3},{2,0},{3,1},{4,6},{5,7},{6,4},{7,5},{8,10},{9,11},{10,... | collective-permute-start | bytes 393224 | tf_op jit(solution)/shard_map/ppermute | solution.py:163
  83.5 6.5 %collective-permute-start.27 = (f32[2,128,128]{2,1,0:T(8,128)S(1)}, f32[2,128,128]{2,1,0:T(8,128)S(1)}, u32[]{:S(2)}, u32[]{:S(2)}) collective-permute-start(f32[2,128,128]{2,1,0:T(8,128)S(1)} %get-tuple-element.94), channel_id=1, source_target_pairs={{0,3},{1,2},{2,1},{3,0},{4,7},{5,6},{6,5},{7,4},{8,11},{9,10},{10,... | collective-permute-start | bytes 393224 | tf_op jit(solution)/shard_map/ppermute | solution.py:163
  91.5 6.5 %collective-permute-start.28 = (f32[256,128]{1,0:T(8,128)S(1)}, f32[256,128]{1,0:T(8,128)S(1)}, u32[]{:S(2)}, u32[]{:S(2)}) collective-permute-start(f32[256,128]{1,0:T(8,128)S(1)} %get-tuple-element.96.refs_6_), channel_id=1, source_target_pairs={{0,8},{8,0},{16,24},{24,16},{1,9},{9,1},{17,25},{25,17},{2,10},{10... | collective-permute-start | bytes 393224 | tf_op jit(solution)/shard_map/ppermute | solution.py:415
  93.1 3.0 %collective-permute-start.31 = (f32[8,128]{1,0:T(8,128)S(1)}, f32[8,128]{1,0:T(8,128)S(1)}, u32[]{:S(2)}, u32[]{:S(2)}) collective-permute-start(f32[8,128]{1,0:T(8,128)S(1)} %get-tuple-element.97.refs_2_), channel_id=1, source_target_pairs={{0,3},{1,2},{2,1},{3,0},{4,7},{5,6},{6,5},{7,4},{8,11},{9,10},{10,... | collective-permute-start | bytes 12296 | tf_op jit(solution)/shard_map/ppermute | solution.py:163
  94.3 3.6 %collective-permute-start.30 = (f32[8,128]{1,0:T(8,128)S(1)}, f32[8,128]{1,0:T(8,128)S(1)}, u32[]{:S(2)}, u32[]{:S(2)}) collective-permute-start(f32[8,128]{1,0:T(8,128)S(1)} %get-tuple-element.97.refs_2_), channel_id=1, source_target_pairs={{0,2},{1,3},{2,0},{3,1},{4,6},{5,7},{6,4},{7,5},{8,10},{9,11},{10,... | collective-permute-start | bytes 12296 | tf_op jit(solution)/shard_map/ppermute | solution.py:163
  94.9 3.1 %collective-permute-start.29 = (f32[8,128]{1,0:T(8,128)S(1)}, f32[8,128]{1,0:T(8,128)S(1)}, u32[]{:S(2)}, u32[]{:S(2)}) collective-permute-start(f32[8,128]{1,0:T(8,128)S(1)} %get-tuple-element.97.refs_2_), channel_id=1, source_target_pairs={{0,1},{1,0},{2,3},{3,2},{4,5},{5,4},{6,7},{7,6},{8,9},{9,8},{10,11... | collective-permute-start | bytes 12296 | tf_op jit(solution)/shard_map/ppermute | solution.py:163
  98.0 8.8 %collective-permute-start.32 = (f32[264,128]{1,0:T(8,128)S(1)}, f32[264,128]{1,0:T(8,128)S(1)}, u32[]{:S(2)}, u32[]{:S(2)}) collective-permute-start(f32[264,128]{1,0:T(8,128)S(1)} %shard_map.93.refs_0_.refs_2_), channel_id=1, source_target_pairs={{0,16},{8,24},{16,0},{24,8},{1,17},{9,25},{17,1},{25,9},{2,18},{10... | collective-permute-start | bytes 405512 | tf_op jit(solution)/shard_map/ppermute | solution.py:415
  106.8 5.1 %collective-permute-start.33 = (f32[264,128]{1,0:T(8,128)S(1)}, f32[264,128]{1,0:T(8,128)S(1)}, u32[]{:S(2)}, u32[]{:S(2)}) collective-permute-start(f32[264,128]{1,0:T(8,128)S(1)} %shard_map.94.refs_0_.refs_2_), channel_id=1, source_target_pairs={{0,8},{8,0},{16,24},{24,16},{1,9},{9,1},{17,25},{25,17},{2,10},{10... | collective-permute-start | bytes 405512 | tf_op jit(solution)/shard_map/ppermute | solution.py:415
  (10 other events, 53.7 us)
where the time goes:
time: 113 us
  waiting for transfers between devices  58.3 us (52%)
  starting transfers between devices  31.3 us (28%)
  Pallas kernels  21 us (19%)
  local copies, waits for them, and re-layouts  1.15 us (1%)
    ppermute x31, waiting for transfers between devices, send(): got[d] = lax.ppermute(blocks[d], axis, [(i, i ^ d) for i in range(size)])  47.4 us
    ppermute x31, starting transfers between devices, send(): got[d] = lax.ppermute(blocks[d], axis, [(i, i ^ d) for i in range(size)])  26.7 us
    pallas_call x19, Pallas kernels, call(): pl.pallas_call(ordered, grid=(1,), out_shape=outs, in_specs=list(specs) +...  21 us
    ppermute x3, waiting for transfers between devices, across(): return lax.ppermute(value, 'freq', [(i, i ^ d) for i in range(freqs)])  11 us
    ppermute x3, starting transfers between devices, across(): return lax.ppermute(value, 'freq', [(i, i ^ d) for i in range(freqs)])  4.62 us
  transfers between devices with their start and end apart: 34, of which 22 were waited for; matrix products, arithmetic and copies ran while one was open for 0% of the time, Pallas kernels for 12%

commit v1 on v0

--- a/solution.py
+++ b/solution.py
@@ -157,10 +157,14 @@
     return jax.ShapeDtypeStruct(shape, jnp.float32)
 
 
+def turns(size):
+    return sorted(range(size), key=lambda d: (d == 1, d))
+
+
 def send(blocks, axis, size):
-    got = [blocks[0]] + [None] * (size - 1)
-    for d in sorted(range(1, size), key=lambda d: (d < 2, d)):
-        got[d] = lax.ppermute(blocks[d], axis, [(i, i ^ d) for i in range(size)])
+    got = [blocks[0]]
+    for d, block in zip(turns(size)[1:], blocks[1:]):
+        got.append(lax.ppermute(block, axis, [(i, i ^ d) for i in range(size)]))
     return got
 
 
@@ -184,7 +188,7 @@
 
 def forward_blocks(real, imag, high_ref, low_ref, out_refs):
     me = lax.axis_index("lat")
-    for d, out in enumerate(out_refs):
+    for d, out in zip(turns(len(out_refs)), out_refs):
         out[0], out[1] = along_y(real, imag, high_ref, low_ref, me ^ d, -1)
 
 
@@ -226,7 +230,7 @@
     outs, (high, low) = rest[:layers], rest[layers:]
     me, layer = lax.axis_index("lat"), lax.axis_index("layer")
     rows, width = parts[0].shape[1:]
-    for d, part in enumerate(parts):
+    for d, part in zip(turns(len(parts)), parts):
         at = pl.ds(pl.multiple_of((me ^ d) * rows, rows), rows)
         for z in range(2):
             high[at, z * width : (z + 1) * width], low[at, z * width : (z + 1) * width] = halves(part[z])
@@ -245,14 +249,14 @@
     me = lax.axis_index("lat")
     mixed = [sum((part[z] for part in parts[1:]), parts[0][z]) for z in range(2)]
     high, low = halves(jnp.concatenate(mixed, axis=1))
-    for d, out in enumerate(outs):
+    for d, out in zip(turns(lat), outs):
         out[0], out[1] = along_x(high_ref, low_ref, me ^ d, high, low, +1)
 
 
 def gather_lanes(parts, field):
     me = lax.axis_index("lat")
     width = parts[0].shape[2]
-    for d, part in enumerate(parts):
+    for d, part in zip(turns(len(parts)), parts):
         at = pl.ds(pl.multiple_of((me ^ d) * width, width), width)
         for z in range(2):
             field[z, :, at] = part[z]
@@ -292,19 +296,22 @@
 
 def deal_body(lat, *refs):
     parts, (source, contrast, efield, high_ref, low_ref), rest = refs[:lat], refs[lat : lat + 5], refs[lat + 5 :]
-    before, kinds, gone, kept, table, field, cell = rest
+    before, gone, kept, cell, field = rest
     cell[...] = before[...] + terms_of(parts, source, contrast, efield, high_ref, low_ref, field)
     bit = lax.axis_index("freq") & 1
-    width = table.shape[1]
+    width = gone.shape[1]
     rows = cell.shape[0] // 2
     for which, out in ((1 - bit, gone), (bit, kept)):
         block = cell[pl.ds(pl.multiple_of(which * rows, rows), rows)]
         for k in range(block.shape[1] // width):
             out[k * rows : (k + 1) * rows] = block[:, k * width : (k + 1) * width]
+
+
+def class_body(cell, kinds, table):
     lines = []
     for c in range(CLASSES):
         chosen = jnp.where(kinds[...] == c, cell[...], 0.0)
-        lines.append(jnp.full((1, width), jnp.sum(chosen), jnp.float32))
+        lines.append(jnp.full((1, table.shape[1]), jnp.sum(chosen), jnp.float32))
     table[...] = jnp.concatenate(lines, axis=0)
 
 
@@ -405,11 +412,10 @@
         return kernel(functools.partial(end_body, lat), [f32(rows, length)], args, specs, scratch=[full])[0]
 
     def deal(parts, cells):
-        specs = field_specs(last) + [pick(efield.shape, last)] + table_specs + [whole((rows, length))] * 2
-        args = (*parts, source, contrast, efield, *col, cells, kinds)
-        outs = [f32(rows // 2 * (length // 128), 128)] * 2 + [f32(CLASSES, 128)]
-        scratch = [full, pltpu.VMEM((rows, length), jnp.float32)]
-        return kernel(functools.partial(deal_body, lat), outs, args, specs, scratch=scratch)
+        specs = field_specs(last) + [pick(efield.shape, last)] + table_specs + [whole((rows, length))]
+        args = (*parts, source, contrast, efield, *col, cells)
+        outs = [f32(rows // 2 * (length // 128), 128)] * 2 + [f32(rows, length)]
+        return kernel(functools.partial(deal_body, lat), outs, args, specs, scratch=[full])
 
     def across(value, d):
         return lax.ppermute(value, "freq", [(i, i ^ d) for i in range(freqs)])
@@ -440,8 +446,9 @@
     cells = jnp.zeros((rows, length), jnp.float32) if last == 0 else None
     for p in range(last):
         cells = end(p, back(chains[p]), cells)
-    gone, kept, found = deal(back(chains[last]), cells)
+    gone, kept, terms = deal(back(chains[last]), cells)
     came = across(gone, 1)
+    found = simple(class_body, (CLASSES, 128), [terms, kinds])
     found = send([found] * lat, "lat", lat)
     kept = simple(keep_body, (kept.shape[0] + CLASSES, 128), [kept, came, *found])
     d = 2

time: 113 us -> 111 us (0.982)
  starting transfers between devices: 31.3 us -> 29.9 us
    pallas_call x19 -> x20, Pallas kernels: 21 us -> 21 us  [call(): pl.pallas_call(ordered, grid=(1,), out_shape=outs, in_specs=list(specs) +...]
where the time goes in v1:
time: 111 us
  waiting for transfers between devices  57.6 us (52%)
  starting transfers between devices  29.9 us (27%)
  Pallas kernels  21 us (19%)
  local copies, waits for them, and re-layouts  1.15 us (1%)
    ppermute x31, waiting for transfers between devices, send(): got.append(lax.ppermute(block, axis, [(i, i ^ d) for i in range(size)]))  46.3 us
    ppermute x31, starting transfers between devices, send(): got.append(lax.ppermute(block, axis, [(i, i ^ d) for i in range(size)]))  25.6 us
    pallas_call x20, Pallas kernels, call(): pl.pallas_call(ordered, grid=(1,), out_shape=outs, in_specs=list(specs) +...  21 us
    ppermute x3, waiting for transfers between devices, across(): return lax.ppermute(value, 'freq', [(i, i ^ d) for i in range(freqs)])  11.3 us
    ppermute x3, starting transfers between devices, across(): return lax.ppermute(value, 'freq', [(i, i ^ d) for i in range(freqs)])  4.37 us
  transfers between devices with their start and end apart: 34, of which 22 were waited for; matrix products, arithmetic and copies ran while one was open for 0% of the time, Pallas kernels for 12%

profile of v1, /device:TPU:0, one launch (start us, length us, event | category | flops | bytes accessed | tf_op | source)
XLA Modules:
  0.0 110.5 jit_solution(4765843033922963789)
XLA Ops:
  0.7 3.4 %shard_map.77 = (f32[2,128,128]{2,1,0:T(8,128)}, f32[2,128,128]{2,1,0:T(8,128)}, f32[2,128,128]{2,1,0:T(8,128)}, f32[2,128,128]{2,1,0:T(8,128)}) custom-call(f32[2,2,128,512]{3,2,1,0:T(8,128)} %bitcast.6, f32[2,128,512]{2,1,0:T(8,128)} %bitcast.12, f32[2,48,512]{2,1,0:T(8,128)} %constant.2.clone.refs_2_.refs_0_), custom_call_target="tpu_custom_call" | custom-call | flops 805306368 | bytes 1048576 | tf_op jit(solution)/shard_map/pallas_call | solution.py:136
  4.0 3.0 %collective-permute-start.3 = (f32[2,128,128]{2,1,0:T(8,128)}, f32[2,128,128]{2,1,0:T(8,128)S(1)}, u32[]{:S(2)}, u32[]{:S(2)}) collective-permute-start(f32[2,128,128]{2,1,0:T(8,128)} %get-tuple-element.60), channel_id=1, source_target_pairs={{0,2},{1,3},{2,0},{3,1},{4,6},{5,7},{6,4},{7,5},{8,10},{9,11},{10,... | collective-permute-start | bytes 393224 | tf_op jit(solution)/shard_map/ppermute | solution.py:167
  11.3 1.8 %collective-permute-done.4.refs_2_ = f32[2,128,128]{2,1,0:T(8,128)S(1)} collective-permute-done((f32[2,128,128]{2,1,0:T(8,128)}, f32[2,128,128]{2,1,0:T(8,128)S(1)}, u32[]{:S(2)}, u32[]{:S(2)}) %collective-permute-start.4) | collective-permute-done | bytes 131104 | tf_op jit(solution)/shard_map/ppermute | solution.py:167
  14.2 1.5 %collective-permute-start.7 = (f32[2,512,128]{2,1,0:T(8,128)S(1)}, f32[2,512,128]{2,1,0:T(8,128)S(1)}, u32[]{:S(2)}, u32[]{:S(2)}) collective-permute-start(f32[2,512,128]{2,1,0:T(8,128)S(1)} %get-tuple-element.66), channel_id=1, source_target_pairs={{0,4},{4,0},{1,5},{5,1},{2,6},{6,2},{3,7},{7,3},{8,12},{12,8},{9,1... | collective-permute-start | bytes 1572872 | tf_op jit(solution)/shard_map/ppermute | solution.py:167
  17.9 4.2 %collective-permute-done.refs_1_ = f32[2,128,128]{2,1,0:T(8,128)S(1)} collective-permute-done((f32[2,128,128]{2,1,0:T(8,128)S(1)}, f32[2,128,128]{2,1,0:T(8,128)S(1)}, u32[]{:S(2)}, u32[]{:S(2)}) %collective-permute-start) | collective-permute-done | bytes 131104 | tf_op jit(solution)/shard_map/ppermute | solution.py:167
  22.0 1.5 %collective-permute-done.1.refs_2_ = f32[2,128,128]{2,1,0:T(8,128)S(1)} collective-permute-done((f32[2,128,128]{2,1,0:T(8,128)S(1)}, f32[2,128,128]{2,1,0:T(8,128)S(1)}, u32[]{:S(2)}, u32[]{:S(2)}) %collective-permute-start.1) | collective-permute-done | bytes 131104 | tf_op jit(solution)/shard_map/ppermute | solution.py:167
  24.9 3.7 %collective-permute-done.7.refs_1_ = f32[2,512,128]{2,1,0:T(8,128)S(1)} collective-permute-done((f32[2,512,128]{2,1,0:T(8,128)S(1)}, f32[2,512,128]{2,1,0:T(8,128)S(1)}, u32[]{:S(2)}, u32[]{:S(2)}) %collective-permute-start.7) | collective-permute-done | bytes 524320 | tf_op jit(solution)/shard_map/ppermute | solution.py:167
  29.6 1.6 %collective-permute-start.8 = (f32[2,128,128]{2,1,0:T(8,128)S(1)}, f32[2,128,128]{2,1,0:T(8,128)S(1)}, u32[]{:S(2)}, u32[]{:S(2)}) collective-permute-start(f32[2,128,128]{2,1,0:T(8,128)S(1)} %get-tuple-element.68), channel_id=1, source_target_pairs={{0,2},{1,3},{2,0},{3,1},{4,6},{5,7},{6,4},{7,5},{8,10},{9,11},{10,... | collective-permute-start | bytes 393224 | tf_op jit(solution)/shard_map/ppermute | solution.py:167
  31.8 3.9 %collective-permute-done.8.refs_1_ = f32[2,128,128]{2,1,0:T(8,128)S(1)} collective-permute-done((f32[2,128,128]{2,1,0:T(8,128)S(1)}, f32[2,128,128]{2,1,0:T(8,128)S(1)}, u32[]{:S(2)}, u32[]{:S(2)}) %collective-permute-start.8) | collective-permute-done | bytes 131104 | tf_op jit(solution)/shard_map/ppermute | solution.py:167
  37.0 1.9 %shard_map.84 = (f32[2,128,128]{2,1,0:T(8,128)S(1)}, f32[2,128,128]{2,1,0:T(8,128)S(1)}, f32[2,128,128]{2,1,0:T(8,128)S(1)}, f32[2,128,128]{2,1,0:T(8,128)S(1)}) custom-call(f32[2,128,128]{2,1,0:T(8,128)S(1)} %get-tuple-element.67.refs_0_.refs_8_, f32[2,128,128]{2,1,0:T(8,128)S(1)} %collective-permute-done.8.refs_1_, ...), custom_call_target="tpu_custom_call" | custom-call | flops 1610612736 | bytes 1048576 | tf_op jit(solution)/shard_map/pallas_call | solution.py:136
  39.0 1.7 %collective-permute-start.14 = (f32[2,128,128]{2,1,0:T(8,128)S(1)}, f32[2,128,128]{2,1,0:T(8,128)S(1)}, u32[]{:S(2)}, u32[]{:S(2)}) collective-permute-start(f32[2,128,128]{2,1,0:T(8,128)S(1)} %get-tuple-element.76), channel_id=1, source_target_pairs={{0,2},{1,3},{2,0},{3,1},{4,6},{5,7},{6,4},{7,5},{8,10},{9,11},{10,... | collective-permute-start | bytes 393224 | tf_op jit(solution)/shard_map/ppermute | solution.py:167
  42.4 1.7 %collective-permute-start.11 = (f32[2,128,128]{2,1,0:T(8,128)S(1)}, f32[2,128,128]{2,1,0:T(8,128)S(1)}, u32[]{:S(2)}, u32[]{:S(2)}) collective-permute-start(f32[2,128,128]{2,1,0:T(8,128)S(1)} %get-tuple-element.73), channel_id=1, source_target_pairs={{0,2},{1,3},{2,0},{3,1},{4,6},{5,7},{6,4},{7,5},{8,10},{9,11},{10,... | collective-permute-start | bytes 393224 | tf_op jit(solution)/shard_map/ppermute | solution.py:167
  45.4 2.6 %collective-permute-done.15.refs_2_ = f32[2,128,128]{2,1,0:T(8,128)S(1)} collective-permute-done((f32[2,128,128]{2,1,0:T(8,128)S(1)}, f32[2,128,128]{2,1,0:T(8,128)S(1)}, u32[]{:S(2)}, u32[]{:S(2)}) %collective-permute-start.15) | collective-permute-done | bytes 131104 | tf_op jit(solution)/shard_map/ppermute | solution.py:167
  49.1 1.5 %collective-permute-start.21 = (f32[2,512,128]{2,1,0:T(8,128)S(1)}, f32[2,512,128]{2,1,0:T(8,128)S(1)}, u32[]{:S(2)}, u32[]{:S(2)}) collective-permute-start(f32[2,512,128]{2,1,0:T(8,128)S(1)} %get-tuple-element.86), channel_id=1, source_target_pairs={{0,4},{4,0},{1,5},{5,1},{2,6},{6,2},{3,7},{7,3},{8,12},{12,8},{9,1... | collective-permute-start | bytes 1572872 | tf_op jit(solution)/shard_map/ppermute | solution.py:167
  51.0 2.6 %collective-permute-done.12.refs_2_ = f32[2,128,128]{2,1,0:T(8,128)S(1)} collective-permute-done((f32[2,128,128]{2,1,0:T(8,128)S(1)}, f32[2,128,128]{2,1,0:T(8,128)S(1)}, u32[]{:S(2)}, u32[]{:S(2)}) %collective-permute-start.12) | collective-permute-done | bytes 131104 | tf_op jit(solution)/shard_map/ppermute | solution.py:167
  53.6 1.9 %shard_map.87 = (f32[2,128,128]{2,1,0:T(8,128)S(1)}, f32[2,128,128]{2,1,0:T(8,128)S(1)}, f32[2,128,128]{2,1,0:T(8,128)S(1)}, f32[2,128,128]{2,1,0:T(8,128)S(1)}) custom-call(f32[2,128,128]{2,1,0:T(8,128)S(1)} %get-tuple-element.72.refs_7_.refs_0_, f32[2,128,128]{2,1,0:T(8,128)S(1)} %collective-permute-done.11.refs_1_, ...), custom_call_target="tpu_custom_call" | custom-call | flops 1610612736 | bytes 1048576 | tf_op jit(solution)/shard_map/pallas_call | solution.py:136
  55.6 1.9 %collective-permute-start.17 = (f32[2,128,128]{2,1,0:T(8,128)S(1)}, f32[2,128,128]{2,1,0:T(8,128)S(1)}, u32[]{:S(2)}, u32[]{:S(2)}) collective-permute-start(f32[2,128,128]{2,1,0:T(8,128)S(1)} %get-tuple-element.81), channel_id=1, source_target_pairs={{0,2},{1,3},{2,0},{3,1},{4,6},{5,7},{6,4},{7,5},{8,10},{9,11},{10,... | collective-permute-start | bytes 393224 | tf_op jit(solution)/shard_map/ppermute | solution.py:167
  57.8 4.2 %collective-permute-done.17.refs_1_ = f32[2,128,128]{2,1,0:T(8,128)S(1)} collective-permute-done((f32[2,128,128]{2,1,0:T(8,128)S(1)}, f32[2,128,128]{2,1,0:T(8,128)S(1)}, u32[]{:S(2)}, u32[]{:S(2)}) %collective-permute-start.17) | collective-permute-done | bytes 131104 | tf_op jit(solution)/shard_map/ppermute | solution.py:167
  62.0 1.4 %collective-permute-done.18.refs_2_ = f32[2,128,128]{2,1,0:T(8,128)S(1)} collective-permute-done((f32[2,128,128]{2,1,0:T(8,128)S(1)}, f32[2,128,128]{2,1,0:T(8,128)S(1)}, u32[]{:S(2)}, u32[]{:S(2)}) %collective-permute-start.18) | collective-permute-done | bytes 131104 | tf_op jit(solution)/shard_map/ppermute | solution.py:167
  64.5 1.6 %collective-permute-start.20 = (f32[2,512,128]{2,1,0:T(8,128)S(1)}, f32[2,512,128]{2,1,0:T(8,128)S(1)}, u32[]{:S(2)}, u32[]{:S(2)}) collective-permute-start(f32[2,512,128]{2,1,0:T(8,128)S(1)} %get-tuple-element.85), channel_id=1, source_target_pairs={{0,4},{4,0},{1,5},{5,1},{2,6},{6,2},{3,7},{7,3},{8,12},{12,8},{9,1... | collective-permute-start | bytes 1572872 | tf_op jit(solution)/shard_map/ppermute | solution.py:167
  67.2 1.7 %collective-permute-start.22 = (f32[2,128,128]{2,1,0:T(8,128)S(1)}, f32[2,128,128]{2,1,0:T(8,128)S(1)}, u32[]{:S(2)}, u32[]{:S(2)}) collective-permute-start(f32[2,128,128]{2,1,0:T(8,128)S(1)} %get-tuple-element.88), channel_id=1, source_target_pairs={{0,2},{1,3},{2,0},{3,1},{4,6},{5,7},{6,4},{7,5},{8,10},{9,11},{10,... | collective-permute-start | bytes 393224 | tf_op jit(solution)/shard_map/ppermute | solution.py:167
  69.4 4.2 %collective-permute-done.22.refs_1_ = f32[2,128,128]{2,1,0:T(8,128)S(1)} collective-permute-done((f32[2,128,128]{2,1,0:T(8,128)S(1)}, f32[2,128,128]{2,1,0:T(8,128)S(1)}, u32[]{:S(2)}, u32[]{:S(2)}) %collective-permute-start.22) | collective-permute-done | bytes 131104 | tf_op jit(solution)/shard_map/ppermute | solution.py:167
  73.6 1.5 %collective-permute-done.23.refs_2_ = f32[2,128,128]{2,1,0:T(8,128)S(1)} collective-permute-done((f32[2,128,128]{2,1,0:T(8,128)S(1)}, f32[2,128,128]{2,1,0:T(8,128)S(1)}, u32[]{:S(2)}, u32[]{:S(2)}) %collective-permute-start.23) | collective-permute-done | bytes 131104 | tf_op jit(solution)/shard_map/ppermute | solution.py:167
  76.1 2.8 %collective-permute-done.20.refs_1_ = f32[2,512,128]{2,1,0:T(8,128)S(1)} collective-permute-done((f32[2,512,128]{2,1,0:T(8,128)S(1)}, f32[2,512,128]{2,1,0:T(8,128)S(1)}, u32[]{:S(2)}, u32[]{:S(2)}) %collective-permute-start.20) | collective-permute-done | bytes 524320 | tf_op jit(solution)/shard_map/ppermute | solution.py:167
  79.9 1.8 %collective-permute-start.25 = (f32[2,128,128]{2,1,0:T(8,128)S(1)}, f32[2,128,128]{2,1,0:T(8,128)S(1)}, u32[]{:S(2)}, u32[]{:S(2)}) collective-permute-start(f32[2,128,128]{2,1,0:T(8,128)S(1)} %get-tuple-element.92), channel_id=1, source_target_pairs={{0,2},{1,3},{2,0},{3,1},{4,6},{5,7},{6,4},{7,5},{8,10},{9,11},{10,... | collective-permute-start | bytes 393224 | tf_op jit(solution)/shard_map/ppermute | solution.py:167
  82.1 3.5 %collective-permute-done.25.refs_1_ = f32[2,128,128]{2,1,0:T(8,128)S(1)} collective-permute-done((f32[2,128,128]{2,1,0:T(8,128)S(1)}, f32[2,128,128]{2,1,0:T(8,128)S(1)}, u32[]{:S(2)}, u32[]{:S(2)}) %collective-permute-start.25) | collective-permute-done | bytes 131104 | tf_op jit(solution)/shard_map/ppermute | solution.py:167
  85.6 1.9 %collective-permute-done.26.refs_2_ = f32[2,128,128]{2,1,0:T(8,128)S(1)} collective-permute-done((f32[2,128,128]{2,1,0:T(8,128)S(1)}, f32[2,128,128]{2,1,0:T(8,128)S(1)}, u32[]{:S(2)}, u32[]{:S(2)}) %collective-permute-start.26) | collective-permute-done | bytes 131104 | tf_op jit(solution)/shard_map/ppermute | solution.py:167
  88.6 1.6 %collective-permute-start.28 = (f32[256,128]{1,0:T(8,128)S(1)}, f32[256,128]{1,0:T(8,128)S(1)}, u32[]{:S(2)}, u32[]{:S(2)}) collective-permute-start(f32[256,128]{1,0:T(8,128)S(1)} %get-tuple-element.96.refs_2_), channel_id=1, source_target_pairs={{0,8},{8,0},{16,24},{24,16},{1,9},{9,1},{17,25},{25,17},{2,10},{10... | collective-permute-start | bytes 393224 | tf_op jit(solution)/shard_map/ppermute | solution.py:421
  93.8 1.9 %collective-permute-done.29.refs_3_ = f32[8,128]{1,0:T(8,128)S(1)} collective-permute-done((f32[8,128]{1,0:T(8,128)S(1)}, f32[8,128]{1,0:T(8,128)S(1)}, u32[]{:S(2)}, u32[]{:S(2)}) %collective-permute-start.29) | collective-permute-done | bytes 4128 | tf_op jit(solution)/shard_map/ppermute | solution.py:167
  95.7 2.7 %collective-permute-start.32 = (f32[264,128]{1,0:T(8,128)S(1)}, f32[264,128]{1,0:T(8,128)S(1)}, u32[]{:S(2)}, u32[]{:S(2)}) collective-permute-start(f32[264,128]{1,0:T(8,128)S(1)} %shard_map.94.refs_0_.refs_2_), channel_id=1, source_target_pairs={{0,16},{8,24},{16,0},{24,8},{1,17},{9,25},{17,1},{25,9},{2,18},{10... | collective-permute-start | bytes 405512 | tf_op jit(solution)/shard_map/ppermute | solution.py:421
  98.4 6.0 %collective-permute-done.32.refs_1_ = f32[264,128]{1,0:T(8,128)S(1)} collective-permute-done((f32[264,128]{1,0:T(8,128)S(1)}, f32[264,128]{1,0:T(8,128)S(1)}, u32[]{:S(2)}, u32[]{:S(2)}) %collective-permute-start.32) | collective-permute-done | bytes 135200 | tf_op jit(solution)/shard_map/ppermute | solution.py:421
  104.5 5.3 %collective-permute-done.33.refs_1_ = f32[264,128]{1,0:T(8,128)S(1)} collective-permute-done((f32[264,128]{1,0:T(8,128)S(1)}, f32[264,128]{1,0:T(8,128)S(1)}, u32[]{:S(2)}, u32[]{:S(2)}) %collective-permute-start.33) | collective-permute-done | bytes 135200 | tf_op jit(solution)/shard_map/ppermute | solution.py:421
  (72 shorter events, 27.2 us)
Async XLA Ops:
  4.0 7.3 %collective-permute-start.3 = (f32[2,128,128]{2,1,0:T(8,128)}, f32[2,128,128]{2,1,0:T(8,128)S(1)}, u32[]{:S(2)}, u32[]{:S(2)}) collective-permute-start(f32[2,128,128]{2,1,0:T(8,128)} %get-tuple-element.60), channel_id=1, source_target_pairs={{0,2},{1,3},{2,0},{3,1},{4,6},{5,7},{6,4},{7,5},{8,10},{9,11},{10,... | collective-permute-start | bytes 393224 | tf_op jit(solution)/shard_map/ppermute | solution.py:167
  7.1 6.1 %collective-permute-start.4 = (f32[2,128,128]{2,1,0:T(8,128)}, f32[2,128,128]{2,1,0:T(8,128)S(1)}, u32[]{:S(2)}, u32[]{:S(2)}) collective-permute-start(f32[2,128,128]{2,1,0:T(8,128)} %get-tuple-element.61), channel_id=1, source_target_pairs={{0,3},{1,2},{2,1},{3,0},{4,7},{5,6},{6,5},{7,4},{8,11},{9,10},{10,... | collective-permute-start | bytes 393224 | tf_op jit(solution)/shard_map/ppermute | solution.py:167
  7.1 6.1 %collective-permute-start.5 = (f32[2,128,128]{2,1,0:T(8,128)}, f32[2,128,128]{2,1,0:T(8,128)S(1)}, u32[]{:S(2)}, u32[]{:S(2)}) collective-permute-start(f32[2,128,128]{2,1,0:T(8,128)} %get-tuple-element.62), channel_id=1, source_target_pairs={{0,1},{1,0},{2,3},{3,2},{4,5},{5,4},{6,7},{7,6},{8,9},{9,8},{10,11... | collective-permute-start | bytes 393224 | tf_op jit(solution)/shard_map/ppermute | solution.py:167
  14.2 14.4 %collective-permute-start.7 = (f32[2,512,128]{2,1,0:T(8,128)S(1)}, f32[2,512,128]{2,1,0:T(8,128)S(1)}, u32[]{:S(2)}, u32[]{:S(2)}) collective-permute-start(f32[2,512,128]{2,1,0:T(8,128)S(1)} %get-tuple-element.66), channel_id=1, source_target_pairs={{0,4},{4,0},{1,5},{5,1},{2,6},{6,2},{3,7},{7,3},{8,12},{12,8},{9,1... | collective-permute-start | bytes 1572872 | tf_op jit(solution)/shard_map/ppermute | solution.py:167
  15.7 6.3 %collective-permute-start = (f32[2,128,128]{2,1,0:T(8,128)S(1)}, f32[2,128,128]{2,1,0:T(8,128)S(1)}, u32[]{:S(2)}, u32[]{:S(2)}) collective-permute-start(f32[2,128,128]{2,1,0:T(8,128)S(1)} %get-tuple-element.55), channel_id=1, source_target_pairs={{0,2},{1,3},{2,0},{3,1},{4,6},{5,7},{6,4},{7,5},{8,10},{9,11},{10,... | collective-permute-start | bytes 393224 | tf_op jit(solution)/shard_map/ppermute | solution.py:167
  16.8 6.7 %collective-permute-start.1 = (f32[2,128,128]{2,1,0:T(8,128)S(1)}, f32[2,128,128]{2,1,0:T(8,128)S(1)}, u32[]{:S(2)}, u32[]{:S(2)}) collective-permute-start(f32[2,128,128]{2,1,0:T(8,128)S(1)} %get-tuple-element.56), channel_id=1, source_target_pairs={{0,3},{1,2},{2,1},{3,0},{4,7},{5,6},{6,5},{7,4},{8,11},{9,10},{10,... | collective-permute-start | bytes 393224 | tf_op jit(solution)/shard_map/ppermute | solution.py:167
  17.4 6.2 %collective-permute-start.2 = (f32[2,128,128]{2,1,0:T(8,128)S(1)}, f32[2,128,128]{2,1,0:T(8,128)S(1)}, u32[]{:S(2)}, u32[]{:S(2)}) collective-permute-start(f32[2,128,128]{2,1,0:T(8,128)S(1)} %get-tuple-element.57), channel_id=1, source_target_pairs={{0,1},{1,0},{2,3},{3,2},{4,5},{5,4},{6,7},{7,6},{8,9},{9,8},{10,11... | collective-permute-start | bytes 393224 | tf_op jit(solution)/shard_map/ppermute | solution.py:167
  24.7 16.7 %collective-permute-start.6 = (f32[2,512,128]{2,1,0:T(8,128)S(1)}, f32[2,512,128]{2,1,0:T(8,128)S(1)}, u32[]{:S(2)}, u32[]{:S(2)}) collective-permute-start(f32[2,512,128]{2,1,0:T(8,128)S(1)} %get-tuple-element.65), channel_id=1, source_target_pairs={{0,4},{4,0},{1,5},{5,1},{2,6},{6,2},{3,7},{7,3},{8,12},{12,8},{9,1... | collective-permute-start | bytes 1572872 | tf_op jit(solution)/shard_map/ppermute | solution.py:167
  29.6 6.1 %collective-permute-start.8 = (f32[2,128,128]{2,1,0:T(8,128)S(1)}, f32[2,128,128]{2,1,0:T(8,128)S(1)}, u32[]{:S(2)}, u32[]{:S(2)}) collective-permute-start(f32[2,128,128]{2,1,0:T(8,128)S(1)} %get-tuple-element.68), channel_id=1, source_target_pairs={{0,2},{1,3},{2,0},{3,1},{4,6},{5,7},{6,4},{7,5},{8,10},{9,11},{10,... | collective-permute-start | bytes 393224 | tf_op jit(solution)/shard_map/ppermute | solution.py:167
  31.2 5.8 %collective-permute-start.9 = (f32[2,128,128]{2,1,0:T(8,128)S(1)}, f32[2,128,128]{2,1,0:T(8,128)S(1)}, u32[]{:S(2)}, u32[]{:S(2)}) collective-permute-start(f32[2,128,128]{2,1,0:T(8,128)S(1)} %get-tuple-element.69), channel_id=1, source_target_pairs={{0,3},{1,2},{2,1},{3,0},{4,7},{5,6},{6,5},{7,4},{8,11},{9,10},{10,... | collective-permute-start | bytes 393224 | tf_op jit(solution)/shard_map/ppermute | solution.py:167
  31.2 5.8 %collective-permute-start.10 = (f32[2,128,128]{2,1,0:T(8,128)S(1)}, f32[2,128,128]{2,1,0:T(8,128)S(1)}, u32[]{:S(2)}, u32[]{:S(2)}) collective-permute-start(f32[2,128,128]{2,1,0:T(8,128)S(1)} %get-tuple-element.70), channel_id=1, source_target_pairs={{0,1},{1,0},{2,3},{3,2},{4,5},{5,4},{6,7},{7,6},{8,9},{9,8},{10,11... | collective-permute-start | bytes 393224 | tf_op jit(solution)/shard_map/ppermute | solution.py:167
  39.0 6.4 %collective-permute-start.14 = (f32[2,128,128]{2,1,0:T(8,128)S(1)}, f32[2,128,128]{2,1,0:T(8,128)S(1)}, u32[]{:S(2)}, u32[]{:S(2)}) collective-permute-start(f32[2,128,128]{2,1,0:T(8,128)S(1)} %get-tuple-element.76), channel_id=1, source_target_pairs={{0,2},{1,3},{2,0},{3,1},{4,6},{5,7},{6,4},{7,5},{8,10},{9,11},{10,... | collective-permute-start | bytes 393224 | tf_op jit(solution)/shard_map/ppermute | solution.py:167
  40.7 7.3 %collective-permute-start.15 = (f32[2,128,128]{2,1,0:T(8,128)S(1)}, f32[2,128,128]{2,1,0:T(8,128)S(1)}, u32[]{:S(2)}, u32[]{:S(2)}) collective-permute-start(f32[2,128,128]{2,1,0:T(8,128)S(1)} %get-tuple-element.77), channel_id=1, source_target_pairs={{0,3},{1,2},{2,1},{3,0},{4,7},{5,6},{6,5},{7,4},{8,11},{9,10},{10,... | collective-permute-start | bytes 393224 | tf_op jit(solution)/shard_map/ppermute | solution.py:167
  41.3 6.7 %collective-permute-start.16 = (f32[2,128,128]{2,1,0:T(8,128)S(1)}, f32[2,128,128]{2,1,0:T(8,128)S(1)}, u32[]{:S(2)}, u32[]{:S(2)}) collective-permute-start(f32[2,128,128]{2,1,0:T(8,128)S(1)} %get-tuple-element.78), channel_id=1, source_target_pairs={{0,1},{1,0},{2,3},{3,2},{4,5},{5,4},{6,7},{7,6},{8,9},{9,8},{10,11... | collective-permute-start | bytes 393224 | tf_op jit(solution)/shard_map/ppermute | solution.py:167
  42.4 8.7 %collective-permute-start.11 = (f32[2,128,128]{2,1,0:T(8,128)S(1)}, f32[2,128,128]{2,1,0:T(8,128)S(1)}, u32[]{:S(2)}, u32[]{:S(2)}) collective-permute-start(f32[2,128,128]{2,1,0:T(8,128)S(1)} %get-tuple-element.73), channel_id=1, source_target_pairs={{0,2},{1,3},{2,0},{3,1},{4,6},{5,7},{6,4},{7,5},{8,10},{9,11},{10,... | collective-permute-start | bytes 393224 | tf_op jit(solution)/shard_map/ppermute | solution.py:167
  44.1 9.6 %collective-permute-start.12 = (f32[2,128,128]{2,1,0:T(8,128)S(1)}, f32[2,128,128]{2,1,0:T(8,128)S(1)}, u32[]{:S(2)}, u32[]{:S(2)}) collective-permute-start(f32[2,128,128]{2,1,0:T(8,128)S(1)} %get-tuple-element.74), channel_id=1, source_target_pairs={{0,3},{1,2},{2,1},{3,0},{4,7},{5,6},{6,5},{7,4},{8,11},{9,10},{10,... | collective-permute-start | bytes 393224 | tf_op jit(solution)/shard_map/ppermute | solution.py:167
  45.4 8.2 %collective-permute-start.13 = (f32[2,128,128]{2,1,0:T(8,128)S(1)}, f32[2,128,128]{2,1,0:T(8,128)S(1)}, u32[]{:S(2)}, u32[]{:S(2)}) collective-permute-start(f32[2,128,128]{2,1,0:T(8,128)S(1)} %get-tuple-element.75), channel_id=1, source_target_pairs={{0,1},{1,0},{2,3},{3,2},{4,5},{5,4},{6,7},{7,6},{8,9},{9,8},{10,11... | collective-permute-start | bytes 393224 | tf_op jit(solution)/shard_map/ppermute | solution.py:167
  49.1 16.9 %collective-permute-start.21 = (f32[2,512,128]{2,1,0:T(8,128)S(1)}, f32[2,512,128]{2,1,0:T(8,128)S(1)}, u32[]{:S(2)}, u32[]{:S(2)}) collective-permute-start(f32[2,512,128]{2,1,0:T(8,128)S(1)} %get-tuple-element.86), channel_id=1, source_target_pairs={{0,4},{4,0},{1,5},{5,1},{2,6},{6,2},{3,7},{7,3},{8,12},{12,8},{9,1... | collective-permute-start | bytes 1572872 | tf_op jit(solution)/shard_map/ppermute | solution.py:167
  55.6 6.4 %collective-permute-start.17 = (f32[2,128,128]{2,1,0:T(8,128)S(1)}, f32[2,128,128]{2,1,0:T(8,128)S(1)}, u32[]{:S(2)}, u32[]{:S(2)}) collective-permute-start(f32[2,128,128]{2,1,0:T(8,128)S(1)} %get-tuple-element.81), channel_id=1, source_target_pairs={{0,2},{1,3},{2,0},{3,1},{4,6},{5,7},{6,4},{7,5},{8,10},{9,11},{10,... | collective-permute-start | bytes 393224 | tf_op jit(solution)/shard_map/ppermute | solution.py:167
  57.5 5.9 %collective-permute-start.18 = (f32[2,128,128]{2,1,0:T(8,128)S(1)}, f32[2,128,128]{2,1,0:T(8,128)S(1)}, u32[]{:S(2)}, u32[]{:S(2)}) collective-permute-start(f32[2,128,128]{2,1,0:T(8,128)S(1)} %get-tuple-element.82), channel_id=1, source_target_pairs={{0,3},{1,2},{2,1},{3,0},{4,7},{5,6},{6,5},{7,4},{8,11},{9,10},{10,... | collective-permute-start | bytes 393224 | tf_op jit(solution)/shard_map/ppermute | solution.py:167
  57.5 5.9 %collective-permute-start.19 = (f32[2,128,128]{2,1,0:T(8,128)S(1)}, f32[2,128,128]{2,1,0:T(8,128)S(1)}, u32[]{:S(2)}, u32[]{:S(2)}) collective-permute-start(f32[2,128,128]{2,1,0:T(8,128)S(1)} %get-tuple-element.83), channel_id=1, source_target_pairs={{0,1},{1,0},{2,3},{3,2},{4,5},{5,4},{6,7},{7,6},{8,9},{9,8},{10,11... | collective-permute-start | bytes 393224 | tf_op jit(solution)/shard_map/ppermute | solution.py:167
  64.5 14.4 %collective-permute-start.20 = (f32[2,512,128]{2,1,0:T(8,128)S(1)}, f32[2,512,128]{2,1,0:T(8,128)S(1)}, u32[]{:S(2)}, u32[]{:S(2)}) collective-permute-start(f32[2,512,128]{2,1,0:T(8,128)S(1)} %get-tuple-element.85), channel_id=1, source_target_pairs={{0,4},{4,0},{1,5},{5,1},{2,6},{6,2},{3,7},{7,3},{8,12},{12,8},{9,1... | collective-permute-start | bytes 1572872 | tf_op jit(solution)/shard_map/ppermute | solution.py:167
  67.2 6.4 %collective-permute-start.22 = (f32[2,128,128]{2,1,0:T(8,128)S(1)}, f32[2,128,128]{2,1,0:T(8,128)S(1)}, u32[]{:S(2)}, u32[]{:S(2)}) collective-permute-start(f32[2,128,128]{2,1,0:T(8,128)S(1)} %get-tuple-element.88), channel_id=1, source_target_pairs={{0,2},{1,3},{2,0},{3,1},{4,6},{5,7},{6,4},{7,5},{8,10},{9,11},{10,... | collective-permute-start | bytes 393224 | tf_op jit(solution)/shard_map/ppermute | solution.py:167
  68.9 6.1 %collective-permute-start.23 = (f32[2,128,128]{2,1,0:T(8,128)S(1)}, f32[2,128,128]{2,1,0:T(8,128)S(1)}, u32[]{:S(2)}, u32[]{:S(2)}) collective-permute-start(f32[2,128,128]{2,1,0:T(8,128)S(1)} %get-tuple-element.89), channel_id=1, source_target_pairs={{0,3},{1,2},{2,1},{3,0},{4,7},{5,6},{6,5},{7,4},{8,11},{9,10},{10,... | collective-permute-start | bytes 393224 | tf_op jit(solution)/shard_map/ppermute | solution.py:167
  69.0 6.1 %collective-permute-start.24 = (f32[2,128,128]{2,1,0:T(8,128)S(1)}, f32[2,128,128]{2,1,0:T(8,128)S(1)}, u32[]{:S(2)}, u32[]{:S(2)}) collective-permute-start(f32[2,128,128]{2,1,0:T(8,128)S(1)} %get-tuple-element.90), channel_id=1, source_target_pairs={{0,1},{1,0},{2,3},{3,2},{4,5},{5,4},{6,7},{7,6},{8,9},{9,8},{10,11... | collective-permute-start | bytes 393224 | tf_op jit(solution)/shard_map/ppermute | solution.py:167
  79.9 5.7 %collective-permute-start.25 = (f32[2,128,128]{2,1,0:T(8,128)S(1)}, f32[2,128,128]{2,1,0:T(8,128)S(1)}, u32[]{:S(2)}, u32[]{:S(2)}) collective-permute-start(f32[2,128,128]{2,1,0:T(8,128)S(1)} %get-tuple-element.92), channel_id=1, source_target_pairs={{0,2},{1,3},{2,0},{3,1},{4,6},{5,7},{6,4},{7,5},{8,10},{9,11},{10,... | collective-permute-start | bytes 393224 | tf_op jit(solution)/shard_map/ppermute | solution.py:167
  81.7 5.8 %collective-permute-start.26 = (f32[2,128,128]{2,1,0:T(8,128)S(1)}, f32[2,128,128]{2,1,0:T(8,128)S(1)}, u32[]{:S(2)}, u32[]{:S(2)}) collective-permute-start(f32[2,128,128]{2,1,0:T(8,128)S(1)} %get-tuple-element.93), channel_id=1, source_target_pairs={{0,3},{1,2},{2,1},{3,0},{4,7},{5,6},{6,5},{7,4},{8,11},{9,10},{10,... | collective-permute-start | bytes 393224 | tf_op jit(solution)/shard_map/ppermute | solution.py:167
  81.7 5.8 %collective-permute-start.27 = (f32[2,128,128]{2,1,0:T(8,128)S(1)}, f32[2,128,128]{2,1,0:T(8,128)S(1)}, u32[]{:S(2)}, u32[]{:S(2)}) collective-permute-start(f32[2,128,128]{2,1,0:T(8,128)S(1)} %get-tuple-element.94), channel_id=1, source_target_pairs={{0,1},{1,0},{2,3},{3,2},{4,5},{5,4},{6,7},{7,6},{8,9},{9,8},{10,11... | collective-permute-start | bytes 393224 | tf_op jit(solution)/shard_map/ppermute | solution.py:167
  88.6 7.1 %collective-permute-start.28 = (f32[256,128]{1,0:T(8,128)S(1)}, f32[256,128]{1,0:T(8,128)S(1)}, u32[]{:S(2)}, u32[]{:S(2)}) collective-permute-start(f32[256,128]{1,0:T(8,128)S(1)} %get-tuple-element.96.refs_2_), channel_id=1, source_target_pairs={{0,8},{8,0},{16,24},{24,16},{1,9},{9,1},{17,25},{25,17},{2,10},{10... | collective-permute-start | bytes 393224 | tf_op jit(solution)/shard_map/ppermute | solution.py:421
  92.1 3.6 %collective-permute-start.29 = (f32[8,128]{1,0:T(8,128)S(1)}, f32[8,128]{1,0:T(8,128)S(1)}, u32[]{:S(2)}, u32[]{:S(2)}) collective-permute-start(f32[8,128]{1,0:T(8,128)S(1)} %shard_map.93.refs_2_.refs_6_), channel_id=1, source_target_pairs={{0,2},{1,3},{2,0},{3,1},{4,6},{5,7},{6,4},{7,5},{8,10},{9,11},{10,... | collective-permute-start | bytes 12296 | tf_op jit(solution)/shard_map/ppermute | solution.py:167
  95.7 8.6 %collective-permute-start.32 = (f32[264,128]{1,0:T(8,128)S(1)}, f32[264,128]{1,0:T(8,128)S(1)}, u32[]{:S(2)}, u32[]{:S(2)}) collective-permute-start(f32[264,128]{1,0:T(8,128)S(1)} %shard_map.94.refs_0_.refs_2_), channel_id=1, source_target_pairs={{0,16},{8,24},{16,0},{24,8},{1,17},{9,25},{17,1},{25,9},{2,18},{10... | collective-permute-start | bytes 405512 | tf_op jit(solution)/shard_map/ppermute | solution.py:421
  104.4 5.4 %collective-permute-start.33 = (f32[264,128]{1,0:T(8,128)S(1)}, f32[264,128]{1,0:T(8,128)S(1)}, u32[]{:S(2)}, u32[]{:S(2)}) collective-permute-start(f32[264,128]{1,0:T(8,128)S(1)} %shard_map.95.refs_0_.refs_2_), channel_id=1, source_target_pairs={{0,8},{8,0},{16,24},{24,16},{1,9},{9,1},{17,25},{25,17},{2,10},{10... | collective-permute-start | bytes 405512 | tf_op jit(solution)/shard_map/ppermute | solution.py:421
  (10 other events, 45.3 us)

commit v2 on v1

--- a/solution.py
+++ b/solution.py
@@ -186,9 +186,9 @@
                     col[k, spot, z * width : (z + 1) * width] = value[:, k * width : (k + 1) * width]
 
 
-def forward_blocks(real, imag, high_ref, low_ref, out_refs):
+def forward_blocks(real, imag, high_ref, low_ref, out_refs, bits):
     me = lax.axis_index("lat")
-    for d, out in zip(turns(len(out_refs)), out_refs):
+    for d, out in zip(bits, out_refs):
         out[0], out[1] = along_y(real, imag, high_ref, low_ref, me ^ d, -1)
 
 
@@ -211,12 +211,12 @@
     copies[1].wait()
     copies[2].wait()
     real, imag = weighted(factor, field[0], field[1])
-    forward_blocks(real, imag, high, low, outs)
+    forward_blocks(real, imag, high, low, outs, turns(lat))
 
 
 def start_body(lat, source, contrast, high_ref, low_ref, *outs):
     real, imag = weighted(contrast, source[0, 0], source[1, 0])
-    forward_blocks(real, imag, high_ref, low_ref, outs)
+    forward_blocks(real, imag, high_ref, low_ref, outs, turns(lat))
 
 
 def turn_body(green, out):
@@ -225,93 +225,129 @@
             out[z, o] = green[z, o].T
 
 
-def couple_body(lat, layers, *refs):
-    parts, (green, high_ref, low_ref), rest = refs[:lat], refs[lat : lat + 3], refs[lat + 3 :]
-    outs, (high, low) = rest[:layers], rest[layers:]
-    me, layer = lax.axis_index("lat"), lax.axis_index("layer")
-    rows, width = parts[0].shape[1:]
-    for d, part in zip(turns(len(parts)), parts):
-        at = pl.ds(pl.multiple_of((me ^ d) * rows, rows), rows)
-        for z in range(2):
-            high[at, z * width : (z + 1) * width], low[at, z * width : (z + 1) * width] = halves(part[z])
-    right_high, right_low = high[...], low[...]
+def blocks_of(bits, width):
+    me = lax.axis_index("lat")
+    return [pl.ds(pl.multiple_of((me ^ d) * width, width), width) for d in bits]
+
+
+def spectrum_part(parts, bits, high_ref, low_ref, k):
+    columns = blocks_of(bits, parts[0].shape[1])
+    high, low = halves(jnp.concatenate([jnp.concatenate([part[0], part[1]], axis=1) for part in parts], axis=0))
+    table_high, table_low = [jnp.concatenate([ref[k, :, at] for at in columns], axis=1) for ref in (high_ref, low_ref)]
+    got = product(table_high, table_low, high, low)
+    rows, width = got.shape[0] // 2, got.shape[1] // 2
+    return got[:rows, :width] + got[rows:, width:], got[:rows, width:] - got[rows:, :width]
+
+
+def spectrum_body(bits, *refs):
+    parts, (high_ref, low_ref, out) = refs[: len(bits)], refs[len(bits) :]
+    rows = high_ref.shape[1] // 2
     for k in range(high_ref.shape[0]):
-        real, imag = along_x(high_ref, low_ref, k, right_high, right_low, -1)
         at = slice(k * rows, (k + 1) * rows)
+        out[0, at], out[1, at] = spectrum_part(parts, bits, high_ref, low_ref, k)
+
+
+def couple_body(bits, *refs):
+    parts, (begun, green, high_ref, low_ref), outs = refs[: len(bits)], refs[len(bits) : len(bits) + 4], refs[len(bits) + 4 :]
+    layer = lax.axis_index("layer")
+    rows = high_ref.shape[1] // 2
+    for k in range(high_ref.shape[0]):
+        at = slice(k * rows, (k + 1) * rows)
+        real, imag = spectrum_part(parts, bits, high_ref, low_ref, k)
+        real, imag = begun[0, at] + real, begun[1, at] + imag
         for e, out in enumerate(outs):
             g_real, g_imag = green[0, layer ^ e, at], green[1, layer ^ e, at]
             out[0, at] = g_real * real - g_imag * imag
             out[1, at] = g_real * imag + g_imag * real
 
 
-def back_body(lat, layers, *refs):
+def back_body(bits, layers, *refs):
     parts, (high_ref, low_ref), outs = refs[:layers], refs[layers : layers + 2], refs[layers + 2 :]
     me = lax.axis_index("lat")
     mixed = [sum((part[z] for part in parts[1:]), parts[0][z]) for z in range(2)]
     high, low = halves(jnp.concatenate(mixed, axis=1))
-    for d, out in zip(turns(lat), outs):
+    for d, out in zip(bits, outs):
         out[0], out[1] = along_x(high_ref, low_ref, me ^ d, high, low, +1)
 
 
-def gather_lanes(parts, field):
-    me = lax.axis_index("lat")
-    width = parts[0].shape[2]
-    for d, part in zip(turns(len(parts)), parts):
-        at = pl.ds(pl.multiple_of((me ^ d) * width, width), width)
-        for z in range(2):
-            field[z, :, at] = part[z]
-
-
-def update(parts, source, contrast, high_ref, low_ref, field):
-    gather_lanes(parts, field)
-    back_real, back_imag = field[0], field[1]
-    width = parts[0].shape[2]
+def field_part(parts, bits, high_ref, low_ref, k, rows):
+    spots = blocks_of(bits, parts[0].shape[2])
+    both = [jnp.concatenate([part[z, rows] for part in parts], axis=1) for z in range(2)]
+    high, low = halves(jnp.concatenate(both, axis=0))
+    table_high, table_low = [jnp.concatenate([ref[k, at] for at in spots], axis=0) for ref in (high_ref, low_ref)]
+    got = product(high, low, table_high, table_low)
+    count, width = got.shape[0] // 2, got.shape[1] // 2
+    return got[:count, :width] - got[count:, width:], got[count:, :width] + got[:count, width:]
+
+
+def field_body(bits, *refs):
+    parts, (high_ref, low_ref, out) = refs[: len(bits)], refs[len(bits) :]
+    width = high_ref.shape[2] // 2
     for k in range(high_ref.shape[0]):
-        real, imag = along_y(back_real, back_imag, high_ref, low_ref, k, +1)
         at = slice(k * width, (k + 1) * width)
-        m_real, m_imag = contrast[0, :, at], contrast[1, :, at]
-        field[0, :, at] = source[0, 0, :, at] + (m_real * real - m_imag * imag)
-        field[1, :, at] = source[1, 0, :, at] + (m_real * imag + m_imag * real)
-
-
-def again_body(lat, *refs):
-    parts, (source, contrast, high_ref, low_ref), rest = refs[:lat], refs[lat : lat + 4], refs[lat + 4 :]
-    outs, field = rest[:-1], rest[-1]
-    update(parts, source, contrast, high_ref, low_ref, field)
-    real, imag = weighted(contrast, field[0], field[1])
-    forward_blocks(real, imag, high_ref, low_ref, outs)
-
-
-def terms_of(parts, source, contrast, efield, high_ref, low_ref, field):
-    update(parts, source, contrast, high_ref, low_ref, field)
-    return efield[0, 0] * field[0] - efield[1, 0] * field[1]
-
-
-def end_body(lat, *refs):
-    parts, (source, contrast, efield, high_ref, low_ref), rest = refs[:lat], refs[lat : lat + 5], refs[lat + 5 :]
+        out[0, :, at], out[1, :, at] = field_part(parts, bits, high_ref, low_ref, k, slice(None))
+
+
+def update(parts, bits, begun, source, contrast, high_ref, low_ref, field, rows=slice(None)):
+    width = high_ref.shape[2] // 2
+    for k in range(high_ref.shape[0]):
+        at = slice(k * width, (k + 1) * width)
+        real, imag = field_part(parts, bits, high_ref, low_ref, k, rows)
+        real, imag = begun[0, rows, at] + real, begun[1, rows, at] + imag
+        m_real, m_imag = contrast[0, rows, at], contrast[1, rows, at]
+        field[0, :, at] = source[0, 0, rows, at] + (m_real * real - m_imag * imag)
+        field[1, :, at] = source[1, 0, rows, at] + (m_real * imag + m_imag * real)
+
+
+def again_body(lat, bits, *refs):
+    parts, (begun, source, contrast, high_ref, low_ref), rest = refs[: len(bits)], refs[len(bits) : len(bits) + 5], refs[len(bits) + 5 :]
+    out, ahead, field = rest
+    update(parts, bits, begun, source, contrast, high_ref, low_ref, field)
+    ahead[0], ahead[1] = weighted(contrast, field[0], field[1])
+    forward_blocks(ahead[0], ahead[1], high_ref, low_ref, [out], turns(lat)[1:2])
+
+
+def rest_body(bits, ahead, high_ref, low_ref, *outs):
+    forward_blocks(ahead[0], ahead[1], high_ref, low_ref, outs, bits)
+
+
+def end_body(bits, *refs):
+    parts, rest = refs[: len(bits)], refs[len(bits) :]
+    (begun, source, contrast, efield, high_ref, low_ref), rest = rest[:6], rest[6:]
     before, out, field = (rest[0] if len(rest) == 3 else None), rest[-2], rest[-1]
-    terms = terms_of(parts, source, contrast, efield, high_ref, low_ref, field)
+    update(parts, bits, begun, source, contrast, high_ref, low_ref, field)
+    terms = efield[0, 0] * field[0] - efield[1, 0] * field[1]
     out[...] = terms if before is None else before[...] + terms
 
 
-def deal_body(lat, *refs):
-    parts, (source, contrast, efield, high_ref, low_ref), rest = refs[:lat], refs[lat : lat + 5], refs[lat + 5 :]
-    before, gone, kept, cell, field = rest
-    cell[...] = before[...] + terms_of(parts, source, contrast, efield, high_ref, low_ref, field)
+def half_rows(which, rows):
+    return pl.ds(pl.multiple_of(which * rows, rows), rows)
+
+
+def deal_body(bits, kept, *refs):
+    parts, rest = refs[: len(bits)], refs[len(bits) :]
+    begun, source, contrast, efield, high_ref, low_ref, before, out, field = rest
     bit = lax.axis_index("freq") & 1
-    width = gone.shape[1]
-    rows = cell.shape[0] // 2
-    for which, out in ((1 - bit, gone), (bit, kept)):
-        block = cell[pl.ds(pl.multiple_of(which * rows, rows), rows)]
-        for k in range(block.shape[1] // width):
-            out[k * rows : (k + 1) * rows] = block[:, k * width : (k + 1) * width]
-
-
-def class_body(cell, kinds, table):
+    count = field.shape[1]
+    at = half_rows(bit if kept else 1 - bit, count)
+    update(parts, bits, begun, source, contrast, high_ref, low_ref, field, at)
+    cell = before[at] + (efield[0, 0, at] * field[0] - efield[1, 0, at] * field[1])
+    width = out.shape[1]
+    for k in range(cell.shape[1] // width):
+        out[k * count : (k + 1) * count] = cell[:, k * width : (k + 1) * width]
+
+
+def class_body(gone, kept, kinds, table):
+    bit = lax.axis_index("freq") & 1
+    count, width = kinds.shape[0] // 2, gone.shape[1]
+    spots = [slice(k * width, (k + 1) * width) for k in range(kinds.shape[1] // width)]
+    sides = []
+    for cell, which in ((gone, 1 - bit), (kept, bit)):
+        sides.append((cell[...], jnp.concatenate([kinds[half_rows(which, count), at] for at in spots], axis=0)))
     lines = []
     for c in range(CLASSES):
-        chosen = jnp.where(kinds[...] == c, cell[...], 0.0)
-        lines.append(jnp.full((1, table.shape[1]), jnp.sum(chosen), jnp.float32))
+        chosen = sum(jnp.where(kind == c, cell, 0.0) for cell, kind in sides)
+        lines.append(jnp.full((1, width), jnp.sum(chosen), jnp.float32))
     table[...] = jnp.concatenate(lines, axis=0)
 
 
@@ -354,11 +390,11 @@
     table_specs, row_specs = [whole(col_shape)] * 2, [whole(row_shape)] * 2
     block = f32(2, rows, rows)
     spectrum = f32(2, length, rows)
-    held = pltpu.VMEM((length, 2 * rows), jnp.bfloat16)
     full = pltpu.VMEM((2, rows, length), jnp.float32)
     stage_flops = 24 * rows * length * length
     last = pols - 1
     order = []
+    bits, near = turns(lat), lat // 2
 
     def kernel(body, outs, args, specs, flops=stage_flops, scratch=(), vmem=VMEM_BYTES):
         got = call(body, outs, args, specs, flops, scratch, tuple(order[-1:]), vmem)
@@ -386,36 +422,63 @@
         return send(kernel(functools.partial(start_body, lat), [block] * lat, (source, contrast, *col), specs), "lat", lat)
 
     def couple(parts):
-        body = functools.partial(couple_body, lat, layers)
-        specs = [whole(block.shape)] * lat + [whole(turned.shape)] + row_specs
-        got = kernel(body, [spectrum] * layers, (*parts, turned, *row), specs, scratch=[held, held])
+        specs = [whole(block.shape)] * near + row_specs
+        begun = kernel(functools.partial(spectrum_body, bits[:near]), [spectrum], (*parts[:near], *row), specs)[0]
+        specs = [whole(block.shape)] * (lat - near) + [whole(spectrum.shape), whole(turned.shape)] + row_specs
+        body = functools.partial(couple_body, bits[near:])
+        got = kernel(body, [spectrum] * layers, (*parts[near:], begun, turned, *row), specs)
         return send(got, "layer", layers)
 
+    early, later = bits[1:2], bits[:1] + bits[2:]
+
+    def turn_block(value, d):
+        return lax.ppermute(value, "lat", [(i, i ^ d) for i in range(lat)])
+
+    def merged(ahead, got):
+        return [got[0], ahead] + [turn_block(value, d) for value, d in zip(got[1:], later[1:])]
+
     def back(parts):
-        body = functools.partial(back_body, lat, layers)
         specs = [whole(spectrum.shape)] * layers + row_specs
-        return send(kernel(body, [block] * lat, (*parts, *row), specs), "lat", lat)
-
-    def field_specs(p):
-        return [whole(block.shape)] * lat + [pick(source.shape, p), whole(contrast.shape)]
+
+        def some(chosen):
+            body = functools.partial(back_body, chosen, layers)
+            return kernel(body, [block] * len(chosen), (*parts, *row), specs, stage_flops * len(chosen) // lat)
+
+        ahead = turn_block(some(early)[0], early[0])
+        return merged(ahead, some(later))
+
+    def fields(p, parts):
+        specs = [whole(block.shape)] * near + table_specs
+        begun = kernel(functools.partial(field_body, bits[:near]), [f32(2, rows, length)], (*parts[:near], *col), specs)[0]
+        specs = [whole(block.shape)] * (lat - near) + [whole(begun.shape), pick(source.shape, p), whole(contrast.shape)]
+        return (*parts[near:], begun, source, contrast), specs
 
     def again(p, parts):
-        args = (*parts, source, contrast, *col)
-        specs = field_specs(p) + table_specs
-        got = kernel(functools.partial(again_body, lat), [block] * lat, args, specs, 2 * stage_flops, [full])
-        return send(got, "lat", lat)
+        args, specs = fields(p, parts)
+        outs = [block, f32(2, rows, length)]
+        body = functools.partial(again_body, lat, bits[near:])
+        got = kernel(body, outs, (*args, *col), specs + table_specs, stage_flops, [full])
+        ahead = turn_block(got[0], early[0])
+        body = functools.partial(rest_body, later)
+        got = kernel(body, [block] * len(later), (got[1], *col), [whole((2, rows, length))] + table_specs)
+        return merged(ahead, got)
 
     def end(p, parts, cells):
         more = () if cells is None else (cells,)
-        specs = field_specs(p) + [pick(efield.shape, p)] + table_specs + [whole((rows, length))] * len(more)
-        args = (*parts, source, contrast, efield, *col, *more)
-        return kernel(functools.partial(end_body, lat), [f32(rows, length)], args, specs, scratch=[full])[0]
-
-    def deal(parts, cells):
-        specs = field_specs(last) + [pick(efield.shape, last)] + table_specs + [whole((rows, length))]
-        args = (*parts, source, contrast, efield, *col, cells)
-        outs = [f32(rows // 2 * (length // 128), 128)] * 2 + [f32(rows, length)]
-        return kernel(functools.partial(deal_body, lat), outs, args, specs, scratch=[full])
+        args, specs = fields(p, parts)
+        specs += [pick(efield.shape, p)] + table_specs + [whole((rows, length))] * len(more)
+        args = (*args, efield, *col, *more)
+        body = functools.partial(end_body, bits[near:])
+        return kernel(body, [f32(rows, length)], args, specs, scratch=[full])[0]
+
+    def deal(operands, cells, kept):
+        args, specs = operands
+        specs = specs + [pick(efield.shape, last)] + table_specs + [whole((rows, length))]
+        args = (*args, efield, *col, cells)
+        outs = [f32(rows // 2 * (length // 128), 128)]
+        scratch = [pltpu.VMEM((2, rows // 2, length), jnp.float32)]
+        body = functools.partial(deal_body, bits[near:], kept)
+        return kernel(body, outs, args, specs, stage_flops // 2, scratch)[0]
 
     def across(value, d):
         return lax.ppermute(value, "freq", [(i, i ^ d) for i in range(freqs)])
@@ -436,19 +499,21 @@
     turned = kernel(turn_body, [f32(2, layers, length, rows)], (green,), [whole(green.shape)], 1 << 20)[0]
     chains = [couple(chain) for chain in chains]
     for step in range(ITERS - 1):
-        turns = [None] * pols
+        moved = [None] * pols
         for p in range(pols):
-            turns[p] = back(chains[p])
+            moved[p] = back(chains[p])
             if p > 0:
-                chains[p - 1] = couple(turns[p - 1])
-            turns[p] = again(p, turns[p])
-        chains[last] = couple(turns[last])
+                chains[p - 1] = couple(moved[p - 1])
+            moved[p] = again(p, moved[p])
+        chains[last] = couple(moved[last])
     cells = jnp.zeros((rows, length), jnp.float32) if last == 0 else None
     for p in range(last):
         cells = end(p, back(chains[p]), cells)
-    gone, kept, terms = deal(back(chains[last]), cells)
+    final = fields(last, back(chains[last]))
+    gone = deal(final, cells, False)
     came = across(gone, 1)
-    found = simple(class_body, (CLASSES, 128), [terms, kinds])
+    kept = deal(final, cells, True)
+    found = simple(class_body, (CLASSES, 128), [gone, kept, kinds])
     found = send([found] * lat, "lat", lat)
     kept = simple(keep_body, (kept.shape[0] + CLASSES, 128), [kept, came, *found])
     d = 2

time: 111 us -> 107 us (0.964)
  waiting for transfers between devices: 57.6 us -> 50.3 us
  Pallas kernels: 21 us -> 24.2 us
    ppermute x31 -> x13, waiting for transfers between devices: 46.3 us -> 17.6 us  [send(): got.append(lax.ppermute(block, axis, [(i, i ^ d) for i in range(size)]))]
    ppermute x0 -> x18, waiting for transfers between devices: none -> 22 us  [turn_block(): return lax.ppermute(value, 'lat', [(i, i ^ d) for i in range(lat)])]
    ppermute x0 -> x18, starting transfers between devices: none -> 13.5 us  [turn_block(): return lax.ppermute(value, 'lat', [(i, i ^ d) for i in range(lat)])]
    ppermute x31 -> x13, starting transfers between devices: 25.6 us -> 12.3 us  [send(): got.append(lax.ppermute(block, axis, [(i, i ^ d) for i in range(size)]))]
    pallas_call x20 -> x35, Pallas kernels: 21 us -> 24.2 us  [call(): pl.pallas_call(ordered, grid=(1,), out_shape=outs, in_specs=list(specs) +...]
  transfers between devices with their start and end apart: 34 -> 34, of which waited for: 22 -> 21; matrix products, arithmetic and copies ran while one was open for 0% -> 0% of each run, Pallas kernels for 12% -> 17%
where the time goes in v2:
time: 107 us
  waiting for transfers between devices  50.3 us (47%)
  starting transfers between devices  30.5 us (29%)
  Pallas kernels  24.2 us (23%)
  local copies, waits for them, and re-layouts  1.14 us (1%)
    pallas_call x35, Pallas kernels, call(): pl.pallas_call(ordered, grid=(1,), out_shape=outs, in_specs=list(specs) +...  24.2 us
    ppermute x18, waiting for transfers between devices, turn_block(): return lax.ppermute(value, 'lat', [(i, i ^ d) for i in range(lat)])  22 us
    ppermute x13, waiting for transfers between devices, send(): got.append(lax.ppermute(block, axis, [(i, i ^ d) for i in range(size)]))  17.6 us
    ppermute x18, starting transfers between devices, turn_block(): return lax.ppermute(value, 'lat', [(i, i ^ d) for i in range(lat)])  13.5 us
    ppermute x13, starting transfers between devices, send(): got.append(lax.ppermute(block, axis, [(i, i ^ d) for i in range(size)]))  12.3 us
    ppermute x3, waiting for transfers between devices, across(): return lax.ppermute(value, 'freq', [(i, i ^ d) for i in range(freqs)])  10.7 us
    ppermute x3, starting transfers between devices, across(): return lax.ppermute(value, 'freq', [(i, i ^ d) for i in range(freqs)])  4.67 us
  transfers between devices with their start and end apart: 34, of which 21 were waited for; matrix products, arithmetic and copies ran while one was open for 0% of the time, Pallas kernels for 17%

profile of v2, /device:TPU:0, one launch (start us, length us, event | category | flops | bytes accessed | tf_op | source)
XLA Modules:
  0.0 107.2 jit_solution(4655103628265196903)
XLA Ops:
  0.7 3.4 %shard_map.77 = (f32[2,128,128]{2,1,0:T(8,128)}, f32[2,128,128]{2,1,0:T(8,128)}, f32[2,128,128]{2,1,0:T(8,128)}, f32[2,128,128]{2,1,0:T(8,128)}) custom-call(f32[2,2,128,512]{3,2,1,0:T(8,128)} %bitcast.6, f32[2,128,512]{2,1,0:T(8,128)} %bitcast.13, f32[2,48,512]{2,1,0:T(8,128)} %constant.2.clone.refs_2_.refs_0_), custom_call_target="tpu_custom_call" | custom-call | flops 805306368 | bytes 1048576 | tf_op jit(solution)/shard_map/pallas_call | solution.py:136
  4.0 3.0 %collective-permute-start.5 = (f32[2,128,128]{2,1,0:T(8,128)}, f32[2,128,128]{2,1,0:T(8,128)S(1)}, u32[]{:S(2)}, u32[]{:S(2)}) collective-permute-start(f32[2,128,128]{2,1,0:T(8,128)} %get-tuple-element.57), channel_id=1, source_target_pairs={{0,2},{1,3},{2,0},{3,1},{4,6},{5,7},{6,4},{7,5},{8,10},{9,11},{10,... | collective-permute-start | bytes 393224 | tf_op jit(solution)/shard_map/ppermute | solution.py:167
  11.9 1.3 %collective-permute-done.3.refs_0_ = f32[2,128,128]{2,1,0:T(8,128)S(1)} collective-permute-done((f32[2,128,128]{2,1,0:T(8,128)}, f32[2,128,128]{2,1,0:T(8,128)S(1)}, u32[]{:S(2)}, u32[]{:S(2)}) %collective-permute-start.3) | collective-permute-done | bytes 131104 | tf_op jit(solution)/shard_map/ppermute | solution.py:167
  13.8 1.5 %collective-permute-start.7 = (f32[2,512,128]{2,1,0:T(8,128)S(1)}, f32[2,512,128]{2,1,0:T(8,128)S(1)}, u32[]{:S(2)}, u32[]{:S(2)}) collective-permute-start(f32[2,512,128]{2,1,0:T(8,128)S(1)} %get-tuple-element.61), channel_id=1, source_target_pairs={{0,4},{4,0},{1,5},{5,1},{2,6},{6,2},{3,7},{7,3},{8,12},{12,8},{9,1... | collective-permute-start | bytes 1572872 | tf_op jit(solution)/shard_map/ppermute | solution.py:167
  15.3 1.2 %collective-permute-start.2 = (f32[2,128,128]{2,1,0:T(8,128)S(1)}, f32[2,128,128]{2,1,0:T(8,128)S(1)}, u32[]{:S(2)}, u32[]{:S(2)}) collective-permute-start(f32[2,128,128]{2,1,0:T(8,128)S(1)} %get-tuple-element.52), channel_id=1, source_target_pairs={{0,2},{1,3},{2,0},{3,1},{4,6},{5,7},{6,4},{7,5},{8,10},{9,11},{10,... | collective-permute-start | bytes 393224 | tf_op jit(solution)/shard_map/ppermute | solution.py:167
  17.4 4.2 %collective-permute-done.2.refs_1_ = f32[2,128,128]{2,1,0:T(8,128)S(1)} collective-permute-done((f32[2,128,128]{2,1,0:T(8,128)S(1)}, f32[2,128,128]{2,1,0:T(8,128)S(1)}, u32[]{:S(2)}, u32[]{:S(2)}) %collective-permute-start.2) | collective-permute-done | bytes 131104 | tf_op jit(solution)/shard_map/ppermute | solution.py:167
  24.1 4.5 %collective-permute-done.7.refs_1_ = f32[2,512,128]{2,1,0:T(8,128)S(1)} collective-permute-done((f32[2,512,128]{2,1,0:T(8,128)S(1)}, f32[2,512,128]{2,1,0:T(8,128)S(1)}, u32[]{:S(2)}, u32[]{:S(2)}) %collective-permute-start.7) | collective-permute-done | bytes 524320 | tf_op jit(solution)/shard_map/ppermute | solution.py:167
  29.0 1.2 %collective-permute-start.10 = (f32[2,128,128]{2,1,0:T(8,128)S(1)}, f32[2,128,128]{2,1,0:T(8,128)S(1)}, u32[]{:S(2)}, u32[]{:S(2)}) collective-permute-start(f32[2,128,128]{2,1,0:T(8,128)S(1)} %shard_map.85.refs_4_), channel_id=1, source_target_pairs={{0,2},{1,3},{2,0},{3,1},{4,6},{5,7},{6,4},{7,5},{8,10},{9,11},{10,... | collective-permute-start | bytes 393224 | tf_op jit(solution)/shard_map/ppermute | solution.py:435
  32.1 2.0 %collective-permute-done.10.refs_1_ = f32[2,128,128]{2,1,0:T(8,128)S(1)} collective-permute-done((f32[2,128,128]{2,1,0:T(8,128)S(1)}, f32[2,128,128]{2,1,0:T(8,128)S(1)}, u32[]{:S(2)}, u32[]{:S(2)}) %collective-permute-start.10) | collective-permute-done | bytes 131104 | tf_op jit(solution)/shard_map/ppermute | solution.py:435
  34.6 2.2 %collective-permute-done.8.refs_0_ = f32[2,128,128]{2,1,0:T(8,128)S(1)} collective-permute-done((f32[2,128,128]{2,1,0:T(8,128)S(1)}, f32[2,128,128]{2,1,0:T(8,128)S(1)}, u32[]{:S(2)}, u32[]{:S(2)}) %collective-permute-start.8) | collective-permute-done | bytes 131104 | tf_op jit(solution)/shard_map/ppermute | solution.py:435
  36.9 1.3 %shard_map.88 = (f32[2,128,128]{2,1,0:T(8,128)S(1)}, f32[2,128,512]{2,1,0:T(8,128)S(1)}) custom-call(f32[2,128,128]{2,1,0:T(8,128)S(1)} %collective-permute-done.8.refs_0_, f32[2,128,128]{2,1,0:T(8,128)S(1)} %collective-permute-done.9.refs_1_, f32[2,128,512]{2,1,0:T(8,128)S(1)} %shard_map.87.refs_2_.refs_7_, f32[2,2,128,512]{3,2,1,0:T(8,128)S(1)} %bitcast.8, ...), custom_call_target="tpu_custom_call" | custom-call | flops 805306368 | bytes 1310720 | tf_op jit(solution)/shard_map/pallas_call | solution.py:136
  40.3 1.2 %collective-permute-start.13 = (f32[2,128,128]{2,1,0:T(8,128)S(1)}, f32[2,128,128]{2,1,0:T(8,128)S(1)}, u32[]{:S(2)}, u32[]{:S(2)}) collective-permute-start(f32[2,128,128]{2,1,0:T(8,128)S(1)} %shard_map.90.refs_4_), channel_id=1, source_target_pairs={{0,2},{1,3},{2,0},{3,1},{4,6},{5,7},{6,4},{7,5},{8,10},{9,11},{10,... | collective-permute-start | bytes 393224 | tf_op jit(solution)/shard_map/ppermute | solution.py:435
  45.2 3.7 %collective-permute-done.14.refs_0_ = f32[2,128,128]{2,1,0:T(8,128)S(1)} collective-permute-done((f32[2,128,128]{2,1,0:T(8,128)S(1)}, f32[2,128,128]{2,1,0:T(8,128)S(1)}, u32[]{:S(2)}, u32[]{:S(2)}) %collective-permute-start.14) | collective-permute-done | bytes 131104 | tf_op jit(solution)/shard_map/ppermute | solution.py:435
  49.5 1.5 %collective-permute-start.21 = (f32[2,512,128]{2,1,0:T(8,128)S(1)}, f32[2,512,128]{2,1,0:T(8,128)S(1)}, u32[]{:S(2)}, u32[]{:S(2)}) collective-permute-start(f32[2,512,128]{2,1,0:T(8,128)S(1)} %get-tuple-element.81), channel_id=1, source_target_pairs={{0,4},{4,0},{1,5},{5,1},{2,6},{6,2},{3,7},{7,3},{8,12},{12,8},{9,1... | collective-permute-start | bytes 1572872 | tf_op jit(solution)/shard_map/ppermute | solution.py:167
  51.7 1.4 %shard_map.95 = (f32[2,128,128]{2,1,0:T(8,128)S(1)}, f32[2,128,512]{2,1,0:T(8,128)S(1)}) custom-call(f32[2,128,128]{2,1,0:T(8,128)S(1)} %collective-permute-done.11.refs_0_, f32[2,128,128]{2,1,0:T(8,128)S(1)} %collective-permute-done.12.refs_1_, f32[2,128,512]{2,1,0:T(8,128)S(1)} %shard_map.94.refs_2_.refs_7_, f32[2,2,128,512]{3,2,1,0:T(8,128)S(1)} %bitcast.9, ...), custom_call_target="tpu_custom_call" | custom-call | flops 805306368 | bytes 1310720 | tf_op jit(solution)/shard_map/pallas_call | solution.py:136
  53.1 2.0 %collective-permute-start.19 = (f32[2,128,128]{2,1,0:T(8,128)S(1)}, f32[2,128,128]{2,1,0:T(8,128)S(1)}, u32[]{:S(2)}, u32[]{:S(2)}) collective-permute-start(f32[2,128,128]{2,1,0:T(8,128)S(1)} %get-tuple-element.75.refs_3_), channel_id=1, source_target_pairs={{0,2},{1,3},{2,0},{3,1},{4,6},{5,7},{6,4},{7,5},{8,10},{9,11},{10,... | collective-permute-start | bytes 393224 | tf_op jit(solution)/shard_map/ppermute | solution.py:435
  56.2 2.9 %collective-permute-done.19.refs_1_ = f32[2,128,128]{2,1,0:T(8,128)S(1)} collective-permute-done((f32[2,128,128]{2,1,0:T(8,128)S(1)}, f32[2,128,128]{2,1,0:T(8,128)S(1)}, u32[]{:S(2)}, u32[]{:S(2)}) %collective-permute-start.19) | collective-permute-done | bytes 131104 | tf_op jit(solution)/shard_map/ppermute | solution.py:435
  59.7 2.2 %collective-permute-done.17.refs_0_ = f32[2,128,128]{2,1,0:T(8,128)S(1)} collective-permute-done((f32[2,128,128]{2,1,0:T(8,128)S(1)}, f32[2,128,128]{2,1,0:T(8,128)S(1)}, u32[]{:S(2)}, u32[]{:S(2)}) %collective-permute-start.17) | collective-permute-done | bytes 131104 | tf_op jit(solution)/shard_map/ppermute | solution.py:435
  62.5 1.4 %collective-permute-start.20 = (f32[2,512,128]{2,1,0:T(8,128)S(1)}, f32[2,512,128]{2,1,0:T(8,128)S(1)}, u32[]{:S(2)}, u32[]{:S(2)}) collective-permute-start(f32[2,512,128]{2,1,0:T(8,128)S(1)} %get-tuple-element.80), channel_id=1, source_target_pairs={{0,4},{4,0},{1,5},{5,1},{2,6},{6,2},{3,7},{7,3},{8,12},{12,8},{9,1... | collective-permute-start | bytes 1572872 | tf_op jit(solution)/shard_map/ppermute | solution.py:167
  64.6 1.7 %collective-permute-start.24 = (f32[2,128,128]{2,1,0:T(8,128)S(1)}, f32[2,128,128]{2,1,0:T(8,128)S(1)}, u32[]{:S(2)}, u32[]{:S(2)}) collective-permute-start(f32[2,128,128]{2,1,0:T(8,128)S(1)} %shard_map.99.refs_4_), channel_id=1, source_target_pairs={{0,2},{1,3},{2,0},{3,1},{4,6},{5,7},{6,4},{7,5},{8,10},{9,11},{10,... | collective-permute-start | bytes 393224 | tf_op jit(solution)/shard_map/ppermute | solution.py:435
  67.7 2.3 %collective-permute-done.24.refs_1_ = f32[2,128,128]{2,1,0:T(8,128)S(1)} collective-permute-done((f32[2,128,128]{2,1,0:T(8,128)S(1)}, f32[2,128,128]{2,1,0:T(8,128)S(1)}, u32[]{:S(2)}, u32[]{:S(2)}) %collective-permute-start.24) | collective-permute-done | bytes 131104 | tf_op jit(solution)/shard_map/ppermute | solution.py:435
  70.6 2.2 %collective-permute-done.22.refs_0_ = f32[2,128,128]{2,1,0:T(8,128)S(1)} collective-permute-done((f32[2,128,128]{2,1,0:T(8,128)S(1)}, f32[2,128,128]{2,1,0:T(8,128)S(1)}, u32[]{:S(2)}, u32[]{:S(2)}) %collective-permute-start.22) | collective-permute-done | bytes 131104 | tf_op jit(solution)/shard_map/ppermute | solution.py:435
  73.4 3.1 %collective-permute-done.20.refs_1_ = f32[2,512,128]{2,1,0:T(8,128)S(1)} collective-permute-done((f32[2,512,128]{2,1,0:T(8,128)S(1)}, f32[2,512,128]{2,1,0:T(8,128)S(1)}, u32[]{:S(2)}, u32[]{:S(2)}) %collective-permute-start.20) | collective-permute-done | bytes 524320 | tf_op jit(solution)/shard_map/ppermute | solution.py:167
  76.9 1.5 %collective-permute-start.27 = (f32[2,128,128]{2,1,0:T(8,128)S(1)}, f32[2,128,128]{2,1,0:T(8,128)S(1)}, u32[]{:S(2)}, u32[]{:S(2)}) collective-permute-start(f32[2,128,128]{2,1,0:T(8,128)S(1)} %shard_map.103.refs_4_), channel_id=1, source_target_pairs={{0,2},{1,3},{2,0},{3,1},{4,6},{5,7},{6,4},{7,5},{8,10},{9,11},{10,... | collective-permute-start | bytes 393224 | tf_op jit(solution)/shard_map/ppermute | solution.py:435
  80.0 2.3 %collective-permute-done.27.refs_1_ = f32[2,128,128]{2,1,0:T(8,128)S(1)} collective-permute-done((f32[2,128,128]{2,1,0:T(8,128)S(1)}, f32[2,128,128]{2,1,0:T(8,128)S(1)}, u32[]{:S(2)}, u32[]{:S(2)}) %collective-permute-start.27) | collective-permute-done | bytes 131104 | tf_op jit(solution)/shard_map/ppermute | solution.py:435
  82.9 2.2 %collective-permute-done.25.refs_0_ = f32[2,128,128]{2,1,0:T(8,128)S(1)} collective-permute-done((f32[2,128,128]{2,1,0:T(8,128)S(1)}, f32[2,128,128]{2,1,0:T(8,128)S(1)}, u32[]{:S(2)}, u32[]{:S(2)}) %collective-permute-start.25) | collective-permute-done | bytes 131104 | tf_op jit(solution)/shard_map/ppermute | solution.py:435
  85.6 1.8 %collective-permute-start.28 = (f32[256,128]{1,0:T(8,128)S(1)}, f32[256,128]{1,0:T(8,128)S(1)}, u32[]{:S(2)}, u32[]{:S(2)}) collective-permute-start(f32[256,128]{1,0:T(8,128)S(1)} %shard_map.106.refs_9_.refs_0_), channel_id=1, source_target_pairs={{0,8},{8,0},{16,24},{24,16},{1,9},{9,1},{17,25},{25,17},{2,10},{10... | collective-permute-start | bytes 393224 | tf_op jit(solution)/shard_map/ppermute | solution.py:484
  89.1 1.2 %collective-permute-start.29 = (f32[8,128]{1,0:T(8,128)S(1)}, f32[8,128]{1,0:T(8,128)S(1)}, u32[]{:S(2)}, u32[]{:S(2)}) collective-permute-start(f32[8,128]{1,0:T(8,128)S(1)} %shard_map.108.refs_2_.refs_6_), channel_id=1, source_target_pairs={{0,2},{1,3},{2,0},{3,1},{4,6},{5,7},{6,4},{7,5},{8,10},{9,11},{10,... | collective-permute-start | bytes 12296 | tf_op jit(solution)/shard_map/ppermute | solution.py:167
  91.3 1.4 %collective-permute-done.29.refs_3_ = f32[8,128]{1,0:T(8,128)S(1)} collective-permute-done((f32[8,128]{1,0:T(8,128)S(1)}, f32[8,128]{1,0:T(8,128)S(1)}, u32[]{:S(2)}, u32[]{:S(2)}) %collective-permute-start.29) | collective-permute-done | bytes 4128 | tf_op jit(solution)/shard_map/ppermute | solution.py:167
  92.8 2.7 %collective-permute-start.32 = (f32[264,128]{1,0:T(8,128)S(1)}, f32[264,128]{1,0:T(8,128)S(1)}, u32[]{:S(2)}, u32[]{:S(2)}) collective-permute-start(f32[264,128]{1,0:T(8,128)S(1)} %shard_map.109.refs_0_.refs_2_), channel_id=1, source_target_pairs={{0,16},{8,24},{16,0},{24,8},{1,17},{9,25},{17,1},{25,9},{2,18},{10... | collective-permute-start | bytes 405512 | tf_op jit(solution)/shard_map/ppermute | solution.py:484
  95.4 5.9 %collective-permute-done.32.refs_1_ = f32[264,128]{1,0:T(8,128)S(1)} collective-permute-done((f32[264,128]{1,0:T(8,128)S(1)}, f32[264,128]{1,0:T(8,128)S(1)}, u32[]{:S(2)}, u32[]{:S(2)}) %collective-permute-start.32) | collective-permute-done | bytes 135200 | tf_op jit(solution)/shard_map/ppermute | solution.py:484
  101.6 4.8 %collective-permute-done.33.refs_1_ = f32[264,128]{1,0:T(8,128)S(1)} collective-permute-done((f32[264,128]{1,0:T(8,128)S(1)}, f32[264,128]{1,0:T(8,128)S(1)}, u32[]{:S(2)}, u32[]{:S(2)}) %collective-permute-start.33) | collective-permute-done | bytes 135200 | tf_op jit(solution)/shard_map/ppermute | solution.py:484
  (85 shorter events, 31.0 us)
Async XLA Ops:
  4.0 7.3 %collective-permute-start.5 = (f32[2,128,128]{2,1,0:T(8,128)}, f32[2,128,128]{2,1,0:T(8,128)S(1)}, u32[]{:S(2)}, u32[]{:S(2)}) collective-permute-start(f32[2,128,128]{2,1,0:T(8,128)} %get-tuple-element.57), channel_id=1, source_target_pairs={{0,2},{1,3},{2,0},{3,1},{4,6},{5,7},{6,4},{7,5},{8,10},{9,11},{10,... | collective-permute-start | bytes 393224 | tf_op jit(solution)/shard_map/ppermute | solution.py:167
  7.1 6.1 %collective-permute-start.3 = (f32[2,128,128]{2,1,0:T(8,128)}, f32[2,128,128]{2,1,0:T(8,128)S(1)}, u32[]{:S(2)}, u32[]{:S(2)}) collective-permute-start(f32[2,128,128]{2,1,0:T(8,128)} %get-tuple-element.55), channel_id=1, source_target_pairs={{0,3},{1,2},{2,1},{3,0},{4,7},{5,6},{6,5},{7,4},{8,11},{9,10},{10,... | collective-permute-start | bytes 393224 | tf_op jit(solution)/shard_map/ppermute | solution.py:167
  7.1 6.1 %collective-permute-start.4 = (f32[2,128,128]{2,1,0:T(8,128)}, f32[2,128,128]{2,1,0:T(8,128)S(1)}, u32[]{:S(2)}, u32[]{:S(2)}) collective-permute-start(f32[2,128,128]{2,1,0:T(8,128)} %get-tuple-element.56), channel_id=1, source_target_pairs={{0,1},{1,0},{2,3},{3,2},{4,5},{5,4},{6,7},{7,6},{8,9},{9,8},{10,11... | collective-permute-start | bytes 393224 | tf_op jit(solution)/shard_map/ppermute | solution.py:167
  13.8 14.8 %collective-permute-start.7 = (f32[2,512,128]{2,1,0:T(8,128)S(1)}, f32[2,512,128]{2,1,0:T(8,128)S(1)}, u32[]{:S(2)}, u32[]{:S(2)}) collective-permute-start(f32[2,512,128]{2,1,0:T(8,128)S(1)} %get-tuple-element.61), channel_id=1, source_target_pairs={{0,4},{4,0},{1,5},{5,1},{2,6},{6,2},{3,7},{7,3},{8,12},{12,8},{9,1... | collective-permute-start | bytes 1572872 | tf_op jit(solution)/shard_map/ppermute | solution.py:167
  15.3 6.3 %collective-permute-start.2 = (f32[2,128,128]{2,1,0:T(8,128)S(1)}, f32[2,128,128]{2,1,0:T(8,128)S(1)}, u32[]{:S(2)}, u32[]{:S(2)}) collective-permute-start(f32[2,128,128]{2,1,0:T(8,128)S(1)} %get-tuple-element.52), channel_id=1, source_target_pairs={{0,2},{1,3},{2,0},{3,1},{4,6},{5,7},{6,4},{7,5},{8,10},{9,11},{10,... | collective-permute-start | bytes 393224 | tf_op jit(solution)/shard_map/ppermute | solution.py:167
  16.5 6.6 %collective-permute-start = (f32[2,128,128]{2,1,0:T(8,128)S(1)}, f32[2,128,128]{2,1,0:T(8,128)S(1)}, u32[]{:S(2)}, u32[]{:S(2)}) collective-permute-start(f32[2,128,128]{2,1,0:T(8,128)S(1)} %get-tuple-element.49), channel_id=1, source_target_pairs={{0,3},{1,2},{2,1},{3,0},{4,7},{5,6},{6,5},{7,4},{8,11},{9,10},{10,... | collective-permute-start | bytes 393224 | tf_op jit(solution)/shard_map/ppermute | solution.py:167
  16.9 6.2 %collective-permute-start.1 = (f32[2,128,128]{2,1,0:T(8,128)S(1)}, f32[2,128,128]{2,1,0:T(8,128)S(1)}, u32[]{:S(2)}, u32[]{:S(2)}) collective-permute-start(f32[2,128,128]{2,1,0:T(8,128)S(1)} %get-tuple-element.50), channel_id=1, source_target_pairs={{0,1},{1,0},{2,3},{3,2},{4,5},{5,4},{6,7},{7,6},{8,9},{9,8},{10,11... | collective-permute-start | bytes 393224 | tf_op jit(solution)/shard_map/ppermute | solution.py:167
  23.8 16.1 %collective-permute-start.6 = (f32[2,512,128]{2,1,0:T(8,128)S(1)}, f32[2,512,128]{2,1,0:T(8,128)S(1)}, u32[]{:S(2)}, u32[]{:S(2)}) collective-permute-start(f32[2,512,128]{2,1,0:T(8,128)S(1)} %get-tuple-element.60), channel_id=1, source_target_pairs={{0,4},{4,0},{1,5},{5,1},{2,6},{6,2},{3,7},{7,3},{8,12},{12,8},{9,1... | collective-permute-start | bytes 1572872 | tf_op jit(solution)/shard_map/ppermute | solution.py:167
  29.0 5.0 %collective-permute-start.10 = (f32[2,128,128]{2,1,0:T(8,128)S(1)}, f32[2,128,128]{2,1,0:T(8,128)S(1)}, u32[]{:S(2)}, u32[]{:S(2)}) collective-permute-start(f32[2,128,128]{2,1,0:T(8,128)S(1)} %shard_map.85.refs_4_), channel_id=1, source_target_pairs={{0,2},{1,3},{2,0},{3,1},{4,6},{5,7},{6,4},{7,5},{8,10},{9,11},{10,... | collective-permute-start | bytes 393224 | tf_op jit(solution)/shard_map/ppermute | solution.py:435
  31.1 5.8 %collective-permute-start.8 = (f32[2,128,128]{2,1,0:T(8,128)S(1)}, f32[2,128,128]{2,1,0:T(8,128)S(1)}, u32[]{:S(2)}, u32[]{:S(2)}) collective-permute-start(f32[2,128,128]{2,1,0:T(8,128)S(1)} %get-tuple-element.62), channel_id=1, source_target_pairs={{0,3},{1,2},{2,1},{3,0},{4,7},{5,6},{6,5},{7,4},{8,11},{9,10},{10,... | collective-permute-start | bytes 393224 | tf_op jit(solution)/shard_map/ppermute | solution.py:435
  31.2 5.7 %collective-permute-start.9 = (f32[2,128,128]{2,1,0:T(8,128)S(1)}, f32[2,128,128]{2,1,0:T(8,128)S(1)}, u32[]{:S(2)}, u32[]{:S(2)}) collective-permute-start(f32[2,128,128]{2,1,0:T(8,128)S(1)} %get-tuple-element.63), channel_id=1, source_target_pairs={{0,1},{1,0},{2,3},{3,2},{4,5},{5,4},{6,7},{7,6},{8,9},{9,8},{10,11... | collective-permute-start | bytes 393224 | tf_op jit(solution)/shard_map/ppermute | solution.py:435
  38.1 6.0 %collective-permute-start.16 = (f32[2,128,128]{2,1,0:T(8,128)S(1)}, f32[2,128,128]{2,1,0:T(8,128)S(1)}, u32[]{:S(2)}, u32[]{:S(2)}) collective-permute-start(f32[2,128,128]{2,1,0:T(8,128)S(1)} %get-tuple-element.66.refs_3_), channel_id=1, source_target_pairs={{0,2},{1,3},{2,0},{3,1},{4,6},{5,7},{6,4},{7,5},{8,10},{9,11},{10,... | collective-permute-start | bytes 393224 | tf_op jit(solution)/shard_map/ppermute | solution.py:435
  40.3 10.7 %collective-permute-start.13 = (f32[2,128,128]{2,1,0:T(8,128)S(1)}, f32[2,128,128]{2,1,0:T(8,128)S(1)}, u32[]{:S(2)}, u32[]{:S(2)}) collective-permute-start(f32[2,128,128]{2,1,0:T(8,128)S(1)} %shard_map.90.refs_4_), channel_id=1, source_target_pairs={{0,2},{1,3},{2,0},{3,1},{4,6},{5,7},{6,4},{7,5},{8,10},{9,11},{10,... | collective-permute-start | bytes 393224 | tf_op jit(solution)/shard_map/ppermute | solution.py:435
  41.5 7.4 %collective-permute-start.14 = (f32[2,128,128]{2,1,0:T(8,128)S(1)}, f32[2,128,128]{2,1,0:T(8,128)S(1)}, u32[]{:S(2)}, u32[]{:S(2)}) collective-permute-start(f32[2,128,128]{2,1,0:T(8,128)S(1)} %get-tuple-element.71), channel_id=1, source_target_pairs={{0,3},{1,2},{2,1},{3,0},{4,7},{5,6},{6,5},{7,4},{8,11},{9,10},{10,... | collective-permute-start | bytes 393224 | tf_op jit(solution)/shard_map/ppermute | solution.py:435
  42.2 6.7 %collective-permute-start.15 = (f32[2,128,128]{2,1,0:T(8,128)S(1)}, f32[2,128,128]{2,1,0:T(8,128)S(1)}, u32[]{:S(2)}, u32[]{:S(2)}) collective-permute-start(f32[2,128,128]{2,1,0:T(8,128)S(1)} %get-tuple-element.72), channel_id=1, source_target_pairs={{0,1},{1,0},{2,3},{3,2},{4,5},{5,4},{6,7},{7,6},{8,9},{9,8},{10,11... | collective-permute-start | bytes 393224 | tf_op jit(solution)/shard_map/ppermute | solution.py:435
  43.4 8.3 %collective-permute-start.11 = (f32[2,128,128]{2,1,0:T(8,128)S(1)}, f32[2,128,128]{2,1,0:T(8,128)S(1)}, u32[]{:S(2)}, u32[]{:S(2)}) collective-permute-start(f32[2,128,128]{2,1,0:T(8,128)S(1)} %get-tuple-element.68), channel_id=1, source_target_pairs={{0,3},{1,2},{2,1},{3,0},{4,7},{5,6},{6,5},{7,4},{8,11},{9,10},{10,... | collective-permute-start | bytes 393224 | tf_op jit(solution)/shard_map/ppermute | solution.py:435
  44.1 7.6 %collective-permute-start.12 = (f32[2,128,128]{2,1,0:T(8,128)S(1)}, f32[2,128,128]{2,1,0:T(8,128)S(1)}, u32[]{:S(2)}, u32[]{:S(2)}) collective-permute-start(f32[2,128,128]{2,1,0:T(8,128)S(1)} %get-tuple-element.69), channel_id=1, source_target_pairs={{0,1},{1,0},{2,3},{3,2},{4,5},{5,4},{6,7},{7,6},{8,9},{9,8},{10,11... | collective-permute-start | bytes 393224 | tf_op jit(solution)/shard_map/ppermute | solution.py:435
  49.5 14.7 %collective-permute-start.21 = (f32[2,512,128]{2,1,0:T(8,128)S(1)}, f32[2,512,128]{2,1,0:T(8,128)S(1)}, u32[]{:S(2)}, u32[]{:S(2)}) collective-permute-start(f32[2,512,128]{2,1,0:T(8,128)S(1)} %get-tuple-element.81), channel_id=1, source_target_pairs={{0,4},{4,0},{1,5},{5,1},{2,6},{6,2},{3,7},{7,3},{8,12},{12,8},{9,1... | collective-permute-start | bytes 1572872 | tf_op jit(solution)/shard_map/ppermute | solution.py:167
  53.1 5.9 %collective-permute-start.19 = (f32[2,128,128]{2,1,0:T(8,128)S(1)}, f32[2,128,128]{2,1,0:T(8,128)S(1)}, u32[]{:S(2)}, u32[]{:S(2)}) collective-permute-start(f32[2,128,128]{2,1,0:T(8,128)S(1)} %get-tuple-element.75.refs_3_), channel_id=1, source_target_pairs={{0,2},{1,3},{2,0},{3,1},{4,6},{5,7},{6,4},{7,5},{8,10},{9,11},{10,... | collective-permute-start | bytes 393224 | tf_op jit(solution)/shard_map/ppermute | solution.py:435
  55.9 5.9 %collective-permute-start.17 = (f32[2,128,128]{2,1,0:T(8,128)S(1)}, f32[2,128,128]{2,1,0:T(8,128)S(1)}, u32[]{:S(2)}, u32[]{:S(2)}) collective-permute-start(f32[2,128,128]{2,1,0:T(8,128)S(1)} %get-tuple-element.76), channel_id=1, source_target_pairs={{0,3},{1,2},{2,1},{3,0},{4,7},{5,6},{6,5},{7,4},{8,11},{9,10},{10,... | collective-permute-start | bytes 393224 | tf_op jit(solution)/shard_map/ppermute | solution.py:435
  56.0 5.9 %collective-permute-start.18 = (f32[2,128,128]{2,1,0:T(8,128)S(1)}, f32[2,128,128]{2,1,0:T(8,128)S(1)}, u32[]{:S(2)}, u32[]{:S(2)}) collective-permute-start(f32[2,128,128]{2,1,0:T(8,128)S(1)} %get-tuple-element.77), channel_id=1, source_target_pairs={{0,1},{1,0},{2,3},{3,2},{4,5},{5,4},{6,7},{7,6},{8,9},{9,8},{10,11... | collective-permute-start | bytes 393224 | tf_op jit(solution)/shard_map/ppermute | solution.py:435
  62.5 14.0 %collective-permute-start.20 = (f32[2,512,128]{2,1,0:T(8,128)S(1)}, f32[2,512,128]{2,1,0:T(8,128)S(1)}, u32[]{:S(2)}, u32[]{:S(2)}) collective-permute-start(f32[2,512,128]{2,1,0:T(8,128)S(1)} %get-tuple-element.80), channel_id=1, source_target_pairs={{0,4},{4,0},{1,5},{5,1},{2,6},{6,2},{3,7},{7,3},{8,12},{12,8},{9,1... | collective-permute-start | bytes 1572872 | tf_op jit(solution)/shard_map/ppermute | solution.py:167
  64.6 5.4 %collective-permute-start.24 = (f32[2,128,128]{2,1,0:T(8,128)S(1)}, f32[2,128,128]{2,1,0:T(8,128)S(1)}, u32[]{:S(2)}, u32[]{:S(2)}) collective-permute-start(f32[2,128,128]{2,1,0:T(8,128)S(1)} %shard_map.99.refs_4_), channel_id=1, source_target_pairs={{0,2},{1,3},{2,0},{3,1},{4,6},{5,7},{6,4},{7,5},{8,10},{9,11},{10,... | collective-permute-start | bytes 393224 | tf_op jit(solution)/shard_map/ppermute | solution.py:435
  67.1 5.7 %collective-permute-start.22 = (f32[2,128,128]{2,1,0:T(8,128)S(1)}, f32[2,128,128]{2,1,0:T(8,128)S(1)}, u32[]{:S(2)}, u32[]{:S(2)}) collective-permute-start(f32[2,128,128]{2,1,0:T(8,128)S(1)} %get-tuple-element.82), channel_id=1, source_target_pairs={{0,3},{1,2},{2,1},{3,0},{4,7},{5,6},{6,5},{7,4},{8,11},{9,10},{10,... | collective-permute-start | bytes 393224 | tf_op jit(solution)/shard_map/ppermute | solution.py:435
  67.2 5.6 %collective-permute-start.23 = (f32[2,128,128]{2,1,0:T(8,128)S(1)}, f32[2,128,128]{2,1,0:T(8,128)S(1)}, u32[]{:S(2)}, u32[]{:S(2)}) collective-permute-start(f32[2,128,128]{2,1,0:T(8,128)S(1)} %get-tuple-element.83), channel_id=1, source_target_pairs={{0,1},{1,0},{2,3},{3,2},{4,5},{5,4},{6,7},{7,6},{8,9},{9,8},{10,11... | collective-permute-start | bytes 393224 | tf_op jit(solution)/shard_map/ppermute | solution.py:435
  76.9 5.4 %collective-permute-start.27 = (f32[2,128,128]{2,1,0:T(8,128)S(1)}, f32[2,128,128]{2,1,0:T(8,128)S(1)}, u32[]{:S(2)}, u32[]{:S(2)}) collective-permute-start(f32[2,128,128]{2,1,0:T(8,128)S(1)} %shard_map.103.refs_4_), channel_id=1, source_target_pairs={{0,2},{1,3},{2,0},{3,1},{4,6},{5,7},{6,4},{7,5},{8,10},{9,11},{10,... | collective-permute-start | bytes 393224 | tf_op jit(solution)/shard_map/ppermute | solution.py:435
  79.3 5.8 %collective-permute-start.25 = (f32[2,128,128]{2,1,0:T(8,128)S(1)}, f32[2,128,128]{2,1,0:T(8,128)S(1)}, u32[]{:S(2)}, u32[]{:S(2)}) collective-permute-start(f32[2,128,128]{2,1,0:T(8,128)S(1)} %get-tuple-element.85), channel_id=1, source_target_pairs={{0,3},{1,2},{2,1},{3,0},{4,7},{5,6},{6,5},{7,4},{8,11},{9,10},{10,... | collective-permute-start | bytes 393224 | tf_op jit(solution)/shard_map/ppermute | solution.py:435
  79.4 5.8 %collective-permute-start.26 = (f32[2,128,128]{2,1,0:T(8,128)S(1)}, f32[2,128,128]{2,1,0:T(8,128)S(1)}, u32[]{:S(2)}, u32[]{:S(2)}) collective-permute-start(f32[2,128,128]{2,1,0:T(8,128)S(1)} %get-tuple-element.86), channel_id=1, source_target_pairs={{0,1},{1,0},{2,3},{3,2},{4,5},{5,4},{6,7},{7,6},{8,9},{9,8},{10,11... | collective-permute-start | bytes 393224 | tf_op jit(solution)/shard_map/ppermute | solution.py:435
  85.6 7.2 %collective-permute-start.28 = (f32[256,128]{1,0:T(8,128)S(1)}, f32[256,128]{1,0:T(8,128)S(1)}, u32[]{:S(2)}, u32[]{:S(2)}) collective-permute-start(f32[256,128]{1,0:T(8,128)S(1)} %shard_map.106.refs_9_.refs_0_), channel_id=1, source_target_pairs={{0,8},{8,0},{16,24},{24,16},{1,9},{9,1},{17,25},{25,17},{2,10},{10... | collective-permute-start | bytes 393224 | tf_op jit(solution)/shard_map/ppermute | solution.py:484
  89.1 3.6 %collective-permute-start.29 = (f32[8,128]{1,0:T(8,128)S(1)}, f32[8,128]{1,0:T(8,128)S(1)}, u32[]{:S(2)}, u32[]{:S(2)}) collective-permute-start(f32[8,128]{1,0:T(8,128)S(1)} %shard_map.108.refs_2_.refs_6_), channel_id=1, source_target_pairs={{0,2},{1,3},{2,0},{3,1},{4,6},{5,7},{6,4},{7,5},{8,10},{9,11},{10,... | collective-permute-start | bytes 12296 | tf_op jit(solution)/shard_map/ppermute | solution.py:167
  92.8 8.6 %collective-permute-start.32 = (f32[264,128]{1,0:T(8,128)S(1)}, f32[264,128]{1,0:T(8,128)S(1)}, u32[]{:S(2)}, u32[]{:S(2)}) collective-permute-start(f32[264,128]{1,0:T(8,128)S(1)} %shard_map.109.refs_0_.refs_2_), channel_id=1, source_target_pairs={{0,16},{8,24},{16,0},{24,8},{1,17},{9,25},{17,1},{25,9},{2,18},{10... | collective-permute-start | bytes 405512 | tf_op jit(solution)/shard_map/ppermute | solution.py:484
  101.3 5.1 %collective-permute-start.33 = (f32[264,128]{1,0:T(8,128)S(1)}, f32[264,128]{1,0:T(8,128)S(1)}, u32[]{:S(2)}, u32[]{:S(2)}) collective-permute-start(f32[264,128]{1,0:T(8,128)S(1)} %shard_map.110.refs_0_.refs_2_), channel_id=1, source_target_pairs={{0,8},{8,0},{16,24},{24,16},{1,9},{9,1},{17,25},{25,17},{2,10},{10... | collective-permute-start | bytes 405512 | tf_op jit(solution)/shard_map/ppermute | solution.py:484
  (9 other events, 35.4 us)

commit v3 on v2

--- a/solution.py
+++ b/solution.py
@@ -83,6 +83,7 @@
 VMEM_BYTES = 40 * 1024 * 1024
 FIRST_VMEM_BYTES = 62 * 1024 * 1024
 FINE = 16
+CHUNKS = 2
 
 
 def small_tables(length):
@@ -255,10 +256,17 @@
         at = slice(k * rows, (k + 1) * rows)
         real, imag = spectrum_part(parts, bits, high_ref, low_ref, k)
         real, imag = begun[0, at] + real, begun[1, at] + imag
-        for e, out in enumerate(outs):
+        chunks = len(outs) // green.shape[1]
+        for e in range(green.shape[1]):
             g_real, g_imag = green[0, layer ^ e, at], green[1, layer ^ e, at]
-            out[0, at] = g_real * real - g_imag * imag
-            out[1, at] = g_real * imag + g_imag * real
+            pair = (g_real * real - g_imag * imag, g_real * imag + g_imag * real)
+            if chunks == 1:
+                outs[e][0, at], outs[e][1, at] = pair
+            else:
+                half = real.shape[1] // chunks
+                for c in range(chunks):
+                    spot = slice(c * half, (c + 1) * half)
+                    outs[e * chunks + c][at] = jnp.concatenate([part[:, spot] for part in pair], axis=1)
 
 
 def back_body(bits, layers, *refs):
@@ -270,29 +278,48 @@
         out[0], out[1] = along_x(high_ref, low_ref, me ^ d, high, low, +1)
 
 
-def field_part(parts, bits, high_ref, low_ref, k, rows):
-    spots = blocks_of(bits, parts[0].shape[2])
-    both = [jnp.concatenate([part[z, rows] for part in parts], axis=1) for z in range(2)]
+def back_chunk_body(bits, layers, *refs):
+    parts, (high_ref, low_ref), outs = refs[:layers], refs[layers : layers + 2], refs[layers + 2 :]
+    me = lax.axis_index("lat")
+    high, low = halves(sum((part[...] for part in parts[1:]), parts[0][...]))
+    for d, out in zip(bits, outs):
+        got = product(high_ref[me ^ d], low_ref[me ^ d], high, low)
+        rows, width = got.shape[0] // 2, got.shape[1]
+        lane = lax.broadcasted_iota(jnp.int32, (rows, width), 1)
+        turned = pltpu.roll(got[rows:], width // 2, 1)
+        out[...] = got[:rows] + jnp.where(lane < width // 2, -turned, turned)
+
+
+def field_part(parts, bits, high_ref, low_ref, k, rows, chunk=None):
+    if chunk is None:
+        spots = blocks_of(bits, parts[0].shape[2])
+        both = [jnp.concatenate([part[z, rows] for part in parts], axis=1) for z in range(2)]
+    else:
+        me = lax.axis_index("lat")
+        half = parts[0].shape[1] // 2
+        spots = [pl.ds(pl.multiple_of(((me ^ d) * CHUNKS + chunk) * half, half), half) for d in bits]
+        lanes = [slice(z * half, (z + 1) * half) for z in range(2)]
+        both = [jnp.concatenate([part[rows, at] for part in parts], axis=1) for at in lanes]
     high, low = halves(jnp.concatenate(both, axis=0))
     table_high, table_low = [jnp.concatenate([ref[k, at] for at in spots], axis=0) for ref in (high_ref, low_ref)]
     got = product(high, low, table_high, table_low)
     count, width = got.shape[0] // 2, got.shape[1] // 2
-    return got[:count, :width] - got[count:, width:], got[count:, :width] + got[:count, width:]
-
-
-def field_body(bits, *refs):
+    return got[:count, :width] - got[count:, width:], got[:count, width:] + got[count:, :width]
+
+
+def field_body(bits, chunk, *refs):
     parts, (high_ref, low_ref, out) = refs[: len(bits)], refs[len(bits) :]
     width = high_ref.shape[2] // 2
     for k in range(high_ref.shape[0]):
         at = slice(k * width, (k + 1) * width)
-        out[0, :, at], out[1, :, at] = field_part(parts, bits, high_ref, low_ref, k, slice(None))
-
-
-def update(parts, bits, begun, source, contrast, high_ref, low_ref, field, rows=slice(None)):
+        out[0, :, at], out[1, :, at] = field_part(parts, bits, high_ref, low_ref, k, slice(None), chunk)
+
+
+def update(parts, bits, begun, source, contrast, high_ref, low_ref, field, rows=slice(None), chunk=None):
     width = high_ref.shape[2] // 2
     for k in range(high_ref.shape[0]):
         at = slice(k * width, (k + 1) * width)
-        real, imag = field_part(parts, bits, high_ref, low_ref, k, rows)
+        real, imag = field_part(parts, bits, high_ref, low_ref, k, rows, chunk)
         real, imag = begun[0, rows, at] + real, begun[1, rows, at] + imag
         m_real, m_imag = contrast[0, rows, at], contrast[1, rows, at]
         field[0, :, at] = source[0, 0, rows, at] + (m_real * real - m_imag * imag)
@@ -330,7 +357,7 @@
     bit = lax.axis_index("freq") & 1
     count = field.shape[1]
     at = half_rows(bit if kept else 1 - bit, count)
-    update(parts, bits, begun, source, contrast, high_ref, low_ref, field, at)
+    update(parts, bits, begun, source, contrast, high_ref, low_ref, field, at, CHUNKS - 1)
     cell = before[at] + (efield[0, 0, at] * field[0] - efield[1, 0, at] * field[1])
     width = out.shape[1]
     for k in range(cell.shape[1] // width):
@@ -421,13 +448,15 @@
         specs = [pick(source.shape, p), whole(contrast.shape)] + table_specs
         return send(kernel(functools.partial(start_body, lat), [block] * lat, (source, contrast, *col), specs), "lat", lat)
 
-    def couple(parts):
+    def couple(parts, chunks=1):
         specs = [whole(block.shape)] * near + row_specs
         begun = kernel(functools.partial(spectrum_body, bits[:near]), [spectrum], (*parts[:near], *row), specs)[0]
         specs = [whole(block.shape)] * (lat - near) + [whole(spectrum.shape), whole(turned.shape)] + row_specs
         body = functools.partial(couple_body, bits[near:])
-        got = kernel(body, [spectrum] * layers, (*parts[near:], begun, turned, *row), specs)
-        return send(got, "layer", layers)
+        outs = [spectrum if chunks == 1 else f32(length, 2 * rows // chunks)] * (layers * chunks)
+        got = kernel(body, outs, (*parts[near:], begun, turned, *row), specs)
+        got = [send(got[c::chunks], "layer", layers) for c in range(chunks)]
+        return got[0] if chunks == 1 else got
 
     early, later = bits[1:2], bits[:1] + bits[2:]
 
@@ -437,19 +466,20 @@
     def merged(ahead, got):
         return [got[0], ahead] + [turn_block(value, d) for value, d in zip(got[1:], later[1:])]
 
-    def back(parts):
-        specs = [whole(spectrum.shape)] * layers + row_specs
+    def back(parts, chunk=False):
+        specs = [whole(parts[0].shape)] * layers + row_specs
 
         def some(chosen):
-            body = functools.partial(back_body, chosen, layers)
-            return kernel(body, [block] * len(chosen), (*parts, *row), specs, stage_flops * len(chosen) // lat)
+            body = functools.partial(back_chunk_body if chunk else back_body, chosen, layers)
+            outs = [f32(rows, parts[0].shape[1]) if chunk else block] * len(chosen)
+            return kernel(body, outs, (*parts, *row), specs, stage_flops * len(chosen) // lat)
 
         ahead = turn_block(some(early)[0], early[0])
         return merged(ahead, some(later))
 
     def fields(p, parts):
         specs = [whole(block.shape)] * near + table_specs
-        begun = kernel(functools.partial(field_body, bits[:near]), [f32(2, rows, length)], (*parts[:near], *col), specs)[0]
+        begun = kernel(functools.partial(field_body, bits[:near], None), [f32(2, rows, length)], (*parts[:near], *col), specs)[0]
         specs = [whole(block.shape)] * (lat - near) + [whole(begun.shape), pick(source.shape, p), whole(contrast.shape)]
         return (*parts[near:], begun, source, contrast), specs
 
@@ -463,13 +493,21 @@
         got = kernel(body, [block] * len(later), (got[1], *col), [whole((2, rows, length))] + table_specs)
         return merged(ahead, got)
 
-    def end(p, parts, cells):
+    def end(p, operands, cells):
         more = () if cells is None else (cells,)
-        args, specs = fields(p, parts)
+        args, specs = operands
         specs += [pick(efield.shape, p)] + table_specs + [whole((rows, length))] * len(more)
         args = (*args, efield, *col, *more)
         body = functools.partial(end_body, bits[near:])
         return kernel(body, [f32(rows, length)], args, specs, scratch=[full])[0]
+
+    def chunk_fields(p, chunks):
+        parts = chunks[0]
+        packed = [whole(part.shape) for part in parts]
+        body = functools.partial(field_body, bits, 0)
+        begun = kernel(body, [f32(2, rows, length)], (*parts, *col), packed + table_specs)[0]
+        specs = packed + [whole(begun.shape), pick(source.shape, p), whole(contrast.shape)]
+        return (*chunks[1], begun, source, contrast), specs
 
     def deal(operands, cells, kept):
         args, specs = operands
@@ -477,7 +515,7 @@
         args = (*args, efield, *col, cells)
         outs = [f32(rows // 2 * (length // 128), 128)]
         scratch = [pltpu.VMEM((2, rows // 2, length), jnp.float32)]
-        body = functools.partial(deal_body, bits[near:], kept)
+        body = functools.partial(deal_body, bits, kept)
         return kernel(body, outs, args, specs, stage_flops // 2, scratch)[0]
 
     def across(value, d):
@@ -505,11 +543,15 @@
             if p > 0:
                 chains[p - 1] = couple(moved[p - 1])
             moved[p] = again(p, moved[p])
-        chains[last] = couple(moved[last])
-    cells = jnp.zeros((rows, length), jnp.float32) if last == 0 else None
-    for p in range(last):
-        cells = end(p, back(chains[p]), cells)
-    final = fields(last, back(chains[last]))
+        chains[last] = couple(moved[last], CHUNKS if step == ITERS - 2 else 1)
+    cells = None
+    for p in range(last - 1):
+        cells = end(p, fields(p, back(chains[p])), cells)
+    begun = fields(last - 1, back(chains[last - 1]))
+    ahead = [back(chains[last][0], True)]
+    cells = end(last - 1, begun, cells)
+    ahead.append(back(chains[last][1], True))
+    final = chunk_fields(last, ahead)
     gone = deal(final, cells, False)
     came = across(gone, 1)
     kept = deal(final, cells, True)

time: 107 us -> 106 us (level)
  waiting for transfers between devices: 50.3 us -> 44.1 us
  starting transfers between devices: 30.5 us -> 33.9 us
  Pallas kernels: 24.2 us -> 25.9 us
    ppermute x18 -> x21, waiting for transfers between devices: 22 us -> 16.8 us  [turn_block(): return lax.ppermute(value, 'lat', [(i, i ^ d) for i in range(lat)])]
    ppermute x18 -> x21, starting transfers between devices: 13.5 us -> 15.9 us  [turn_block(): return lax.ppermute(value, 'lat', [(i, i ^ d) for i in range(lat)])]
    pallas_call x35 -> x37, Pallas kernels: 24.2 us -> 25.9 us  [call(): pl.pallas_call(ordered, grid=(1,), out_shape=outs, in_specs=list(specs) +...]
    ppermute x13 -> x14, waiting for transfers between devices: 17.6 us -> 15.9 us  [send(): got.append(lax.ppermute(block, axis, [(i, i ^ d) for i in range(size)]))]
    ppermute x13 -> x14, starting transfers between devices: 12.3 us -> 13.6 us  [send(): got.append(lax.ppermute(block, axis, [(i, i ^ d) for i in range(size)]))]
  transfers between devices with their start and end apart: 34 -> 38, of which waited for: 21 -> 20; matrix products, arithmetic and copies ran while one was open for 0% -> 0% of each run, Pallas kernels for 17% -> 19%
where the time goes in v3:
time: 106 us
  waiting for transfers between devices  44.1 us (42%)
  starting transfers between devices  33.9 us (32%)
  Pallas kernels  25.9 us (24%)
  local copies, waits for them, and re-layouts  1.15 us (1%)
  between operations  1.06 us (1%)
    pallas_call x37, Pallas kernels, call(): pl.pallas_call(ordered, grid=(1,), out_shape=outs, in_specs=list(specs) +...  25.9 us
    ppermute x21, waiting for transfers between devices, turn_block(): return lax.ppermute(value, 'lat', [(i, i ^ d) for i in range(lat)])  16.8 us
    ppermute x14, waiting for transfers between devices, send(): got.append(lax.ppermute(block, axis, [(i, i ^ d) for i in range(size)]))  15.9 us
    ppermute x21, starting transfers between devices, turn_block(): return lax.ppermute(value, 'lat', [(i, i ^ d) for i in range(lat)])  15.9 us
    ppermute x14, starting transfers between devices, send(): got.append(lax.ppermute(block, axis, [(i, i ^ d) for i in range(size)]))  13.6 us
    ppermute x3, waiting for transfers between devices, across(): return lax.ppermute(value, 'freq', [(i, i ^ d) for i in range(freqs)])  11.4 us
    ppermute x3, starting transfers between devices, across(): return lax.ppermute(value, 'freq', [(i, i ^ d) for i in range(freqs)])  4.44 us
  transfers between devices with their start and end apart: 38, of which 20 were waited for; matrix products, arithmetic and copies ran while one was open for 0% of the time, Pallas kernels for 19%

profile of v3, /device:TPU:0, one launch (start us, length us, event | category | flops | bytes accessed | tf_op | source)
XLA Modules:
  0.0 106.1 jit_solution(16753682480516696622)
XLA Ops:
  0.7 3.4 %shard_map.77 = (f32[2,128,128]{2,1,0:T(8,128)}, f32[2,128,128]{2,1,0:T(8,128)}, f32[2,128,128]{2,1,0:T(8,128)}, f32[2,128,128]{2,1,0:T(8,128)}) custom-call(f32[2,2,128,512]{3,2,1,0:T(8,128)} %bitcast.6, f32[2,128,512]{2,1,0:T(8,128)} %bitcast.13, f32[2,48,512]{2,1,0:T(8,128)} %constant.2.clone.refs_2_.refs_0_), custom_call_target="tpu_custom_call" | custom-call | flops 805306368 | bytes 1048576 | tf_op jit(solution)/shard_map/pallas_call | solution.py:137
  4.0 3.0 %collective-permute-start.5 = (f32[2,128,128]{2,1,0:T(8,128)}, f32[2,128,128]{2,1,0:T(8,128)S(1)}, u32[]{:S(2)}, u32[]{:S(2)}) collective-permute-start(f32[2,128,128]{2,1,0:T(8,128)} %get-tuple-element.62), channel_id=1, source_target_pairs={{0,2},{1,3},{2,0},{3,1},{4,6},{5,7},{6,4},{7,5},{8,10},{9,11},{10,... | collective-permute-start | bytes 393224 | tf_op jit(solution)/shard_map/ppermute | solution.py:168
  8.8 1.0 shard_map.79
  11.9 1.3 %collective-permute-done.3.refs_0_ = f32[2,128,128]{2,1,0:T(8,128)S(1)} collective-permute-done((f32[2,128,128]{2,1,0:T(8,128)}, f32[2,128,128]{2,1,0:T(8,128)S(1)}, u32[]{:S(2)}, u32[]{:S(2)}) %collective-permute-start.3) | collective-permute-done | bytes 131104 | tf_op jit(solution)/shard_map/ppermute | solution.py:168
  13.8 1.5 %collective-permute-start.7 = (f32[2,512,128]{2,1,0:T(8,128)S(1)}, f32[2,512,128]{2,1,0:T(8,128)S(1)}, u32[]{:S(2)}, u32[]{:S(2)}) collective-permute-start(f32[2,512,128]{2,1,0:T(8,128)S(1)} %get-tuple-element.66), channel_id=1, source_target_pairs={{0,4},{4,0},{1,5},{5,1},{2,6},{6,2},{3,7},{7,3},{8,12},{12,8},{9,1... | collective-permute-start | bytes 1572872 | tf_op jit(solution)/shard_map/ppermute | solution.py:168
  15.3 1.2 %collective-permute-start.2 = (f32[2,128,128]{2,1,0:T(8,128)S(1)}, f32[2,128,128]{2,1,0:T(8,128)S(1)}, u32[]{:S(2)}, u32[]{:S(2)}) collective-permute-start(f32[2,128,128]{2,1,0:T(8,128)S(1)} %get-tuple-element.57), channel_id=1, source_target_pairs={{0,2},{1,3},{2,0},{3,1},{4,6},{5,7},{6,4},{7,5},{8,10},{9,11},{10,... | collective-permute-start | bytes 393224 | tf_op jit(solution)/shard_map/ppermute | solution.py:168
  17.4 4.2 %collective-permute-done.2.refs_1_ = f32[2,128,128]{2,1,0:T(8,128)S(1)} collective-permute-done((f32[2,128,128]{2,1,0:T(8,128)S(1)}, f32[2,128,128]{2,1,0:T(8,128)S(1)}, u32[]{:S(2)}, u32[]{:S(2)}) %collective-permute-start.2) | collective-permute-done | bytes 131104 | tf_op jit(solution)/shard_map/ppermute | solution.py:168
  24.1 4.5 %collective-permute-done.7.refs_1_ = f32[2,512,128]{2,1,0:T(8,128)S(1)} collective-permute-done((f32[2,512,128]{2,1,0:T(8,128)S(1)}, f32[2,512,128]{2,1,0:T(8,128)S(1)}, u32[]{:S(2)}, u32[]{:S(2)}) %collective-permute-start.7) | collective-permute-done | bytes 524320 | tf_op jit(solution)/shard_map/ppermute | solution.py:168
  29.0 1.2 %collective-permute-start.10 = (f32[2,128,128]{2,1,0:T(8,128)S(1)}, f32[2,128,128]{2,1,0:T(8,128)S(1)}, u32[]{:S(2)}, u32[]{:S(2)}) collective-permute-start(f32[2,128,128]{2,1,0:T(8,128)S(1)} %shard_map.85.refs_4_), channel_id=1, source_target_pairs={{0,2},{1,3},{2,0},{3,1},{4,6},{5,7},{6,4},{7,5},{8,10},{9,11},{10,... | collective-permute-start | bytes 393224 | tf_op jit(solution)/shard_map/ppermute | solution.py:464
  32.1 2.0 %collective-permute-done.10.refs_1_ = f32[2,128,128]{2,1,0:T(8,128)S(1)} collective-permute-done((f32[2,128,128]{2,1,0:T(8,128)S(1)}, f32[2,128,128]{2,1,0:T(8,128)S(1)}, u32[]{:S(2)}, u32[]{:S(2)}) %collective-permute-start.10) | collective-permute-done | bytes 131104 | tf_op jit(solution)/shard_map/ppermute | solution.py:464
  34.6 2.2 %collective-permute-done.8.refs_0_ = f32[2,128,128]{2,1,0:T(8,128)S(1)} collective-permute-done((f32[2,128,128]{2,1,0:T(8,128)S(1)}, f32[2,128,128]{2,1,0:T(8,128)S(1)}, u32[]{:S(2)}, u32[]{:S(2)}) %collective-permute-start.8) | collective-permute-done | bytes 131104 | tf_op jit(solution)/shard_map/ppermute | solution.py:464
  36.9 1.3 %shard_map.88 = (f32[2,128,128]{2,1,0:T(8,128)S(1)}, f32[2,128,512]{2,1,0:T(8,128)S(1)}) custom-call(f32[2,128,128]{2,1,0:T(8,128)S(1)} %collective-permute-done.8.refs_0_, f32[2,128,128]{2,1,0:T(8,128)S(1)} %collective-permute-done.9.refs_1_, f32[2,128,512]{2,1,0:T(8,128)S(1)} %shard_map.87.refs_2_.refs_7_, f32[2,2,128,512]{3,2,1,0:T(8,128)S(1)} %bitcast.8, ...), custom_call_target="tpu_custom_call" | custom-call | flops 805306368 | bytes 1310720 | tf_op jit(solution)/shard_map/pallas_call | solution.py:137
  40.3 1.2 %collective-permute-start.13 = (f32[2,128,128]{2,1,0:T(8,128)S(1)}, f32[2,128,128]{2,1,0:T(8,128)S(1)}, u32[]{:S(2)}, u32[]{:S(2)}) collective-permute-start(f32[2,128,128]{2,1,0:T(8,128)S(1)} %shard_map.90.refs_4_), channel_id=1, source_target_pairs={{0,2},{1,3},{2,0},{3,1},{4,6},{5,7},{6,4},{7,5},{8,10},{9,11},{10,... | collective-permute-start | bytes 393224 | tf_op jit(solution)/shard_map/ppermute | solution.py:464
  45.2 3.7 %collective-permute-done.14.refs_0_ = f32[2,128,128]{2,1,0:T(8,128)S(1)} collective-permute-done((f32[2,128,128]{2,1,0:T(8,128)S(1)}, f32[2,128,128]{2,1,0:T(8,128)S(1)}, u32[]{:S(2)}, u32[]{:S(2)}) %collective-permute-start.14) | collective-permute-done | bytes 131104 | tf_op jit(solution)/shard_map/ppermute | solution.py:464
  49.5 1.5 %collective-permute-start.21 = (f32[2,512,128]{2,1,0:T(8,128)S(1)}, f32[2,512,128]{2,1,0:T(8,128)S(1)}, u32[]{:S(2)}, u32[]{:S(2)}) collective-permute-start(f32[2,512,128]{2,1,0:T(8,128)S(1)} %get-tuple-element.86), channel_id=1, source_target_pairs={{0,4},{4,0},{1,5},{5,1},{2,6},{6,2},{3,7},{7,3},{8,12},{12,8},{9,1... | collective-permute-start | bytes 1572872 | tf_op jit(solution)/shard_map/ppermute | solution.py:168
  51.7 1.4 %shard_map.95 = (f32[2,128,128]{2,1,0:T(8,128)S(1)}, f32[2,128,512]{2,1,0:T(8,128)S(1)}) custom-call(f32[2,128,128]{2,1,0:T(8,128)S(1)} %collective-permute-done.11.refs_0_, f32[2,128,128]{2,1,0:T(8,128)S(1)} %collective-permute-done.12.refs_1_, f32[2,128,512]{2,1,0:T(8,128)S(1)} %shard_map.94.refs_2_.refs_7_, f32[2,2,128,512]{3,2,1,0:T(8,128)S(1)} %bitcast.9, ...), custom_call_target="tpu_custom_call" | custom-call | flops 805306368 | bytes 1310720 | tf_op jit(solution)/shard_map/pallas_call | solution.py:137
  53.1 2.0 %collective-permute-start.19 = (f32[2,128,128]{2,1,0:T(8,128)S(1)}, f32[2,128,128]{2,1,0:T(8,128)S(1)}, u32[]{:S(2)}, u32[]{:S(2)}) collective-permute-start(f32[2,128,128]{2,1,0:T(8,128)S(1)} %get-tuple-element.80.refs_3_), channel_id=1, source_target_pairs={{0,2},{1,3},{2,0},{3,1},{4,6},{5,7},{6,4},{7,5},{8,10},{9,11},{10,... | collective-permute-start | bytes 393224 | tf_op jit(solution)/shard_map/ppermute | solution.py:464
  56.2 2.9 %collective-permute-done.19.refs_1_ = f32[2,128,128]{2,1,0:T(8,128)S(1)} collective-permute-done((f32[2,128,128]{2,1,0:T(8,128)S(1)}, f32[2,128,128]{2,1,0:T(8,128)S(1)}, u32[]{:S(2)}, u32[]{:S(2)}) %collective-permute-start.19) | collective-permute-done | bytes 131104 | tf_op jit(solution)/shard_map/ppermute | solution.py:464
  59.7 2.2 %collective-permute-done.17.refs_0_ = f32[2,128,128]{2,1,0:T(8,128)S(1)} collective-permute-done((f32[2,128,128]{2,1,0:T(8,128)S(1)}, f32[2,128,128]{2,1,0:T(8,128)S(1)}, u32[]{:S(2)}, u32[]{:S(2)}) %collective-permute-start.17) | collective-permute-done | bytes 131104 | tf_op jit(solution)/shard_map/ppermute | solution.py:464
  62.6 1.4 %collective-permute-start.25 = (f32[512,128]{1,0:T(8,128)S(1)}, f32[512,128]{1,0:T(8,128)S(1)}, u32[]{:S(2)}, u32[]{:S(2)}) collective-permute-start(f32[512,128]{1,0:T(8,128)S(1)} %get-tuple-element.91), channel_id=1, source_target_pairs={{0,4},{4,0},{1,5},{5,1},{2,6},{6,2},{3,7},{7,3},{8,12},{12,8},{9,1... | collective-permute-start | bytes 786440 | tf_op jit(solution)/shard_map/ppermute | solution.py:168
  64.6 1.7 %collective-permute-start.24 = (f32[2,128,128]{2,1,0:T(8,128)S(1)}, f32[2,128,128]{2,1,0:T(8,128)S(1)}, u32[]{:S(2)}, u32[]{:S(2)}) collective-permute-start(f32[2,128,128]{2,1,0:T(8,128)S(1)} %shard_map.99.refs_4_), channel_id=1, source_target_pairs={{0,2},{1,3},{2,0},{3,1},{4,6},{5,7},{6,4},{7,5},{8,10},{9,11},{10,... | collective-permute-start | bytes 393224 | tf_op jit(solution)/shard_map/ppermute | solution.py:464
  66.3 1.4 %collective-permute-start.20 = (f32[512,128]{1,0:T(8,128)S(1)}, f32[512,128]{1,0:T(8,128)S(1)}, u32[]{:S(2)}, u32[]{:S(2)}) collective-permute-start(f32[512,128]{1,0:T(8,128)S(1)} %get-tuple-element.85), channel_id=1, source_target_pairs={{0,4},{4,0},{1,5},{5,1},{2,6},{6,2},{3,7},{7,3},{8,12},{12,8},{9,1... | collective-permute-start | bytes 786440 | tf_op jit(solution)/shard_map/ppermute | solution.py:168
  70.5 1.3 %collective-permute-done.25.refs_1_ = f32[512,128]{1,0:T(8,128)S(1)} collective-permute-done((f32[512,128]{1,0:T(8,128)S(1)}, f32[512,128]{1,0:T(8,128)S(1)}, u32[]{:S(2)}, u32[]{:S(2)}) %collective-permute-start.25) | collective-permute-done | bytes 262176 | tf_op jit(solution)/shard_map/ppermute | solution.py:168
  74.0 1.5 %collective-permute-start.31 = (f32[128,128]{1,0:T(8,128)S(1)}, f32[128,128]{1,0:T(8,128)S(1)}, u32[]{:S(2)}, u32[]{:S(2)}) collective-permute-start(f32[128,128]{1,0:T(8,128)S(1)} %get-tuple-element.97), channel_id=1, source_target_pairs={{0,1},{1,0},{2,3},{3,2},{4,5},{5,4},{6,7},{7,6},{8,9},{9,8},{10,11... | collective-permute-start | bytes 196616 | tf_op jit(solution)/shard_map/ppermute | solution.py:464
  77.1 1.5 %collective-permute-start.26 = (f32[128,128]{1,0:T(8,128)S(1)}, f32[128,128]{1,0:T(8,128)S(1)}, u32[]{:S(2)}, u32[]{:S(2)}) collective-permute-start(f32[128,128]{1,0:T(8,128)S(1)} %shard_map.105.refs_4_), channel_id=1, source_target_pairs={{0,2},{1,3},{2,0},{3,1},{4,6},{5,7},{6,4},{7,5},{8,10},{9,11},{10,... | collective-permute-start | bytes 196616 | tf_op jit(solution)/shard_map/ppermute | solution.py:464
  80.9 3.0 %collective-permute-done.27.refs_2_ = f32[128,128]{1,0:T(8,128)S(1)} collective-permute-done((f32[128,128]{1,0:T(8,128)S(1)}, f32[128,128]{1,0:T(8,128)S(1)}, u32[]{:S(2)}, u32[]{:S(2)}) %collective-permute-start.27) | collective-permute-done | bytes 65568 | tf_op jit(solution)/shard_map/ppermute | solution.py:464
  84.4 1.7 %collective-permute-start.32 = (f32[256,128]{1,0:T(8,128)S(1)}, f32[256,128]{1,0:T(8,128)S(1)}, u32[]{:S(2)}, u32[]{:S(2)}) collective-permute-start(f32[256,128]{1,0:T(8,128)S(1)} %shard_map.108.refs_11_.refs_0_), channel_id=1, source_target_pairs={{0,8},{8,0},{16,24},{24,16},{1,9},{9,1},{17,25},{25,17},{2,10},{10... | collective-permute-start | bytes 393224 | tf_op jit(solution)/shard_map/ppermute | solution.py:522
  87.6 1.5 %collective-permute-start.33 = (f32[8,128]{1,0:T(8,128)S(1)}, f32[8,128]{1,0:T(8,128)S(1)}, u32[]{:S(2)}, u32[]{:S(2)}) collective-permute-start(f32[8,128]{1,0:T(8,128)S(1)} %shard_map.110.refs_2_.refs_6_), channel_id=1, source_target_pairs={{0,2},{1,3},{2,0},{3,1},{4,6},{5,7},{6,4},{7,5},{8,10},{9,11},{10,... | collective-permute-start | bytes 12296 | tf_op jit(solution)/shard_map/ppermute | solution.py:168
  90.1 1.1 %collective-permute-done.33.refs_3_ = f32[8,128]{1,0:T(8,128)S(1)} collective-permute-done((f32[8,128]{1,0:T(8,128)S(1)}, f32[8,128]{1,0:T(8,128)S(1)}, u32[]{:S(2)}, u32[]{:S(2)}) %collective-permute-start.33) | collective-permute-done | bytes 4128 | tf_op jit(solution)/shard_map/ppermute | solution.py:168
  91.3 2.7 %collective-permute-start.36 = (f32[264,128]{1,0:T(8,128)S(1)}, f32[264,128]{1,0:T(8,128)S(1)}, u32[]{:S(2)}, u32[]{:S(2)}) collective-permute-start(f32[264,128]{1,0:T(8,128)S(1)} %shard_map.111.refs_0_.refs_2_), channel_id=1, source_target_pairs={{0,16},{8,24},{16,0},{24,8},{1,17},{9,25},{17,1},{25,9},{2,18},{10... | collective-permute-start | bytes 405512 | tf_op jit(solution)/shard_map/ppermute | solution.py:522
  93.9 6.0 %collective-permute-done.36.refs_1_ = f32[264,128]{1,0:T(8,128)S(1)} collective-permute-done((f32[264,128]{1,0:T(8,128)S(1)}, f32[264,128]{1,0:T(8,128)S(1)}, u32[]{:S(2)}, u32[]{:S(2)}) %collective-permute-start.36) | collective-permute-done | bytes 135200 | tf_op jit(solution)/shard_map/ppermute | solution.py:522
  100.1 5.3 %collective-permute-done.37.refs_1_ = f32[264,128]{1,0:T(8,128)S(1)} collective-permute-done((f32[264,128]{1,0:T(8,128)S(1)}, f32[264,128]{1,0:T(8,128)S(1)}, u32[]{:S(2)}, u32[]{:S(2)}) %collective-permute-start.37) | collective-permute-done | bytes 135200 | tf_op jit(solution)/shard_map/ppermute | solution.py:522
  (95 shorter events, 33.5 us)
Async XLA Ops:
  4.0 7.3 %collective-permute-start.5 = (f32[2,128,128]{2,1,0:T(8,128)}, f32[2,128,128]{2,1,0:T(8,128)S(1)}, u32[]{:S(2)}, u32[]{:S(2)}) collective-permute-start(f32[2,128,128]{2,1,0:T(8,128)} %get-tuple-element.62), channel_id=1, source_target_pairs={{0,2},{1,3},{2,0},{3,1},{4,6},{5,7},{6,4},{7,5},{8,10},{9,11},{10,... | collective-permute-start | bytes 393224 | tf_op jit(solution)/shard_map/ppermute | solution.py:168
  7.1 6.1 %collective-permute-start.3 = (f32[2,128,128]{2,1,0:T(8,128)}, f32[2,128,128]{2,1,0:T(8,128)S(1)}, u32[]{:S(2)}, u32[]{:S(2)}) collective-permute-start(f32[2,128,128]{2,1,0:T(8,128)} %get-tuple-element.60), channel_id=1, source_target_pairs={{0,3},{1,2},{2,1},{3,0},{4,7},{5,6},{6,5},{7,4},{8,11},{9,10},{10,... | collective-permute-start | bytes 393224 | tf_op jit(solution)/shard_map/ppermute | solution.py:168
  7.1 6.1 %collective-permute-start.4 = (f32[2,128,128]{2,1,0:T(8,128)}, f32[2,128,128]{2,1,0:T(8,128)S(1)}, u32[]{:S(2)}, u32[]{:S(2)}) collective-permute-start(f32[2,128,128]{2,1,0:T(8,128)} %get-tuple-element.61), channel_id=1, source_target_pairs={{0,1},{1,0},{2,3},{3,2},{4,5},{5,4},{6,7},{7,6},{8,9},{9,8},{10,11... | collective-permute-start | bytes 393224 | tf_op jit(solution)/shard_map/ppermute | solution.py:168
  13.8 14.8 %collective-permute-start.7 = (f32[2,512,128]{2,1,0:T(8,128)S(1)}, f32[2,512,128]{2,1,0:T(8,128)S(1)}, u32[]{:S(2)}, u32[]{:S(2)}) collective-permute-start(f32[2,512,128]{2,1,0:T(8,128)S(1)} %get-tuple-element.66), channel_id=1, source_target_pairs={{0,4},{4,0},{1,5},{5,1},{2,6},{6,2},{3,7},{7,3},{8,12},{12,8},{9,1... | collective-permute-start | bytes 1572872 | tf_op jit(solution)/shard_map/ppermute | solution.py:168
  15.3 6.3 %collective-permute-start.2 = (f32[2,128,128]{2,1,0:T(8,128)S(1)}, f32[2,128,128]{2,1,0:T(8,128)S(1)}, u32[]{:S(2)}, u32[]{:S(2)}) collective-permute-start(f32[2,128,128]{2,1,0:T(8,128)S(1)} %get-tuple-element.57), channel_id=1, source_target_pairs={{0,2},{1,3},{2,0},{3,1},{4,6},{5,7},{6,4},{7,5},{8,10},{9,11},{10,... | collective-permute-start | bytes 393224 | tf_op jit(solution)/shard_map/ppermute | solution.py:168
  16.5 6.6 %collective-permute-start = (f32[2,128,128]{2,1,0:T(8,128)S(1)}, f32[2,128,128]{2,1,0:T(8,128)S(1)}, u32[]{:S(2)}, u32[]{:S(2)}) collective-permute-start(f32[2,128,128]{2,1,0:T(8,128)S(1)} %get-tuple-element.54), channel_id=1, source_target_pairs={{0,3},{1,2},{2,1},{3,0},{4,7},{5,6},{6,5},{7,4},{8,11},{9,10},{10,... | collective-permute-start | bytes 393224 | tf_op jit(solution)/shard_map/ppermute | solution.py:168
  16.9 6.2 %collective-permute-start.1 = (f32[2,128,128]{2,1,0:T(8,128)S(1)}, f32[2,128,128]{2,1,0:T(8,128)S(1)}, u32[]{:S(2)}, u32[]{:S(2)}) collective-permute-start(f32[2,128,128]{2,1,0:T(8,128)S(1)} %get-tuple-element.55), channel_id=1, source_target_pairs={{0,1},{1,0},{2,3},{3,2},{4,5},{5,4},{6,7},{7,6},{8,9},{9,8},{10,11... | collective-permute-start | bytes 393224 | tf_op jit(solution)/shard_map/ppermute | solution.py:168
  23.8 16.1 %collective-permute-start.6 = (f32[2,512,128]{2,1,0:T(8,128)S(1)}, f32[2,512,128]{2,1,0:T(8,128)S(1)}, u32[]{:S(2)}, u32[]{:S(2)}) collective-permute-start(f32[2,512,128]{2,1,0:T(8,128)S(1)} %get-tuple-element.65), channel_id=1, source_target_pairs={{0,4},{4,0},{1,5},{5,1},{2,6},{6,2},{3,7},{7,3},{8,12},{12,8},{9,1... | collective-permute-start | bytes 1572872 | tf_op jit(solution)/shard_map/ppermute | solution.py:168
  31.1 5.8 %collective-permute-start.8 = (f32[2,128,128]{2,1,0:T(8,128)S(1)}, f32[2,128,128]{2,1,0:T(8,128)S(1)}, u32[]{:S(2)}, u32[]{:S(2)}) collective-permute-start(f32[2,128,128]{2,1,0:T(8,128)S(1)} %get-tuple-element.67), channel_id=1, source_target_pairs={{0,3},{1,2},{2,1},{3,0},{4,7},{5,6},{6,5},{7,4},{8,11},{9,10},{10,... | collective-permute-start | bytes 393224 | tf_op jit(solution)/shard_map/ppermute | solution.py:464
  31.1 5.7 %collective-permute-start.9 = (f32[2,128,128]{2,1,0:T(8,128)S(1)}, f32[2,128,128]{2,1,0:T(8,128)S(1)}, u32[]{:S(2)}, u32[]{:S(2)}) collective-permute-start(f32[2,128,128]{2,1,0:T(8,128)S(1)} %get-tuple-element.68), channel_id=1, source_target_pairs={{0,1},{1,0},{2,3},{3,2},{4,5},{5,4},{6,7},{7,6},{8,9},{9,8},{10,11... | collective-permute-start | bytes 393224 | tf_op jit(solution)/shard_map/ppermute | solution.py:464
  38.1 6.0 %collective-permute-start.16 = (f32[2,128,128]{2,1,0:T(8,128)S(1)}, f32[2,128,128]{2,1,0:T(8,128)S(1)}, u32[]{:S(2)}, u32[]{:S(2)}) collective-permute-start(f32[2,128,128]{2,1,0:T(8,128)S(1)} %get-tuple-element.71.refs_3_), channel_id=1, source_target_pairs={{0,2},{1,3},{2,0},{3,1},{4,6},{5,7},{6,4},{7,5},{8,10},{9,11},{10,... | collective-permute-start | bytes 393224 | tf_op jit(solution)/shard_map/ppermute | solution.py:464
  40.3 10.7 %collective-permute-start.13 = (f32[2,128,128]{2,1,0:T(8,128)S(1)}, f32[2,128,128]{2,1,0:T(8,128)S(1)}, u32[]{:S(2)}, u32[]{:S(2)}) collective-permute-start(f32[2,128,128]{2,1,0:T(8,128)S(1)} %shard_map.90.refs_4_), channel_id=1, source_target_pairs={{0,2},{1,3},{2,0},{3,1},{4,6},{5,7},{6,4},{7,5},{8,10},{9,11},{10,... | collective-permute-start | bytes 393224 | tf_op jit(solution)/shard_map/ppermute | solution.py:464
  41.5 7.4 %collective-permute-start.14 = (f32[2,128,128]{2,1,0:T(8,128)S(1)}, f32[2,128,128]{2,1,0:T(8,128)S(1)}, u32[]{:S(2)}, u32[]{:S(2)}) collective-permute-start(f32[2,128,128]{2,1,0:T(8,128)S(1)} %get-tuple-element.76), channel_id=1, source_target_pairs={{0,3},{1,2},{2,1},{3,0},{4,7},{5,6},{6,5},{7,4},{8,11},{9,10},{10,... | collective-permute-start | bytes 393224 | tf_op jit(solution)/shard_map/ppermute | solution.py:464
  42.2 6.7 %collective-permute-start.15 = (f32[2,128,128]{2,1,0:T(8,128)S(1)}, f32[2,128,128]{2,1,0:T(8,128)S(1)}, u32[]{:S(2)}, u32[]{:S(2)}) collective-permute-start(f32[2,128,128]{2,1,0:T(8,128)S(1)} %get-tuple-element.77), channel_id=1, source_target_pairs={{0,1},{1,0},{2,3},{3,2},{4,5},{5,4},{6,7},{7,6},{8,9},{9,8},{10,11... | collective-permute-start | bytes 393224 | tf_op jit(solution)/shard_map/ppermute | solution.py:464
  43.3 8.3 %collective-permute-start.11 = (f32[2,128,128]{2,1,0:T(8,128)S(1)}, f32[2,128,128]{2,1,0:T(8,128)S(1)}, u32[]{:S(2)}, u32[]{:S(2)}) collective-permute-start(f32[2,128,128]{2,1,0:T(8,128)S(1)} %get-tuple-element.73), channel_id=1, source_target_pairs={{0,3},{1,2},{2,1},{3,0},{4,7},{5,6},{6,5},{7,4},{8,11},{9,10},{10,... | collective-permute-start | bytes 393224 | tf_op jit(solution)/shard_map/ppermute | solution.py:464
  44.1 7.6 %collective-permute-start.12 = (f32[2,128,128]{2,1,0:T(8,128)S(1)}, f32[2,128,128]{2,1,0:T(8,128)S(1)}, u32[]{:S(2)}, u32[]{:S(2)}) collective-permute-start(f32[2,128,128]{2,1,0:T(8,128)S(1)} %get-tuple-element.74), channel_id=1, source_target_pairs={{0,1},{1,0},{2,3},{3,2},{4,5},{5,4},{6,7},{7,6},{8,9},{9,8},{10,11... | collective-permute-start | bytes 393224 | tf_op jit(solution)/shard_map/ppermute | solution.py:464
  49.5 14.6 %collective-permute-start.21 = (f32[2,512,128]{2,1,0:T(8,128)S(1)}, f32[2,512,128]{2,1,0:T(8,128)S(1)}, u32[]{:S(2)}, u32[]{:S(2)}) collective-permute-start(f32[2,512,128]{2,1,0:T(8,128)S(1)} %get-tuple-element.86), channel_id=1, source_target_pairs={{0,4},{4,0},{1,5},{5,1},{2,6},{6,2},{3,7},{7,3},{8,12},{12,8},{9,1... | collective-permute-start | bytes 1572872 | tf_op jit(solution)/shard_map/ppermute | solution.py:168
  53.1 5.9 %collective-permute-start.19 = (f32[2,128,128]{2,1,0:T(8,128)S(1)}, f32[2,128,128]{2,1,0:T(8,128)S(1)}, u32[]{:S(2)}, u32[]{:S(2)}) collective-permute-start(f32[2,128,128]{2,1,0:T(8,128)S(1)} %get-tuple-element.80.refs_3_), channel_id=1, source_target_pairs={{0,2},{1,3},{2,0},{3,1},{4,6},{5,7},{6,4},{7,5},{8,10},{9,11},{10,... | collective-permute-start | bytes 393224 | tf_op jit(solution)/shard_map/ppermute | solution.py:464
  55.9 5.9 %collective-permute-start.17 = (f32[2,128,128]{2,1,0:T(8,128)S(1)}, f32[2,128,128]{2,1,0:T(8,128)S(1)}, u32[]{:S(2)}, u32[]{:S(2)}) collective-permute-start(f32[2,128,128]{2,1,0:T(8,128)S(1)} %get-tuple-element.81), channel_id=1, source_target_pairs={{0,3},{1,2},{2,1},{3,0},{4,7},{5,6},{6,5},{7,4},{8,11},{9,10},{10,... | collective-permute-start | bytes 393224 | tf_op jit(solution)/shard_map/ppermute | solution.py:464
  56.0 5.9 %collective-permute-start.18 = (f32[2,128,128]{2,1,0:T(8,128)S(1)}, f32[2,128,128]{2,1,0:T(8,128)S(1)}, u32[]{:S(2)}, u32[]{:S(2)}) collective-permute-start(f32[2,128,128]{2,1,0:T(8,128)S(1)} %get-tuple-element.82), channel_id=1, source_target_pairs={{0,1},{1,0},{2,3},{3,2},{4,5},{5,4},{6,7},{7,6},{8,9},{9,8},{10,11... | collective-permute-start | bytes 393224 | tf_op jit(solution)/shard_map/ppermute | solution.py:464
  62.6 9.2 %collective-permute-start.25 = (f32[512,128]{1,0:T(8,128)S(1)}, f32[512,128]{1,0:T(8,128)S(1)}, u32[]{:S(2)}, u32[]{:S(2)}) collective-permute-start(f32[512,128]{1,0:T(8,128)S(1)} %get-tuple-element.91), channel_id=1, source_target_pairs={{0,4},{4,0},{1,5},{5,1},{2,6},{6,2},{3,7},{7,3},{8,12},{12,8},{9,1... | collective-permute-start | bytes 786440 | tf_op jit(solution)/shard_map/ppermute | solution.py:168
  64.6 5.3 %collective-permute-start.24 = (f32[2,128,128]{2,1,0:T(8,128)S(1)}, f32[2,128,128]{2,1,0:T(8,128)S(1)}, u32[]{:S(2)}, u32[]{:S(2)}) collective-permute-start(f32[2,128,128]{2,1,0:T(8,128)S(1)} %shard_map.99.refs_4_), channel_id=1, source_target_pairs={{0,2},{1,3},{2,0},{3,1},{4,6},{5,7},{6,4},{7,5},{8,10},{9,11},{10,... | collective-permute-start | bytes 393224 | tf_op jit(solution)/shard_map/ppermute | solution.py:464
  66.3 10.4 %collective-permute-start.20 = (f32[512,128]{1,0:T(8,128)S(1)}, f32[512,128]{1,0:T(8,128)S(1)}, u32[]{:S(2)}, u32[]{:S(2)}) collective-permute-start(f32[512,128]{1,0:T(8,128)S(1)} %get-tuple-element.85), channel_id=1, source_target_pairs={{0,4},{4,0},{1,5},{5,1},{2,6},{6,2},{3,7},{7,3},{8,12},{12,8},{9,1... | collective-permute-start | bytes 786440 | tf_op jit(solution)/shard_map/ppermute | solution.py:168
  68.4 5.5 %collective-permute-start.22 = (f32[2,128,128]{2,1,0:T(8,128)S(1)}, f32[2,128,128]{2,1,0:T(8,128)S(1)}, u32[]{:S(2)}, u32[]{:S(2)}) collective-permute-start(f32[2,128,128]{2,1,0:T(8,128)S(1)} %get-tuple-element.88), channel_id=1, source_target_pairs={{0,3},{1,2},{2,1},{3,0},{4,7},{5,6},{6,5},{7,4},{8,11},{9,10},{10,... | collective-permute-start | bytes 393224 | tf_op jit(solution)/shard_map/ppermute | solution.py:464
  68.5 6.9 %collective-permute-start.23 = (f32[2,128,128]{2,1,0:T(8,128)S(1)}, f32[2,128,128]{2,1,0:T(8,128)S(1)}, u32[]{:S(2)}, u32[]{:S(2)}) collective-permute-start(f32[2,128,128]{2,1,0:T(8,128)S(1)} %get-tuple-element.89), channel_id=1, source_target_pairs={{0,1},{1,0},{2,3},{3,2},{4,5},{5,4},{6,7},{7,6},{8,9},{9,8},{10,11... | collective-permute-start | bytes 393224 | tf_op jit(solution)/shard_map/ppermute | solution.py:464
  72.3 8.0 %collective-permute-start.29 = (f32[128,128]{1,0:T(8,128)S(1)}, f32[128,128]{1,0:T(8,128)S(1)}, u32[]{:S(2)}, u32[]{:S(2)}) collective-permute-start(f32[128,128]{1,0:T(8,128)S(1)} %shard_map.102.refs_4_), channel_id=1, source_target_pairs={{0,2},{1,3},{2,0},{3,1},{4,6},{5,7},{6,4},{7,5},{8,10},{9,11},{10,... | collective-permute-start | bytes 196616 | tf_op jit(solution)/shard_map/ppermute | solution.py:464
  73.9 5.7 %collective-permute-start.30 = (f32[128,128]{1,0:T(8,128)S(1)}, f32[128,128]{1,0:T(8,128)S(1)}, u32[]{:S(2)}, u32[]{:S(2)}) collective-permute-start(f32[128,128]{1,0:T(8,128)S(1)} %get-tuple-element.96), channel_id=1, source_target_pairs={{0,3},{1,2},{2,1},{3,0},{4,7},{5,6},{6,5},{7,4},{8,11},{9,10},{10,... | collective-permute-start | bytes 196616 | tf_op jit(solution)/shard_map/ppermute | solution.py:464
  74.0 6.3 %collective-permute-start.31 = (f32[128,128]{1,0:T(8,128)S(1)}, f32[128,128]{1,0:T(8,128)S(1)}, u32[]{:S(2)}, u32[]{:S(2)}) collective-permute-start(f32[128,128]{1,0:T(8,128)S(1)} %get-tuple-element.97), channel_id=1, source_target_pairs={{0,1},{1,0},{2,3},{3,2},{4,5},{5,4},{6,7},{7,6},{8,9},{9,8},{10,11... | collective-permute-start | bytes 196616 | tf_op jit(solution)/shard_map/ppermute | solution.py:464
  77.1 6.8 %collective-permute-start.26 = (f32[128,128]{1,0:T(8,128)S(1)}, f32[128,128]{1,0:T(8,128)S(1)}, u32[]{:S(2)}, u32[]{:S(2)}) collective-permute-start(f32[128,128]{1,0:T(8,128)S(1)} %shard_map.105.refs_4_), channel_id=1, source_target_pairs={{0,2},{1,3},{2,0},{3,1},{4,6},{5,7},{6,4},{7,5},{8,10},{9,11},{10,... | collective-permute-start | bytes 196616 | tf_op jit(solution)/shard_map/ppermute | solution.py:464
  84.4 6.8 %collective-permute-start.32 = (f32[256,128]{1,0:T(8,128)S(1)}, f32[256,128]{1,0:T(8,128)S(1)}, u32[]{:S(2)}, u32[]{:S(2)}) collective-permute-start(f32[256,128]{1,0:T(8,128)S(1)} %shard_map.108.refs_11_.refs_0_), channel_id=1, source_target_pairs={{0,8},{8,0},{16,24},{24,16},{1,9},{9,1},{17,25},{25,17},{2,10},{10... | collective-permute-start | bytes 393224 | tf_op jit(solution)/shard_map/ppermute | solution.py:522
  91.3 8.7 %collective-permute-start.36 = (f32[264,128]{1,0:T(8,128)S(1)}, f32[264,128]{1,0:T(8,128)S(1)}, u32[]{:S(2)}, u32[]{:S(2)}) collective-permute-start(f32[264,128]{1,0:T(8,128)S(1)} %shard_map.111.refs_0_.refs_2_), channel_id=1, source_target_pairs={{0,16},{8,24},{16,0},{24,8},{1,17},{9,25},{17,1},{25,9},{2,18},{10... | collective-permute-start | bytes 405512 | tf_op jit(solution)/shard_map/ppermute | solution.py:522
  100.0 5.4 %collective-permute-start.37 = (f32[264,128]{1,0:T(8,128)S(1)}, f32[264,128]{1,0:T(8,128)S(1)}, u32[]{:S(2)}, u32[]{:S(2)}) collective-permute-start(f32[264,128]{1,0:T(8,128)S(1)} %shard_map.112.refs_0_.refs_2_), channel_id=1, source_target_pairs={{0,8},{8,0},{16,24},{24,16},{1,9},{9,1},{17,25},{25,17},{2,10},{10... | collective-permute-start | bytes 405512 | tf_op jit(solution)/shard_map/ppermute | solution.py:522
  (13 other events, 53.2 us)

commit v4 on v3

--- a/solution.py
+++ b/solution.py
@@ -199,7 +199,7 @@
 
 
 def first_body(lat, source, contrast, small, *refs):
-    outs, (field, factor, waves, high, low, sems) = refs[:lat], refs[lat:]
+    outs, (field, factor, waves, high, low, sems) = refs[: lat * CHUNKS], refs[lat * CHUNKS :]
     copies = [
         pltpu.make_async_copy(small, waves, sems.at[0]),
         pltpu.make_async_copy(source.at[:, 0], field, sems.at[1]),
@@ -212,7 +212,12 @@
     copies[1].wait()
     copies[2].wait()
     real, imag = weighted(factor, field[0], field[1])
-    forward_blocks(real, imag, high, low, outs, turns(lat))
+    me = lax.axis_index("lat")
+    for i, d in enumerate(turns(lat)):
+        got = along_y(real, imag, high, low, me ^ d, -1)
+        half = got[0].shape[1] // CHUNKS
+        for c in range(CHUNKS):
+            outs[c * lat + i][...] = jnp.concatenate([part[:, c * half : (c + 1) * half] for part in got], axis=1)
 
 
 def start_body(lat, source, contrast, high_ref, low_ref, *outs):
@@ -269,6 +274,58 @@
                     outs[e * chunks + c][at] = jnp.concatenate([part[:, spot] for part in pair], axis=1)
 
 
+def swap(packed):
+    return pltpu.roll(packed, packed.shape[1] // 2, 1)
+
+
+def spectrum_chunk(parts, bits, high_ref, low_ref, k):
+    columns = blocks_of(bits, parts[0].shape[0])
+    high, low = halves(jnp.concatenate([part[...] for part in parts], axis=0))
+    table_high, table_low = [jnp.concatenate([ref[k, :, at] for at in columns], axis=1) for ref in (high_ref, low_ref)]
+    got = product(table_high, table_low, high, low)
+    rows, width = got.shape[0] // 2, got.shape[1]
+    lane = lax.broadcasted_iota(jnp.int32, (rows, width), 1)
+    turned = swap(got[rows:])
+    return got[:rows] + jnp.where(lane < width // 2, turned, -turned)
+
+
+def spectrum_chunk_body(bits, *refs):
+    parts, (high_ref, low_ref, out) = refs[: len(bits)], refs[len(bits) :]
+    rows = high_ref.shape[1] // 2
+    for k in range(high_ref.shape[0]):
+        out[k * rows : (k + 1) * rows] = spectrum_chunk(parts, bits, high_ref, low_ref, k)
+
+
+def couple_chunk_body(bits, chunk, *refs):
+    parts, (begun, green, high_ref, low_ref), outs = refs[: len(bits)], refs[len(bits) : len(bits) + 4], refs[len(bits) + 4 :]
+    layer = lax.axis_index("layer")
+    rows, half = high_ref.shape[1] // 2, begun.shape[1] // 2
+    for k in range(high_ref.shape[0]):
+        at = slice(k * rows, (k + 1) * rows)
+        spectra = begun[at] + spectrum_chunk(parts, bits, high_ref, low_ref, k)
+        swapped = swap(spectra)
+        for e, out in enumerate(outs):
+            g_real, g_imag = [green[z, layer ^ e, at][:, chunk * half : (chunk + 1) * half] for z in range(2)]
+            both = jnp.concatenate([g_real, g_real], axis=1)
+            cross = jnp.concatenate([-g_imag, g_imag], axis=1)
+            out[at] = both * spectra + cross * swapped
+
+
+def back_pair_body(bits, layers, *refs):
+    count = layers * CHUNKS
+    parts, (high_ref, low_ref), outs = refs[:count], refs[count : count + 2], refs[count + 2 :]
+    me = lax.axis_index("lat")
+    mixed = []
+    for c in range(CHUNKS):
+        chunk = parts[c * layers : (c + 1) * layers]
+        mixed.append(sum((part[...] for part in chunk[1:]), chunk[0][...]))
+    half = mixed[0].shape[1] // 2
+    pieces = [part[:, z * half : (z + 1) * half] for z in range(2) for part in mixed]
+    high, low = halves(jnp.concatenate(pieces, axis=1))
+    for d, out in zip(bits, outs):
+        out[0], out[1] = along_x(high_ref, low_ref, me ^ d, high, low, +1)
+
+
 def back_body(bits, layers, *refs):
     parts, (high_ref, low_ref), outs = refs[:layers], refs[layers : layers + 2], refs[layers + 2 :]
     me = lax.axis_index("lat")
@@ -442,7 +499,9 @@
         ]
         body = functools.partial(first_body, lat)
         args = (source, contrast, small)
-        return send(kernel(body, [block] * lat, args, specs, scratch=scratch, vmem=FIRST_VMEM_BYTES), "lat", lat)
+        outs = [f32(rows, 2 * rows // CHUNKS)] * (lat * CHUNKS)
+        got = kernel(body, outs, args, specs, scratch=scratch, vmem=FIRST_VMEM_BYTES)
+        return [send(got[c * lat : (c + 1) * lat], "lat", lat) for c in range(CHUNKS)]
 
     def start(p):
         specs = [pick(source.shape, p), whole(contrast.shape)] + table_specs
@@ -458,6 +517,14 @@
         got = [send(got[c::chunks], "layer", layers) for c in range(chunks)]
         return got[0] if chunks == 1 else got
 
+    def couple_chunk(parts, c):
+        packed, spread = [whole(part.shape) for part in parts], f32(length, parts[0].shape[1])
+        body = functools.partial(spectrum_chunk_body, bits[:near])
+        begun = kernel(body, [spread], (*parts[:near], *row), packed[:near] + row_specs)[0]
+        body = functools.partial(couple_chunk_body, bits[near:], c)
+        specs = packed[near:] + [whole(spread.shape), whole(turned.shape)] + row_specs
+        return send(kernel(body, [spread] * layers, (*parts[near:], begun, turned, *row), specs), "layer", layers)
+
     early, later = bits[1:2], bits[:1] + bits[2:]
 
     def turn_block(value, d):
@@ -467,10 +534,11 @@
         return [got[0], ahead] + [turn_block(value, d) for value, d in zip(got[1:], later[1:])]
 
     def back(parts, chunk=False):
-        specs = [whole(parts[0].shape)] * layers + row_specs
+        specs = [whole(part.shape) for part in parts] + row_specs
+        whole_body = back_pair_body if len(parts) > layers else back_body
 
         def some(chosen):
-            body = functools.partial(back_chunk_body if chunk else back_body, chosen, layers)
+            body = functools.partial(back_chunk_body if chunk else whole_body, chosen, layers)
             outs = [f32(rows, parts[0].shape[1]) if chunk else block] * len(chosen)
             return kernel(body, outs, (*parts, *row), specs, stage_flops * len(chosen) // lat)
 
@@ -533,9 +601,13 @@
         1 << 20,
     )
     col, row = tuple(tables[:2]), tuple(tables[2:])
+    turned = kernel(turn_body, [f32(2, layers, length, rows)], (green,), [whole(green.shape)], 1 << 20)[0]
+    chunks = chains[0]
+    chains[0] = couple_chunk(chunks[0], 0)
     chains += [start(p) for p in range(1, pols)]
-    turned = kernel(turn_body, [f32(2, layers, length, rows)], (green,), [whole(green.shape)], 1 << 20)[0]
-    chains = [couple(chain) for chain in chains]
+    for c in range(1, CHUNKS):
+        chains[0] = chains[0] + couple_chunk(chunks[c], c)
+    chains[1:] = [couple(chain) for chain in chains[1:]]
     for step in range(ITERS - 1):
         moved = [None] * pols
         for p in range(pols):

time: 106 us -> 105 us (level)
  waiting for transfers between devices: 44.1 us -> 38.6 us
  starting transfers between devices: 33.9 us -> 35.8 us
  Pallas kernels: 25.9 us -> 27.7 us
    ppermute x14 -> x18, waiting for transfers between devices: 15.9 us -> 11 us  [send(): got.append(lax.ppermute(block, axis, [(i, i ^ d) for i in range(size)]))]
    ppermute x14 -> x18, starting transfers between devices: 13.6 us -> 15.9 us  [send(): got.append(lax.ppermute(block, axis, [(i, i ^ d) for i in range(size)]))]
    pallas_call x37 -> x39, Pallas kernels: 25.9 us -> 27.7 us  [call(): pl.pallas_call(ordered, grid=(1,), out_shape=outs, in_specs=list(specs) +...]
  transfers between devices with their start and end apart: 38 -> 42, of which waited for: 20 -> 17; matrix products, arithmetic and copies ran while one was open for 0% -> 0% of each run, Pallas kernels for 19% -> 22%
where the time goes in v4:
time: 105 us
  waiting for transfers between devices  38.6 us (37%)
  starting transfers between devices  35.8 us (34%)
  Pallas kernels  27.7 us (26%)
  local copies, waits for them, and re-layouts  1.37 us (1%)
  between operations  1.12 us (1%)
    pallas_call x39, Pallas kernels, call(): pl.pallas_call(ordered, grid=(1,), out_shape=outs, in_specs=list(specs) +...  27.7 us
    ppermute x21, waiting for transfers between devices, turn_block(): return lax.ppermute(value, 'lat', [(i, i ^ d) for i in range(lat)])  16.7 us
    ppermute x18, starting transfers between devices, send(): got.append(lax.ppermute(block, axis, [(i, i ^ d) for i in range(size)]))  15.9 us
    ppermute x21, starting transfers between devices, turn_block(): return lax.ppermute(value, 'lat', [(i, i ^ d) for i in range(lat)])  15.5 us
    ppermute x18, waiting for transfers between devices, send(): got.append(lax.ppermute(block, axis, [(i, i ^ d) for i in range(size)]))  11 us
    ppermute x3, waiting for transfers between devices, across(): return lax.ppermute(value, 'freq', [(i, i ^ d) for i in range(freqs)])  10.9 us
    ppermute x3, starting transfers between devices, across(): return lax.ppermute(value, 'freq', [(i, i ^ d) for i in range(freqs)])  4.37 us
  transfers between devices with their start and end apart: 42, of which 17 were waited for; matrix products, arithmetic and copies ran while one was open for 0% of the time, Pallas kernels for 22%

profile of v4, /device:TPU:0, one launch (start us, length us, event | category | flops | bytes accessed | tf_op | source)
XLA Modules:
  0.0 104.5 jit_solution(16667023317709508818)
XLA Ops:
  0.7 3.4 %shard_map.77 = (f32[128,128]{1,0:T(8,128)}, f32[128,128]{1,0:T(8,128)}, f32[128,128]{1,0:T(8,128)}, f32[128,128]{1,0:T(8,128)}, f32[128,128]{1,0:T(8,128)}, /*i...) custom-call(f32[2,2,128,512]{3,2,1,0:T(8,128)} %bitcast.6, f32[2,128,512]{2,1,0:T(8,128)} %bitcast.13, ...), custom_call_target="tpu_custom_call" | custom-call | flops 805306368 | bytes 1048576 | tf_op jit(solution)/shard_map/pallas_call | solution.py:137
  4.1 3.0 %collective-permute-start.2 = (f32[128,128]{1,0:T(8,128)}, f32[128,128]{1,0:T(8,128)S(1)}, u32[]{:S(2)}, u32[]{:S(2)}) collective-permute-start(f32[128,128]{1,0:T(8,128)} %get-tuple-element.62), channel_id=1, source_target_pairs={{0,2},{1,3},{2,0},{3,1},{4,6},{5,7},{6,4},{7,5},{8,10},{9,11},{10,... | collective-permute-start | bytes 196616 | tf_op jit(solution)/shard_map/ppermute | solution.py:168
  7.3 1.6 %collective-permute-start.6 = (f32[128,128]{1,0:T(8,128)}, f32[128,128]{1,0:T(8,128)S(1)}, u32[]{:S(2)}, u32[]{:S(2)}) collective-permute-start(f32[128,128]{1,0:T(8,128)} %get-tuple-element.70), channel_id=1, source_target_pairs={{0,3},{1,2},{2,1},{3,0},{4,7},{5,6},{6,5},{7,4},{8,11},{9,10},{10,... | collective-permute-start | bytes 196616 | tf_op jit(solution)/shard_map/ppermute | solution.py:168
  13.3 1.9 %collective-permute-start.10 = (f32[512,128]{1,0:T(8,128)S(1)}, f32[512,128]{1,0:T(8,128)S(1)}, u32[]{:S(2)}, u32[]{:S(2)}) collective-permute-start(f32[512,128]{1,0:T(8,128)S(1)} %get-tuple-element.77), channel_id=1, source_target_pairs={{0,4},{4,0},{1,5},{5,1},{2,6},{6,2},{3,7},{7,3},{8,12},{12,8},{9,1... | collective-permute-start | bytes 786440 | tf_op jit(solution)/shard_map/ppermute | solution.py:168
  20.2 4.7 %collective-permute-done.5.refs_1_ = f32[2,128,128]{2,1,0:T(8,128)S(1)} collective-permute-done((f32[2,128,128]{2,1,0:T(8,128)S(1)}, f32[2,128,128]{2,1,0:T(8,128)S(1)}, u32[]{:S(2)}, u32[]{:S(2)}) %collective-permute-start.5) | collective-permute-done | bytes 131104 | tf_op jit(solution)/shard_map/ppermute | solution.py:168
  26.8 1.4 %collective-permute-done.11.refs_3_ = f32[512,128]{1,0:T(8,128)S(1)} collective-permute-done((f32[512,128]{1,0:T(8,128)S(1)}, f32[512,128]{1,0:T(8,128)S(1)}, u32[]{:S(2)}, u32[]{:S(2)}) %collective-permute-start.11) | collective-permute-done | bytes 262176 | tf_op jit(solution)/shard_map/ppermute | solution.py:168
  28.7 1.4 %collective-permute-start.14 = (f32[2,128,128]{2,1,0:T(8,128)S(1)}, f32[2,128,128]{2,1,0:T(8,128)S(1)}, u32[]{:S(2)}, u32[]{:S(2)}) collective-permute-start(f32[2,128,128]{2,1,0:T(8,128)S(1)} %shard_map.87.refs_6_), channel_id=1, source_target_pairs={{0,2},{1,3},{2,0},{3,1},{4,6},{5,7},{6,4},{7,5},{8,10},{9,11},{10,... | collective-permute-start | bytes 393224 | tf_op jit(solution)/shard_map/ppermute | solution.py:531
  31.9 1.8 %collective-permute-done.14.refs_1_ = f32[2,128,128]{2,1,0:T(8,128)S(1)} collective-permute-done((f32[2,128,128]{2,1,0:T(8,128)S(1)}, f32[2,128,128]{2,1,0:T(8,128)S(1)}, u32[]{:S(2)}, u32[]{:S(2)}) %collective-permute-start.14) | collective-permute-done | bytes 131104 | tf_op jit(solution)/shard_map/ppermute | solution.py:531
  34.3 2.2 %collective-permute-done.12.refs_0_ = f32[2,128,128]{2,1,0:T(8,128)S(1)} collective-permute-done((f32[2,128,128]{2,1,0:T(8,128)S(1)}, f32[2,128,128]{2,1,0:T(8,128)S(1)}, u32[]{:S(2)}, u32[]{:S(2)}) %collective-permute-start.12) | collective-permute-done | bytes 131104 | tf_op jit(solution)/shard_map/ppermute | solution.py:531
  36.5 1.3 %shard_map.90 = (f32[2,128,128]{2,1,0:T(8,128)S(1)}, f32[2,128,512]{2,1,0:T(8,128)S(1)}) custom-call(f32[2,128,128]{2,1,0:T(8,128)S(1)} %collective-permute-done.12.refs_0_, f32[2,128,128]{2,1,0:T(8,128)S(1)} %collective-permute-done.13.refs_1_, f32[2,128,512]{2,1,0:T(8,128)S(1)} %shard_map.89.refs_2_.refs_7_, f32[2,2,128,512]{3,2,1,0:T(8,128)S(1)} %bitcast.8, ...), custom_call_target="tpu_custom_call" | custom-call | flops 805306368 | bytes 1310720 | tf_op jit(solution)/shard_map/pallas_call | solution.py:137
  37.8 1.1 %collective-permute-start.20 = (f32[2,128,128]{2,1,0:T(8,128)S(1)}, f32[2,128,128]{2,1,0:T(8,128)S(1)}, u32[]{:S(2)}, u32[]{:S(2)}) collective-permute-start(f32[2,128,128]{2,1,0:T(8,128)S(1)} %get-tuple-element.83.refs_3_), channel_id=1, source_target_pairs={{0,2},{1,3},{2,0},{3,1},{4,6},{5,7},{6,4},{7,5},{8,10},{9,11},{10,... | collective-permute-start | bytes 393224 | tf_op jit(solution)/shard_map/ppermute | solution.py:531
  41.3 1.1 %collective-permute-start.17 = (f32[2,128,128]{2,1,0:T(8,128)S(1)}, f32[2,128,128]{2,1,0:T(8,128)S(1)}, u32[]{:S(2)}, u32[]{:S(2)}) collective-permute-start(f32[2,128,128]{2,1,0:T(8,128)S(1)} %shard_map.92.refs_4_), channel_id=1, source_target_pairs={{0,2},{1,3},{2,0},{3,1},{4,6},{5,7},{6,4},{7,5},{8,10},{9,11},{10,... | collective-permute-start | bytes 393224 | tf_op jit(solution)/shard_map/ppermute | solution.py:531
  47.0 1.8 %collective-permute-done.17.refs_1_ = f32[2,128,128]{2,1,0:T(8,128)S(1)} collective-permute-done((f32[2,128,128]{2,1,0:T(8,128)S(1)}, f32[2,128,128]{2,1,0:T(8,128)S(1)}, u32[]{:S(2)}, u32[]{:S(2)}) %collective-permute-start.17) | collective-permute-done | bytes 131104 | tf_op jit(solution)/shard_map/ppermute | solution.py:531
  49.3 2.0 %collective-permute-done.15.refs_0_ = f32[2,128,128]{2,1,0:T(8,128)S(1)} collective-permute-done((f32[2,128,128]{2,1,0:T(8,128)S(1)}, f32[2,128,128]{2,1,0:T(8,128)S(1)}, u32[]{:S(2)}, u32[]{:S(2)}) %collective-permute-start.15) | collective-permute-done | bytes 131104 | tf_op jit(solution)/shard_map/ppermute | solution.py:531
  51.3 1.3 %shard_map.97 = (f32[2,128,128]{2,1,0:T(8,128)S(1)}, f32[2,128,512]{2,1,0:T(8,128)S(1)}) custom-call(f32[2,128,128]{2,1,0:T(8,128)S(1)} %collective-permute-done.15.refs_0_, f32[2,128,128]{2,1,0:T(8,128)S(1)} %collective-permute-done.16.refs_1_, f32[2,128,512]{2,1,0:T(8,128)S(1)} %shard_map.96.refs_2_.refs_7_, f32[2,2,128,512]{3,2,1,0:T(8,128)S(1)} %bitcast.9, ...), custom_call_target="tpu_custom_call" | custom-call | flops 805306368 | bytes 1310720 | tf_op jit(solution)/shard_map/pallas_call | solution.py:137
  52.6 1.3 %collective-permute-start.23 = (f32[2,128,128]{2,1,0:T(8,128)S(1)}, f32[2,128,128]{2,1,0:T(8,128)S(1)}, u32[]{:S(2)}, u32[]{:S(2)}) collective-permute-start(f32[2,128,128]{2,1,0:T(8,128)S(1)} %get-tuple-element.92.refs_3_), channel_id=1, source_target_pairs={{0,2},{1,3},{2,0},{3,1},{4,6},{5,7},{6,4},{7,5},{8,10},{9,11},{10,... | collective-permute-start | bytes 393224 | tf_op jit(solution)/shard_map/ppermute | solution.py:531
  55.6 3.2 %collective-permute-done.23.refs_1_ = f32[2,128,128]{2,1,0:T(8,128)S(1)} collective-permute-done((f32[2,128,128]{2,1,0:T(8,128)S(1)}, f32[2,128,128]{2,1,0:T(8,128)S(1)}, u32[]{:S(2)}, u32[]{:S(2)}) %collective-permute-start.23) | collective-permute-done | bytes 131104 | tf_op jit(solution)/shard_map/ppermute | solution.py:531
  59.4 1.2 %collective-permute-done.21.refs_0_ = f32[2,128,128]{2,1,0:T(8,128)S(1)} collective-permute-done((f32[2,128,128]{2,1,0:T(8,128)S(1)}, f32[2,128,128]{2,1,0:T(8,128)S(1)}, u32[]{:S(2)}, u32[]{:S(2)}) %collective-permute-start.21) | collective-permute-done | bytes 131104 | tf_op jit(solution)/shard_map/ppermute | solution.py:531
  61.4 1.2 %collective-permute-start.29 = (f32[512,128]{1,0:T(8,128)S(1)}, f32[512,128]{1,0:T(8,128)S(1)}, u32[]{:S(2)}, u32[]{:S(2)}) collective-permute-start(f32[512,128]{1,0:T(8,128)S(1)} %get-tuple-element.103), channel_id=1, source_target_pairs={{0,4},{4,0},{1,5},{5,1},{2,6},{6,2},{3,7},{7,3},{8,12},{12,8},{9,1... | collective-permute-start | bytes 786440 | tf_op jit(solution)/shard_map/ppermute | solution.py:168
  63.0 1.5 %collective-permute-start.28 = (f32[2,128,128]{2,1,0:T(8,128)S(1)}, f32[2,128,128]{2,1,0:T(8,128)S(1)}, u32[]{:S(2)}, u32[]{:S(2)}) collective-permute-start(f32[2,128,128]{2,1,0:T(8,128)S(1)} %shard_map.101.refs_4_), channel_id=1, source_target_pairs={{0,2},{1,3},{2,0},{3,1},{4,6},{5,7},{6,4},{7,5},{8,10},{9,11},{10,... | collective-permute-start | bytes 393224 | tf_op jit(solution)/shard_map/ppermute | solution.py:531
  64.5 1.4 %collective-permute-start.24 = (f32[512,128]{1,0:T(8,128)S(1)}, f32[512,128]{1,0:T(8,128)S(1)}, u32[]{:S(2)}, u32[]{:S(2)}) collective-permute-start(f32[512,128]{1,0:T(8,128)S(1)} %get-tuple-element.97), channel_id=1, source_target_pairs={{0,4},{4,0},{1,5},{5,1},{2,6},{6,2},{3,7},{7,3},{8,12},{12,8},{9,1... | collective-permute-start | bytes 786440 | tf_op jit(solution)/shard_map/ppermute | solution.py:168
  67.0 1.3 %collective-permute-done.28.refs_1_ = f32[2,128,128]{2,1,0:T(8,128)S(1)} collective-permute-done((f32[2,128,128]{2,1,0:T(8,128)S(1)}, f32[2,128,128]{2,1,0:T(8,128)S(1)}, u32[]{:S(2)}, u32[]{:S(2)}) %collective-permute-start.28) | collective-permute-done | bytes 131104 | tf_op jit(solution)/shard_map/ppermute | solution.py:531
  68.9 1.7 %collective-permute-done.29.refs_1_ = f32[512,128]{1,0:T(8,128)S(1)} collective-permute-done((f32[512,128]{1,0:T(8,128)S(1)}, f32[512,128]{1,0:T(8,128)S(1)}, u32[]{:S(2)}, u32[]{:S(2)}) %collective-permute-start.29) | collective-permute-done | bytes 262176 | tf_op jit(solution)/shard_map/ppermute | solution.py:168
  71.0 2.0 %collective-permute-start.33 = (f32[128,128]{1,0:T(8,128)S(1)}, f32[128,128]{1,0:T(8,128)S(1)}, u32[]{:S(2)}, u32[]{:S(2)}) collective-permute-start(f32[128,128]{1,0:T(8,128)S(1)} %shard_map.104.refs_4_), channel_id=1, source_target_pairs={{0,2},{1,3},{2,0},{3,1},{4,6},{5,7},{6,4},{7,5},{8,10},{9,11},{10,... | collective-permute-start | bytes 196616 | tf_op jit(solution)/shard_map/ppermute | solution.py:531
  76.1 1.8 %collective-permute-start.30 = (f32[128,128]{1,0:T(8,128)S(1)}, f32[128,128]{1,0:T(8,128)S(1)}, u32[]{:S(2)}, u32[]{:S(2)}) collective-permute-start(f32[128,128]{1,0:T(8,128)S(1)} %shard_map.107.refs_4_), channel_id=1, source_target_pairs={{0,2},{1,3},{2,0},{3,1},{4,6},{5,7},{6,4},{7,5},{8,10},{9,11},{10,... | collective-permute-start | bytes 196616 | tf_op jit(solution)/shard_map/ppermute | solution.py:531
  79.9 2.7 %collective-permute-done.31.refs_2_ = f32[128,128]{1,0:T(8,128)S(1)} collective-permute-done((f32[128,128]{1,0:T(8,128)S(1)}, f32[128,128]{1,0:T(8,128)S(1)}, u32[]{:S(2)}, u32[]{:S(2)}) %collective-permute-start.31) | collective-permute-done | bytes 65568 | tf_op jit(solution)/shard_map/ppermute | solution.py:531
  83.0 1.6 %collective-permute-start.36 = (f32[256,128]{1,0:T(8,128)S(1)}, f32[256,128]{1,0:T(8,128)S(1)}, u32[]{:S(2)}, u32[]{:S(2)}) collective-permute-start(f32[256,128]{1,0:T(8,128)S(1)} %shard_map.110.refs_11_.refs_0_), channel_id=1, source_target_pairs={{0,8},{8,0},{16,24},{24,16},{1,9},{9,1},{17,25},{25,17},{2,10},{10... | collective-permute-start | bytes 393224 | tf_op jit(solution)/shard_map/ppermute | solution.py:590
  86.5 1.3 %collective-permute-start.37 = (f32[8,128]{1,0:T(8,128)S(1)}, f32[8,128]{1,0:T(8,128)S(1)}, u32[]{:S(2)}, u32[]{:S(2)}) collective-permute-start(f32[8,128]{1,0:T(8,128)S(1)} %shard_map.112.refs_2_.refs_6_), channel_id=1, source_target_pairs={{0,2},{1,3},{2,0},{3,1},{4,6},{5,7},{6,4},{7,5},{8,10},{9,11},{10,... | collective-permute-start | bytes 12296 | tf_op jit(solution)/shard_map/ppermute | solution.py:168
  88.7 1.4 %collective-permute-done.37.refs_3_ = f32[8,128]{1,0:T(8,128)S(1)} collective-permute-done((f32[8,128]{1,0:T(8,128)S(1)}, f32[8,128]{1,0:T(8,128)S(1)}, u32[]{:S(2)}, u32[]{:S(2)}) %collective-permute-start.37) | collective-permute-done | bytes 4128 | tf_op jit(solution)/shard_map/ppermute | solution.py:168
  90.1 2.7 %collective-permute-start.40 = (f32[264,128]{1,0:T(8,128)S(1)}, f32[264,128]{1,0:T(8,128)S(1)}, u32[]{:S(2)}, u32[]{:S(2)}) collective-permute-start(f32[264,128]{1,0:T(8,128)S(1)} %shard_map.113.refs_0_.refs_2_), channel_id=1, source_target_pairs={{0,16},{8,24},{16,0},{24,8},{1,17},{9,25},{17,1},{25,9},{2,18},{10... | collective-permute-start | bytes 405512 | tf_op jit(solution)/shard_map/ppermute | solution.py:590
  92.8 5.7 %collective-permute-done.40.refs_1_ = f32[264,128]{1,0:T(8,128)S(1)} collective-permute-done((f32[264,128]{1,0:T(8,128)S(1)}, f32[264,128]{1,0:T(8,128)S(1)}, u32[]{:S(2)}, u32[]{:S(2)}) %collective-permute-start.40) | collective-permute-done | bytes 135200 | tf_op jit(solution)/shard_map/ppermute | solution.py:590
  98.6 5.1 %collective-permute-done.41.refs_1_ = f32[264,128]{1,0:T(8,128)S(1)} collective-permute-done((f32[264,128]{1,0:T(8,128)S(1)}, f32[264,128]{1,0:T(8,128)S(1)}, u32[]{:S(2)}, u32[]{:S(2)}) %collective-permute-start.41) | collective-permute-done | bytes 135200 | tf_op jit(solution)/shard_map/ppermute | solution.py:590
  (109 shorter events, 36.3 us)
Async XLA Ops:
  4.1 7.1 %collective-permute-start.2 = (f32[128,128]{1,0:T(8,128)}, f32[128,128]{1,0:T(8,128)S(1)}, u32[]{:S(2)}, u32[]{:S(2)}) collective-permute-start(f32[128,128]{1,0:T(8,128)} %get-tuple-element.62), channel_id=1, source_target_pairs={{0,2},{1,3},{2,0},{3,1},{4,6},{5,7},{6,4},{7,5},{8,10},{9,11},{10,... | collective-permute-start | bytes 196616 | tf_op jit(solution)/shard_map/ppermute | solution.py:168
  7.1 5.4 %collective-permute-start = (f32[128,128]{1,0:T(8,128)}, f32[128,128]{1,0:T(8,128)S(1)}, u32[]{:S(2)}, u32[]{:S(2)}) collective-permute-start(f32[128,128]{1,0:T(8,128)} %get-tuple-element.60), channel_id=1, source_target_pairs={{0,3},{1,2},{2,1},{3,0},{4,7},{5,6},{6,5},{7,4},{8,11},{9,10},{10,... | collective-permute-start | bytes 196616 | tf_op jit(solution)/shard_map/ppermute | solution.py:168
  7.1 5.4 %collective-permute-start.1 = (f32[128,128]{1,0:T(8,128)}, f32[128,128]{1,0:T(8,128)S(1)}, u32[]{:S(2)}, u32[]{:S(2)}) collective-permute-start(f32[128,128]{1,0:T(8,128)} %get-tuple-element.61), channel_id=1, source_target_pairs={{0,1},{1,0},{2,3},{3,2},{4,5},{5,4},{6,7},{7,6},{8,9},{9,8},{10,11... | collective-permute-start | bytes 196616 | tf_op jit(solution)/shard_map/ppermute | solution.py:168
  7.3 11.2 %collective-permute-start.6 = (f32[128,128]{1,0:T(8,128)}, f32[128,128]{1,0:T(8,128)S(1)}, u32[]{:S(2)}, u32[]{:S(2)}) collective-permute-start(f32[128,128]{1,0:T(8,128)} %get-tuple-element.70), channel_id=1, source_target_pairs={{0,3},{1,2},{2,1},{3,0},{4,7},{5,6},{6,5},{7,4},{8,11},{9,10},{10,... | collective-permute-start | bytes 196616 | tf_op jit(solution)/shard_map/ppermute | solution.py:168
  8.9 10.0 %collective-permute-start.7 = (f32[128,128]{1,0:T(8,128)}, f32[128,128]{1,0:T(8,128)S(1)}, u32[]{:S(2)}, u32[]{:S(2)}) collective-permute-start(f32[128,128]{1,0:T(8,128)} %get-tuple-element.71), channel_id=1, source_target_pairs={{0,1},{1,0},{2,3},{3,2},{4,5},{5,4},{6,7},{7,6},{8,9},{9,8},{10,11... | collective-permute-start | bytes 196616 | tf_op jit(solution)/shard_map/ppermute | solution.py:168
  13.3 13.4 %collective-permute-start.10 = (f32[512,128]{1,0:T(8,128)S(1)}, f32[512,128]{1,0:T(8,128)S(1)}, u32[]{:S(2)}, u32[]{:S(2)}) collective-permute-start(f32[512,128]{1,0:T(8,128)S(1)} %get-tuple-element.77), channel_id=1, source_target_pairs={{0,4},{4,0},{1,5},{5,1},{2,6},{6,2},{3,7},{7,3},{8,12},{12,8},{9,1... | collective-permute-start | bytes 786440 | tf_op jit(solution)/shard_map/ppermute | solution.py:168
  16.2 9.3 %collective-permute-start.3 = (f32[2,128,128]{2,1,0:T(8,128)S(1)}, f32[2,128,128]{2,1,0:T(8,128)S(1)}, u32[]{:S(2)}, u32[]{:S(2)}) collective-permute-start(f32[2,128,128]{2,1,0:T(8,128)S(1)} %get-tuple-element.66), channel_id=1, source_target_pairs={{0,3},{1,2},{2,1},{3,0},{4,7},{5,6},{6,5},{7,4},{8,11},{9,10},{10,... | collective-permute-start | bytes 393224 | tf_op jit(solution)/shard_map/ppermute | solution.py:168
  16.9 8.0 %collective-permute-start.5 = (f32[2,128,128]{2,1,0:T(8,128)S(1)}, f32[2,128,128]{2,1,0:T(8,128)S(1)}, u32[]{:S(2)}, u32[]{:S(2)}) collective-permute-start(f32[2,128,128]{2,1,0:T(8,128)S(1)} %get-tuple-element.69), channel_id=1, source_target_pairs={{0,2},{1,3},{2,0},{3,1},{4,6},{5,7},{6,4},{7,5},{8,10},{9,11},{10,... | collective-permute-start | bytes 393224 | tf_op jit(solution)/shard_map/ppermute | solution.py:168
  18.6 6.9 %collective-permute-start.4 = (f32[2,128,128]{2,1,0:T(8,128)S(1)}, f32[2,128,128]{2,1,0:T(8,128)S(1)}, u32[]{:S(2)}, u32[]{:S(2)}) collective-permute-start(f32[2,128,128]{2,1,0:T(8,128)S(1)} %get-tuple-element.67), channel_id=1, source_target_pairs={{0,1},{1,0},{2,3},{3,2},{4,5},{5,4},{6,7},{7,6},{8,9},{9,8},{10,11... | collective-permute-start | bytes 393224 | tf_op jit(solution)/shard_map/ppermute | solution.py:168
  19.6 8.5 %collective-permute-start.11 = (f32[512,128]{1,0:T(8,128)S(1)}, f32[512,128]{1,0:T(8,128)S(1)}, u32[]{:S(2)}, u32[]{:S(2)}) collective-permute-start(f32[512,128]{1,0:T(8,128)S(1)} %get-tuple-element.78), channel_id=1, source_target_pairs={{0,4},{4,0},{1,5},{5,1},{2,6},{6,2},{3,7},{7,3},{8,12},{12,8},{9,1... | collective-permute-start | bytes 786440 | tf_op jit(solution)/shard_map/ppermute | solution.py:168
  26.2 14.7 %collective-permute-start.9 = (f32[2,512,128]{2,1,0:T(8,128)S(1)}, f32[2,512,128]{2,1,0:T(8,128)S(1)}, u32[]{:S(2)}, u32[]{:S(2)}) collective-permute-start(f32[2,512,128]{2,1,0:T(8,128)S(1)} %get-tuple-element.76), channel_id=1, source_target_pairs={{0,4},{4,0},{1,5},{5,1},{2,6},{6,2},{3,7},{7,3},{8,12},{12,8},{9,1... | collective-permute-start | bytes 1572872 | tf_op jit(solution)/shard_map/ppermute | solution.py:168
  31.0 5.5 %collective-permute-start.12 = (f32[2,128,128]{2,1,0:T(8,128)S(1)}, f32[2,128,128]{2,1,0:T(8,128)S(1)}, u32[]{:S(2)}, u32[]{:S(2)}) collective-permute-start(f32[2,128,128]{2,1,0:T(8,128)S(1)} %get-tuple-element.79), channel_id=1, source_target_pairs={{0,3},{1,2},{2,1},{3,0},{4,7},{5,6},{6,5},{7,4},{8,11},{9,10},{10,... | collective-permute-start | bytes 393224 | tf_op jit(solution)/shard_map/ppermute | solution.py:531
  31.1 5.5 %collective-permute-start.13 = (f32[2,128,128]{2,1,0:T(8,128)S(1)}, f32[2,128,128]{2,1,0:T(8,128)S(1)}, u32[]{:S(2)}, u32[]{:S(2)}) collective-permute-start(f32[2,128,128]{2,1,0:T(8,128)S(1)} %get-tuple-element.80), channel_id=1, source_target_pairs={{0,1},{1,0},{2,3},{3,2},{4,5},{5,4},{6,7},{7,6},{8,9},{9,8},{10,11... | collective-permute-start | bytes 393224 | tf_op jit(solution)/shard_map/ppermute | solution.py:531
  37.8 5.9 %collective-permute-start.20 = (f32[2,128,128]{2,1,0:T(8,128)S(1)}, f32[2,128,128]{2,1,0:T(8,128)S(1)}, u32[]{:S(2)}, u32[]{:S(2)}) collective-permute-start(f32[2,128,128]{2,1,0:T(8,128)S(1)} %get-tuple-element.83.refs_3_), channel_id=1, source_target_pairs={{0,2},{1,3},{2,0},{3,1},{4,6},{5,7},{6,4},{7,5},{8,10},{9,11},{10,... | collective-permute-start | bytes 393224 | tf_op jit(solution)/shard_map/ppermute | solution.py:531
  39.8 5.9 %collective-permute-start.18 = (f32[2,128,128]{2,1,0:T(8,128)S(1)}, f32[2,128,128]{2,1,0:T(8,128)S(1)}, u32[]{:S(2)}, u32[]{:S(2)}) collective-permute-start(f32[2,128,128]{2,1,0:T(8,128)S(1)} %get-tuple-element.88), channel_id=1, source_target_pairs={{0,3},{1,2},{2,1},{3,0},{4,7},{5,6},{6,5},{7,4},{8,11},{9,10},{10,... | collective-permute-start | bytes 393224 | tf_op jit(solution)/shard_map/ppermute | solution.py:531
  39.8 5.8 %collective-permute-start.19 = (f32[2,128,128]{2,1,0:T(8,128)S(1)}, f32[2,128,128]{2,1,0:T(8,128)S(1)}, u32[]{:S(2)}, u32[]{:S(2)}) collective-permute-start(f32[2,128,128]{2,1,0:T(8,128)S(1)} %get-tuple-element.89), channel_id=1, source_target_pairs={{0,1},{1,0},{2,3},{3,2},{4,5},{5,4},{6,7},{7,6},{8,9},{9,8},{10,11... | collective-permute-start | bytes 393224 | tf_op jit(solution)/shard_map/ppermute | solution.py:531
  41.3 7.5 %collective-permute-start.17 = (f32[2,128,128]{2,1,0:T(8,128)S(1)}, f32[2,128,128]{2,1,0:T(8,128)S(1)}, u32[]{:S(2)}, u32[]{:S(2)}) collective-permute-start(f32[2,128,128]{2,1,0:T(8,128)S(1)} %shard_map.92.refs_4_), channel_id=1, source_target_pairs={{0,2},{1,3},{2,0},{3,1},{4,6},{5,7},{6,4},{7,5},{8,10},{9,11},{10,... | collective-permute-start | bytes 393224 | tf_op jit(solution)/shard_map/ppermute | solution.py:531
  43.2 8.0 %collective-permute-start.15 = (f32[2,128,128]{2,1,0:T(8,128)S(1)}, f32[2,128,128]{2,1,0:T(8,128)S(1)}, u32[]{:S(2)}, u32[]{:S(2)}) collective-permute-start(f32[2,128,128]{2,1,0:T(8,128)S(1)} %get-tuple-element.85), channel_id=1, source_target_pairs={{0,3},{1,2},{2,1},{3,0},{4,7},{5,6},{6,5},{7,4},{8,11},{9,10},{10,... | collective-permute-start | bytes 393224 | tf_op jit(solution)/shard_map/ppermute | solution.py:531
  43.8 7.5 %collective-permute-start.16 = (f32[2,128,128]{2,1,0:T(8,128)S(1)}, f32[2,128,128]{2,1,0:T(8,128)S(1)}, u32[]{:S(2)}, u32[]{:S(2)}) collective-permute-start(f32[2,128,128]{2,1,0:T(8,128)S(1)} %get-tuple-element.86), channel_id=1, source_target_pairs={{0,1},{1,0},{2,3},{3,2},{4,5},{5,4},{6,7},{7,6},{8,9},{9,8},{10,11... | collective-permute-start | bytes 393224 | tf_op jit(solution)/shard_map/ppermute | solution.py:531
  46.3 16.3 %collective-permute-start.25 = (f32[2,512,128]{2,1,0:T(8,128)S(1)}, f32[2,512,128]{2,1,0:T(8,128)S(1)}, u32[]{:S(2)}, u32[]{:S(2)}) collective-permute-start(f32[2,512,128]{2,1,0:T(8,128)S(1)} %get-tuple-element.98), channel_id=1, source_target_pairs={{0,4},{4,0},{1,5},{5,1},{2,6},{6,2},{3,7},{7,3},{8,12},{12,8},{9,1... | collective-permute-start | bytes 1572872 | tf_op jit(solution)/shard_map/ppermute | solution.py:168
  52.6 6.2 %collective-permute-start.23 = (f32[2,128,128]{2,1,0:T(8,128)S(1)}, f32[2,128,128]{2,1,0:T(8,128)S(1)}, u32[]{:S(2)}, u32[]{:S(2)}) collective-permute-start(f32[2,128,128]{2,1,0:T(8,128)S(1)} %get-tuple-element.92.refs_3_), channel_id=1, source_target_pairs={{0,2},{1,3},{2,0},{3,1},{4,6},{5,7},{6,4},{7,5},{8,10},{9,11},{10,... | collective-permute-start | bytes 393224 | tf_op jit(solution)/shard_map/ppermute | solution.py:531
  54.7 5.9 %collective-permute-start.21 = (f32[2,128,128]{2,1,0:T(8,128)S(1)}, f32[2,128,128]{2,1,0:T(8,128)S(1)}, u32[]{:S(2)}, u32[]{:S(2)}) collective-permute-start(f32[2,128,128]{2,1,0:T(8,128)S(1)} %get-tuple-element.93), channel_id=1, source_target_pairs={{0,3},{1,2},{2,1},{3,0},{4,7},{5,6},{6,5},{7,4},{8,11},{9,10},{10,... | collective-permute-start | bytes 393224 | tf_op jit(solution)/shard_map/ppermute | solution.py:531
  55.1 5.5 %collective-permute-start.22 = (f32[2,128,128]{2,1,0:T(8,128)S(1)}, f32[2,128,128]{2,1,0:T(8,128)S(1)}, u32[]{:S(2)}, u32[]{:S(2)}) collective-permute-start(f32[2,128,128]{2,1,0:T(8,128)S(1)} %get-tuple-element.94), channel_id=1, source_target_pairs={{0,1},{1,0},{2,3},{3,2},{4,5},{5,4},{6,7},{7,6},{8,9},{9,8},{10,11... | collective-permute-start | bytes 393224 | tf_op jit(solution)/shard_map/ppermute | solution.py:531
  61.4 9.2 %collective-permute-start.29 = (f32[512,128]{1,0:T(8,128)S(1)}, f32[512,128]{1,0:T(8,128)S(1)}, u32[]{:S(2)}, u32[]{:S(2)}) collective-permute-start(f32[512,128]{1,0:T(8,128)S(1)} %get-tuple-element.103), channel_id=1, source_target_pairs={{0,4},{4,0},{1,5},{5,1},{2,6},{6,2},{3,7},{7,3},{8,12},{12,8},{9,1... | collective-permute-start | bytes 786440 | tf_op jit(solution)/shard_map/ppermute | solution.py:168
  63.0 5.3 %collective-permute-start.28 = (f32[2,128,128]{2,1,0:T(8,128)S(1)}, f32[2,128,128]{2,1,0:T(8,128)S(1)}, u32[]{:S(2)}, u32[]{:S(2)}) collective-permute-start(f32[2,128,128]{2,1,0:T(8,128)S(1)} %shard_map.101.refs_4_), channel_id=1, source_target_pairs={{0,2},{1,3},{2,0},{3,1},{4,6},{5,7},{6,4},{7,5},{8,10},{9,11},{10,... | collective-permute-start | bytes 393224 | tf_op jit(solution)/shard_map/ppermute | solution.py:531
  64.5 11.1 %collective-permute-start.24 = (f32[512,128]{1,0:T(8,128)S(1)}, f32[512,128]{1,0:T(8,128)S(1)}, u32[]{:S(2)}, u32[]{:S(2)}) collective-permute-start(f32[512,128]{1,0:T(8,128)S(1)} %get-tuple-element.97), channel_id=1, source_target_pairs={{0,4},{4,0},{1,5},{5,1},{2,6},{6,2},{3,7},{7,3},{8,12},{12,8},{9,1... | collective-permute-start | bytes 786440 | tf_op jit(solution)/shard_map/ppermute | solution.py:168
  66.7 7.3 %collective-permute-start.26 = (f32[2,128,128]{2,1,0:T(8,128)S(1)}, f32[2,128,128]{2,1,0:T(8,128)S(1)}, u32[]{:S(2)}, u32[]{:S(2)}) collective-permute-start(f32[2,128,128]{2,1,0:T(8,128)S(1)} %get-tuple-element.100), channel_id=1, source_target_pairs={{0,3},{1,2},{2,1},{3,0},{4,7},{5,6},{6,5},{7,4},{8,11},{9,10},{10,... | collective-permute-start | bytes 393224 | tf_op jit(solution)/shard_map/ppermute | solution.py:531
  66.8 7.4 %collective-permute-start.27 = (f32[2,128,128]{2,1,0:T(8,128)S(1)}, f32[2,128,128]{2,1,0:T(8,128)S(1)}, u32[]{:S(2)}, u32[]{:S(2)}) collective-permute-start(f32[2,128,128]{2,1,0:T(8,128)S(1)} %get-tuple-element.101), channel_id=1, source_target_pairs={{0,1},{1,0},{2,3},{3,2},{4,5},{5,4},{6,7},{7,6},{8,9},{9,8},{10,11... | collective-permute-start | bytes 393224 | tf_op jit(solution)/shard_map/ppermute | solution.py:531
  71.0 8.2 %collective-permute-start.33 = (f32[128,128]{1,0:T(8,128)S(1)}, f32[128,128]{1,0:T(8,128)S(1)}, u32[]{:S(2)}, u32[]{:S(2)}) collective-permute-start(f32[128,128]{1,0:T(8,128)S(1)} %shard_map.104.refs_4_), channel_id=1, source_target_pairs={{0,2},{1,3},{2,0},{3,1},{4,6},{5,7},{6,4},{7,5},{8,10},{9,11},{10,... | collective-permute-start | bytes 196616 | tf_op jit(solution)/shard_map/ppermute | solution.py:531
  76.1 6.5 %collective-permute-start.30 = (f32[128,128]{1,0:T(8,128)S(1)}, f32[128,128]{1,0:T(8,128)S(1)}, u32[]{:S(2)}, u32[]{:S(2)}) collective-permute-start(f32[128,128]{1,0:T(8,128)S(1)} %shard_map.107.refs_4_), channel_id=1, source_target_pairs={{0,2},{1,3},{2,0},{3,1},{4,6},{5,7},{6,4},{7,5},{8,10},{9,11},{10,... | collective-permute-start | bytes 196616 | tf_op jit(solution)/shard_map/ppermute | solution.py:531
  83.0 7.1 %collective-permute-start.36 = (f32[256,128]{1,0:T(8,128)S(1)}, f32[256,128]{1,0:T(8,128)S(1)}, u32[]{:S(2)}, u32[]{:S(2)}) collective-permute-start(f32[256,128]{1,0:T(8,128)S(1)} %shard_map.110.refs_11_.refs_0_), channel_id=1, source_target_pairs={{0,8},{8,0},{16,24},{24,16},{1,9},{9,1},{17,25},{25,17},{2,10},{10... | collective-permute-start | bytes 393224 | tf_op jit(solution)/shard_map/ppermute | solution.py:590
  90.1 8.4 %collective-permute-start.40 = (f32[264,128]{1,0:T(8,128)S(1)}, f32[264,128]{1,0:T(8,128)S(1)}, u32[]{:S(2)}, u32[]{:S(2)}) collective-permute-start(f32[264,128]{1,0:T(8,128)S(1)} %shard_map.113.refs_0_.refs_2_), channel_id=1, source_target_pairs={{0,16},{8,24},{16,0},{24,8},{1,17},{9,25},{17,1},{25,9},{2,18},{10... | collective-permute-start | bytes 405512 | tf_op jit(solution)/shard_map/ppermute | solution.py:590
  (19 other events, 76.0 us)

commit v5 on v4

--- a/solution.py
+++ b/solution.py
@@ -311,21 +311,6 @@
             out[at] = both * spectra + cross * swapped
 
 
-def back_pair_body(bits, layers, *refs):
-    count = layers * CHUNKS
-    parts, (high_ref, low_ref), outs = refs[:count], refs[count : count + 2], refs[count + 2 :]
-    me = lax.axis_index("lat")
-    mixed = []
-    for c in range(CHUNKS):
-        chunk = parts[c * layers : (c + 1) * layers]
-        mixed.append(sum((part[...] for part in chunk[1:]), chunk[0][...]))
-    half = mixed[0].shape[1] // 2
-    pieces = [part[:, z * half : (z + 1) * half] for z in range(2) for part in mixed]
-    high, low = halves(jnp.concatenate(pieces, axis=1))
-    for d, out in zip(bits, outs):
-        out[0], out[1] = along_x(high_ref, low_ref, me ^ d, high, low, +1)
-
-
 def back_body(bits, layers, *refs):
     parts, (high_ref, low_ref), outs = refs[:layers], refs[layers : layers + 2], refs[layers + 2 :]
     me = lax.axis_index("lat")
@@ -383,10 +368,10 @@
         field[1, :, at] = source[1, 0, rows, at] + (m_real * imag + m_imag * real)
 
 
-def again_body(lat, bits, *refs):
+def again_body(lat, bits, chunk, *refs):
     parts, (begun, source, contrast, high_ref, low_ref), rest = refs[: len(bits)], refs[len(bits) : len(bits) + 5], refs[len(bits) + 5 :]
     out, ahead, field = rest
-    update(parts, bits, begun, source, contrast, high_ref, low_ref, field)
+    update(parts, bits, begun, source, contrast, high_ref, low_ref, field, chunk=chunk)
     ahead[0], ahead[1] = weighted(contrast, field[0], field[1])
     forward_blocks(ahead[0], ahead[1], high_ref, low_ref, [out], turns(lat)[1:2])
 
@@ -535,10 +520,9 @@
 
     def back(parts, chunk=False):
         specs = [whole(part.shape) for part in parts] + row_specs
-        whole_body = back_pair_body if len(parts) > layers else back_body
 
         def some(chosen):
-            body = functools.partial(back_chunk_body if chunk else whole_body, chosen, layers)
+            body = functools.partial(back_chunk_body if chunk else back_body, chosen, layers)
             outs = [f32(rows, parts[0].shape[1]) if chunk else block] * len(chosen)
             return kernel(body, outs, (*parts, *row), specs, stage_flops * len(chosen) // lat)
 
@@ -551,10 +535,10 @@
         specs = [whole(block.shape)] * (lat - near) + [whole(begun.shape), pick(source.shape, p), whole(contrast.shape)]
         return (*parts[near:], begun, source, contrast), specs
 
-    def again(p, parts):
-        args, specs = fields(p, parts)
+    def again(operands, chosen, chunk=None):
+        args, specs = operands
         outs = [block, f32(2, rows, length)]
-        body = functools.partial(again_body, lat, bits[near:])
+        body = functools.partial(again_body, lat, chosen, chunk)
         got = kernel(body, outs, (*args, *col), specs + table_specs, stage_flops, [full])
         ahead = turn_block(got[0], early[0])
         body = functools.partial(rest_body, later)
@@ -603,18 +587,23 @@
     col, row = tuple(tables[:2]), tuple(tables[2:])
     turned = kernel(turn_body, [f32(2, layers, length, rows)], (green,), [whole(green.shape)], 1 << 20)[0]
     chunks = chains[0]
-    chains[0] = couple_chunk(chunks[0], 0)
+    summed = [couple_chunk(chunks[0], 0)]
     chains += [start(p) for p in range(1, pols)]
     for c in range(1, CHUNKS):
-        chains[0] = chains[0] + couple_chunk(chunks[c], c)
+        summed.append(couple_chunk(chunks[c], c))
+    ahead = [back(chunk, True) for chunk in summed[:-1]]
     chains[1:] = [couple(chain) for chain in chains[1:]]
     for step in range(ITERS - 1):
         moved = [None] * pols
         for p in range(pols):
+            if p == 0 and step == 0:
+                ahead.append(back(summed[-1], True))
+                moved[p] = again(chunk_fields(p, ahead), bits, CHUNKS - 1)
+                continue
             moved[p] = back(chains[p])
             if p > 0:
                 chains[p - 1] = couple(moved[p - 1])
-            moved[p] = again(p, moved[p])
+            moved[p] = again(fields(p, moved[p]), bits[near:])
         chains[last] = couple(moved[last], CHUNKS if step == ITERS - 2 else 1)
     cells = None
     for p in range(last - 1):

time: 105 us -> 106 us (level)
  starting transfers between devices: 35.8 us -> 38.3 us
  waiting for transfers between devices: 38.6 us -> 36.8 us
  Pallas kernels: 27.7 us -> 29 us
    ppermute x21 -> x24, waiting for transfers between devices: 16.7 us -> 14.5 us  [turn_block(): return lax.ppermute(value, 'lat', [(i, i ^ d) for i in range(lat)])]
    ppermute x21 -> x24, starting transfers between devices: 15.5 us -> 17.4 us  [turn_block(): return lax.ppermute(value, 'lat', [(i, i ^ d) for i in range(lat)])]
    pallas_call x39 -> x41, Pallas kernels: 27.7 us -> 29 us  [call(): pl.pallas_call(ordered, grid=(1,), out_shape=outs, in_specs=list(specs) +...]
  transfers between devices with their start and end apart: 42 -> 45, of which waited for: 17 -> 20; matrix products, arithmetic and copies ran while one was open for 0% -> 0% of each run, Pallas kernels for 22% -> 22%
where the time goes in v5:
time: 106 us
  starting transfers between devices  38.3 us (36%)
  waiting for transfers between devices  36.8 us (35%)
  Pallas kernels  29 us (27%)
  between operations  1.12 us (1%)
    pallas_call x41, Pallas kernels, call(): pl.pallas_call(ordered, grid=(1,), out_shape=outs, in_specs=list(specs) +...  29 us
    ppermute x24, starting transfers between devices, turn_block(): return lax.ppermute(value, 'lat', [(i, i ^ d) for i in range(lat)])  17.4 us
    ppermute x18, starting transfers between devices, send(): got.append(lax.ppermute(block, axis, [(i, i ^ d) for i in range(size)]))  16.3 us
    ppermute x24, waiting for transfers between devices, turn_block(): return lax.ppermute(value, 'lat', [(i, i ^ d) for i in range(lat)])  14.5 us
    ppermute x18, waiting for transfers between devices, send(): got.append(lax.ppermute(block, axis, [(i, i ^ d) for i in range(size)]))  11.7 us
    ppermute x3, waiting for transfers between devices, across(): return lax.ppermute(value, 'freq', [(i, i ^ d) for i in range(freqs)])  10.7 us
    ppermute x3, starting transfers between devices, across(): return lax.ppermute(value, 'freq', [(i, i ^ d) for i in range(freqs)])  4.58 us
  transfers between devices with their start and end apart: 45, of which 20 were waited for; matrix products, arithmetic and copies ran while one was open for 0% of the time, Pallas kernels for 22%

profile of v5, /device:TPU:0, one launch (start us, length us, event | category | flops | bytes accessed | tf_op | source)
XLA Modules:
  0.0 106.2 jit_solution(7956673347831618602)
XLA Ops:
  0.7 3.4 %shard_map.77 = (f32[128,128]{1,0:T(8,128)}, f32[128,128]{1,0:T(8,128)}, f32[128,128]{1,0:T(8,128)}, f32[128,128]{1,0:T(8,128)}, f32[128,128]{1,0:T(8,128)}, /*i...) custom-call(f32[2,2,128,512]{3,2,1,0:T(8,128)} %bitcast.6, f32[2,128,512]{2,1,0:T(8,128)} %bitcast.13, ...), custom_call_target="tpu_custom_call" | custom-call | flops 805306368 | bytes 1048576 | tf_op jit(solution)/shard_map/pallas_call | solution.py:137
  4.1 3.0 %collective-permute-start.2 = (f32[128,128]{1,0:T(8,128)}, f32[128,128]{1,0:T(8,128)S(1)}, u32[]{:S(2)}, u32[]{:S(2)}) collective-permute-start(f32[128,128]{1,0:T(8,128)} %get-tuple-element.65), channel_id=1, source_target_pairs={{0,2},{1,3},{2,0},{3,1},{4,6},{5,7},{6,4},{7,5},{8,10},{9,11},{10,... | collective-permute-start | bytes 196616 | tf_op jit(solution)/shard_map/ppermute | solution.py:168
  10.3 1.2 %collective-permute-done.refs_0_ = f32[128,128]{1,0:T(8,128)S(1)} collective-permute-done((f32[128,128]{1,0:T(8,128)}, f32[128,128]{1,0:T(8,128)S(1)}, u32[]{:S(2)}, u32[]{:S(2)}) %collective-permute-start) | collective-permute-done | bytes 65568 | tf_op jit(solution)/shard_map/ppermute | solution.py:168
  12.2 1.6 %collective-permute-start.6 = (f32[512,128]{1,0:T(8,128)S(1)}, f32[512,128]{1,0:T(8,128)S(1)}, u32[]{:S(2)}, u32[]{:S(2)}) collective-permute-start(f32[512,128]{1,0:T(8,128)S(1)} %get-tuple-element.73), channel_id=1, source_target_pairs={{0,4},{4,0},{1,5},{5,1},{2,6},{6,2},{3,7},{7,3},{8,12},{12,8},{9,1... | collective-permute-start | bytes 786440 | tf_op jit(solution)/shard_map/ppermute | solution.py:168
  17.9 1.8 %collective-permute-done.9.refs_1_ = f32[128,128]{1,0:T(8,128)S(1)} collective-permute-done((f32[128,128]{1,0:T(8,128)S(1)}, f32[128,128]{1,0:T(8,128)S(1)}, u32[]{:S(2)}, u32[]{:S(2)}) %collective-permute-start.9) | collective-permute-done | bytes 65568 | tf_op jit(solution)/shard_map/ppermute | solution.py:168
  20.3 1.2 %collective-permute-start.5 = (f32[2,128,128]{2,1,0:T(8,128)S(1)}, f32[2,128,128]{2,1,0:T(8,128)S(1)}, u32[]{:S(2)}, u32[]{:S(2)}) collective-permute-start(f32[2,128,128]{2,1,0:T(8,128)S(1)} %get-tuple-element.72), channel_id=1, source_target_pairs={{0,2},{1,3},{2,0},{3,1},{4,6},{5,7},{6,4},{7,5},{8,10},{9,11},{10,... | collective-permute-start | bytes 393224 | tf_op jit(solution)/shard_map/ppermute | solution.py:168
  23.9 2.3 %collective-permute-done.5.refs_1_ = f32[2,128,128]{2,1,0:T(8,128)S(1)} collective-permute-done((f32[2,128,128]{2,1,0:T(8,128)S(1)}, f32[2,128,128]{2,1,0:T(8,128)S(1)}, u32[]{:S(2)}, u32[]{:S(2)}) %collective-permute-start.5) | collective-permute-done | bytes 131104 | tf_op jit(solution)/shard_map/ppermute | solution.py:168
  27.8 1.3 %collective-permute-start.15 = (f32[128,128]{1,0:T(8,128)S(1)}, f32[128,128]{1,0:T(8,128)S(1)}, u32[]{:S(2)}, u32[]{:S(2)}) collective-permute-start(f32[128,128]{1,0:T(8,128)S(1)} %shard_map.85.refs_4_), channel_id=1, source_target_pairs={{0,2},{1,3},{2,0},{3,1},{4,6},{5,7},{6,4},{7,5},{8,10},{9,11},{10,... | collective-permute-start | bytes 196616 | tf_op jit(solution)/shard_map/ppermute | solution.py:516
  30.0 1.4 %collective-permute-done.11.refs_1_ = f32[512,128]{1,0:T(8,128)S(1)} collective-permute-done((f32[512,128]{1,0:T(8,128)S(1)}, f32[512,128]{1,0:T(8,128)S(1)}, u32[]{:S(2)}, u32[]{:S(2)}) %collective-permute-start.11) | collective-permute-done | bytes 262176 | tf_op jit(solution)/shard_map/ppermute | solution.py:168
  33.5 1.3 %collective-permute-start.13 = (f32[128,128]{1,0:T(8,128)S(1)}, f32[128,128]{1,0:T(8,128)S(1)}, u32[]{:S(2)}, u32[]{:S(2)}) collective-permute-start(f32[128,128]{1,0:T(8,128)S(1)} %get-tuple-element.84), channel_id=1, source_target_pairs={{0,3},{1,2},{2,1},{3,0},{4,7},{5,6},{6,5},{7,4},{8,11},{9,10},{10,... | collective-permute-start | bytes 196616 | tf_op jit(solution)/shard_map/ppermute | solution.py:516
  35.7 2.0 %collective-permute-done.13.refs_2_ = f32[128,128]{1,0:T(8,128)S(1)} collective-permute-done((f32[128,128]{1,0:T(8,128)S(1)}, f32[128,128]{1,0:T(8,128)S(1)}, u32[]{:S(2)}, u32[]{:S(2)}) %collective-permute-start.13) | collective-permute-done | bytes 65568 | tf_op jit(solution)/shard_map/ppermute | solution.py:516
  37.7 1.3 %shard_map.92 = (f32[2,128,128]{2,1,0:T(8,128)S(1)}, f32[2,128,512]{2,1,0:T(8,128)S(1)}) custom-call(f32[128,128]{1,0:T(8,128)S(1)} %get-tuple-element.83.refs_6_.refs_0_, f32[128,128]{1,0:T(8,128)S(1)} %collective-permute-done.12.refs_1_, f32[128,128]{1,0:T(8,128)S(1)} %collective-permute-done.13.refs_2_, f32[128,128]{1,0:T(8,128)S(1)} %collective-permute-done.14.refs_3_, ...), custom_call_target="tpu_custom_call" | custom-call | flops 805306368 | bytes 1310720 | tf_op jit(solution)/shard_map/pallas_call | solution.py:137
  39.0 1.2 %collective-permute-start.23 = (f32[2,128,128]{2,1,0:T(8,128)S(1)}, f32[2,128,128]{2,1,0:T(8,128)S(1)}, u32[]{:S(2)}, u32[]{:S(2)}) collective-permute-start(f32[2,128,128]{2,1,0:T(8,128)S(1)} %get-tuple-element.89.refs_3_), channel_id=1, source_target_pairs={{0,2},{1,3},{2,0},{3,1},{4,6},{5,7},{6,4},{7,5},{8,10},{9,11},{10,... | collective-permute-start | bytes 393224 | tf_op jit(solution)/shard_map/ppermute | solution.py:516
  42.6 1.2 %collective-permute-start.20 = (f32[2,128,128]{2,1,0:T(8,128)S(1)}, f32[2,128,128]{2,1,0:T(8,128)S(1)}, u32[]{:S(2)}, u32[]{:S(2)}) collective-permute-start(f32[2,128,128]{2,1,0:T(8,128)S(1)} %shard_map.94.refs_4_), channel_id=1, source_target_pairs={{0,2},{1,3},{2,0},{3,1},{4,6},{5,7},{6,4},{7,5},{8,10},{9,11},{10,... | collective-permute-start | bytes 393224 | tf_op jit(solution)/shard_map/ppermute | solution.py:516
  47.9 1.9 %collective-permute-start.28 = (f32[2,512,128]{2,1,0:T(8,128)S(1)}, f32[2,512,128]{2,1,0:T(8,128)S(1)}, u32[]{:S(2)}, u32[]{:S(2)}) collective-permute-start(f32[2,512,128]{2,1,0:T(8,128)S(1)} %get-tuple-element.104), channel_id=1, source_target_pairs={{0,4},{4,0},{1,5},{5,1},{2,6},{6,2},{3,7},{7,3},{8,12},{12,8},{9,1... | collective-permute-start | bytes 1572872 | tf_op jit(solution)/shard_map/ppermute | solution.py:168
  49.8 1.2 %collective-permute-done.20.refs_1_ = f32[2,128,128]{2,1,0:T(8,128)S(1)} collective-permute-done((f32[2,128,128]{2,1,0:T(8,128)S(1)}, f32[2,128,128]{2,1,0:T(8,128)S(1)}, u32[]{:S(2)}, u32[]{:S(2)}) %collective-permute-start.20) | collective-permute-done | bytes 131104 | tf_op jit(solution)/shard_map/ppermute | solution.py:516
  51.5 1.3 %collective-permute-done.18.refs_0_ = f32[2,128,128]{2,1,0:T(8,128)S(1)} collective-permute-done((f32[2,128,128]{2,1,0:T(8,128)S(1)}, f32[2,128,128]{2,1,0:T(8,128)S(1)}, u32[]{:S(2)}, u32[]{:S(2)}) %collective-permute-start.18) | collective-permute-done | bytes 131104 | tf_op jit(solution)/shard_map/ppermute | solution.py:516
  52.8 1.3 %shard_map.99 = (f32[2,128,128]{2,1,0:T(8,128)S(1)}, f32[2,128,512]{2,1,0:T(8,128)S(1)}) custom-call(f32[2,128,128]{2,1,0:T(8,128)S(1)} %collective-permute-done.18.refs_0_, f32[2,128,128]{2,1,0:T(8,128)S(1)} %collective-permute-done.19.refs_1_, f32[2,128,512]{2,1,0:T(8,128)S(1)} %shard_map.98.refs_2_.refs_7_, f32[2,2,128,512]{3,2,1,0:T(8,128)S(1)} %bitcast.9, ...), custom_call_target="tpu_custom_call" | custom-call | flops 805306368 | bytes 1310720 | tf_op jit(solution)/shard_map/pallas_call | solution.py:137
  54.1 1.5 %collective-permute-start.26 = (f32[2,128,128]{2,1,0:T(8,128)S(1)}, f32[2,128,128]{2,1,0:T(8,128)S(1)}, u32[]{:S(2)}, u32[]{:S(2)}) collective-permute-start(f32[2,128,128]{2,1,0:T(8,128)S(1)} %get-tuple-element.98.refs_3_), channel_id=1, source_target_pairs={{0,2},{1,3},{2,0},{3,1},{4,6},{5,7},{6,4},{7,5},{8,10},{9,11},{10,... | collective-permute-start | bytes 393224 | tf_op jit(solution)/shard_map/ppermute | solution.py:516
  57.2 3.3 %collective-permute-done.26.refs_1_ = f32[2,128,128]{2,1,0:T(8,128)S(1)} collective-permute-done((f32[2,128,128]{2,1,0:T(8,128)S(1)}, f32[2,128,128]{2,1,0:T(8,128)S(1)}, u32[]{:S(2)}, u32[]{:S(2)}) %collective-permute-start.26) | collective-permute-done | bytes 131104 | tf_op jit(solution)/shard_map/ppermute | solution.py:516
  61.0 1.6 %collective-permute-done.24.refs_0_ = f32[2,128,128]{2,1,0:T(8,128)S(1)} collective-permute-done((f32[2,128,128]{2,1,0:T(8,128)S(1)}, f32[2,128,128]{2,1,0:T(8,128)S(1)}, u32[]{:S(2)}, u32[]{:S(2)}) %collective-permute-start.24) | collective-permute-done | bytes 131104 | tf_op jit(solution)/shard_map/ppermute | solution.py:516
  63.5 1.4 %collective-permute-start.32 = (f32[512,128]{1,0:T(8,128)S(1)}, f32[512,128]{1,0:T(8,128)S(1)}, u32[]{:S(2)}, u32[]{:S(2)}) collective-permute-start(f32[512,128]{1,0:T(8,128)S(1)} %get-tuple-element.109), channel_id=1, source_target_pairs={{0,4},{4,0},{1,5},{5,1},{2,6},{6,2},{3,7},{7,3},{8,12},{12,8},{9,1... | collective-permute-start | bytes 786440 | tf_op jit(solution)/shard_map/ppermute | solution.py:168
  69.1 1.7 %collective-permute-done.31.refs_1_ = f32[2,128,128]{2,1,0:T(8,128)S(1)} collective-permute-done((f32[2,128,128]{2,1,0:T(8,128)S(1)}, f32[2,128,128]{2,1,0:T(8,128)S(1)}, u32[]{:S(2)}, u32[]{:S(2)}) %collective-permute-start.31) | collective-permute-done | bytes 131104 | tf_op jit(solution)/shard_map/ppermute | solution.py:516
  71.3 1.4 %collective-permute-done.32.refs_1_ = f32[512,128]{1,0:T(8,128)S(1)} collective-permute-done((f32[512,128]{1,0:T(8,128)S(1)}, f32[512,128]{1,0:T(8,128)S(1)}, u32[]{:S(2)}, u32[]{:S(2)}) %collective-permute-start.32) | collective-permute-done | bytes 262176 | tf_op jit(solution)/shard_map/ppermute | solution.py:168
  73.2 1.1 %collective-permute-start.36 = (f32[128,128]{1,0:T(8,128)S(1)}, f32[128,128]{1,0:T(8,128)S(1)}, u32[]{:S(2)}, u32[]{:S(2)}) collective-permute-start(f32[128,128]{1,0:T(8,128)S(1)} %shard_map.106.refs_4_), channel_id=1, source_target_pairs={{0,2},{1,3},{2,0},{3,1},{4,6},{5,7},{6,4},{7,5},{8,10},{9,11},{10,... | collective-permute-start | bytes 196616 | tf_op jit(solution)/shard_map/ppermute | solution.py:516
  77.9 1.4 %collective-permute-start.33 = (f32[128,128]{1,0:T(8,128)S(1)}, f32[128,128]{1,0:T(8,128)S(1)}, u32[]{:S(2)}, u32[]{:S(2)}) collective-permute-start(f32[128,128]{1,0:T(8,128)S(1)} %shard_map.109.refs_4_), channel_id=1, source_target_pairs={{0,2},{1,3},{2,0},{3,1},{4,6},{5,7},{6,4},{7,5},{8,10},{9,11},{10,... | collective-permute-start | bytes 196616 | tf_op jit(solution)/shard_map/ppermute | solution.py:516
  81.7 2.2 %collective-permute-done.34.refs_2_ = f32[128,128]{1,0:T(8,128)S(1)} collective-permute-done((f32[128,128]{1,0:T(8,128)S(1)}, f32[128,128]{1,0:T(8,128)S(1)}, u32[]{:S(2)}, u32[]{:S(2)}) %collective-permute-start.34) | collective-permute-done | bytes 65568 | tf_op jit(solution)/shard_map/ppermute | solution.py:516
  84.5 1.9 %collective-permute-start.39 = (f32[256,128]{1,0:T(8,128)S(1)}, f32[256,128]{1,0:T(8,128)S(1)}, u32[]{:S(2)}, u32[]{:S(2)}) collective-permute-start(f32[256,128]{1,0:T(8,128)S(1)} %shard_map.112.refs_11_.refs_0_), channel_id=1, source_target_pairs={{0,8},{8,0},{16,24},{24,16},{1,9},{9,1},{17,25},{25,17},{2,10},{10... | collective-permute-start | bytes 393224 | tf_op jit(solution)/shard_map/ppermute | solution.py:574
  90.4 1.6 %collective-permute-done.40.refs_3_ = f32[8,128]{1,0:T(8,128)S(1)} collective-permute-done((f32[8,128]{1,0:T(8,128)S(1)}, f32[8,128]{1,0:T(8,128)S(1)}, u32[]{:S(2)}, u32[]{:S(2)}) %collective-permute-start.40) | collective-permute-done | bytes 4128 | tf_op jit(solution)/shard_map/ppermute | solution.py:168
  92.0 2.6 %collective-permute-start.43 = (f32[264,128]{1,0:T(8,128)S(1)}, f32[264,128]{1,0:T(8,128)S(1)}, u32[]{:S(2)}, u32[]{:S(2)}) collective-permute-start(f32[264,128]{1,0:T(8,128)S(1)} %shard_map.115.refs_0_.refs_2_), channel_id=1, source_target_pairs={{0,16},{8,24},{16,0},{24,8},{1,17},{9,25},{17,1},{25,9},{2,18},{10... | collective-permute-start | bytes 405512 | tf_op jit(solution)/shard_map/ppermute | solution.py:574
  94.7 5.6 %collective-permute-done.43.refs_1_ = f32[264,128]{1,0:T(8,128)S(1)} collective-permute-done((f32[264,128]{1,0:T(8,128)S(1)}, f32[264,128]{1,0:T(8,128)S(1)}, u32[]{:S(2)}, u32[]{:S(2)}) %collective-permute-start.43) | collective-permute-done | bytes 135200 | tf_op jit(solution)/shard_map/ppermute | solution.py:574
  100.4 5.0 %collective-permute-done.44.refs_1_ = f32[264,128]{1,0:T(8,128)S(1)} collective-permute-done((f32[264,128]{1,0:T(8,128)S(1)}, f32[264,128]{1,0:T(8,128)S(1)}, u32[]{:S(2)}, u32[]{:S(2)}) %collective-permute-start.44) | collective-permute-done | bytes 135200 | tf_op jit(solution)/shard_map/ppermute | solution.py:574
  (121 shorter events, 42.9 us)
Async XLA Ops:
  4.1 5.5 %collective-permute-start.2 = (f32[128,128]{1,0:T(8,128)}, f32[128,128]{1,0:T(8,128)S(1)}, u32[]{:S(2)}, u32[]{:S(2)}) collective-permute-start(f32[128,128]{1,0:T(8,128)} %get-tuple-element.65), channel_id=1, source_target_pairs={{0,2},{1,3},{2,0},{3,1},{4,6},{5,7},{6,4},{7,5},{8,10},{9,11},{10,... | collective-permute-start | bytes 196616 | tf_op jit(solution)/shard_map/ppermute | solution.py:168
  12.2 10.4 %collective-permute-start.6 = (f32[512,128]{1,0:T(8,128)S(1)}, f32[512,128]{1,0:T(8,128)S(1)}, u32[]{:S(2)}, u32[]{:S(2)}) collective-permute-start(f32[512,128]{1,0:T(8,128)S(1)} %get-tuple-element.73), channel_id=1, source_target_pairs={{0,4},{4,0},{1,5},{5,1},{2,6},{6,2},{3,7},{7,3},{8,12},{12,8},{9,1... | collective-permute-start | bytes 786440 | tf_op jit(solution)/shard_map/ppermute | solution.py:168
  13.8 6.5 %collective-permute-start.7 = (f32[128,128]{1,0:T(8,128)S(1)}, f32[128,128]{1,0:T(8,128)S(1)}, u32[]{:S(2)}, u32[]{:S(2)}) collective-permute-start(f32[128,128]{1,0:T(8,128)S(1)} %copy-done.9), channel_id=1, source_target_pairs={{0,3},{1,2},{2,1},{3,0},{4,7},{5,6},{6,5},{7,4},{8,11},{9,10},{10,... | collective-permute-start | bytes 196616 | tf_op jit(solution)/shard_map/ppermute | solution.py:168
  14.4 7.1 %collective-permute-start.8 = (f32[128,128]{1,0:T(8,128)S(1)}, f32[128,128]{1,0:T(8,128)S(1)}, u32[]{:S(2)}, u32[]{:S(2)}) collective-permute-start(f32[128,128]{1,0:T(8,128)S(1)} %copy-done.8), channel_id=1, source_target_pairs={{0,1},{1,0},{2,3},{3,2},{4,5},{5,4},{6,7},{7,6},{8,9},{9,8},{10,11... | collective-permute-start | bytes 196616 | tf_op jit(solution)/shard_map/ppermute | solution.py:168
  17.0 9.9 %collective-permute-start.3 = (f32[2,128,128]{2,1,0:T(8,128)S(1)}, f32[2,128,128]{2,1,0:T(8,128)S(1)}, u32[]{:S(2)}, u32[]{:S(2)}) collective-permute-start(f32[2,128,128]{2,1,0:T(8,128)S(1)} %get-tuple-element.69), channel_id=1, source_target_pairs={{0,3},{1,2},{2,1},{3,0},{4,7},{5,6},{6,5},{7,4},{8,11},{9,10},{10,... | collective-permute-start | bytes 393224 | tf_op jit(solution)/shard_map/ppermute | solution.py:168
  19.6 7.2 %collective-permute-start.4 = (f32[2,128,128]{2,1,0:T(8,128)S(1)}, f32[2,128,128]{2,1,0:T(8,128)S(1)}, u32[]{:S(2)}, u32[]{:S(2)}) collective-permute-start(f32[2,128,128]{2,1,0:T(8,128)S(1)} %get-tuple-element.70), channel_id=1, source_target_pairs={{0,1},{1,0},{2,3},{3,2},{4,5},{5,4},{6,7},{7,6},{8,9},{9,8},{10,11... | collective-permute-start | bytes 393224 | tf_op jit(solution)/shard_map/ppermute | solution.py:168
  20.3 6.0 %collective-permute-start.5 = (f32[2,128,128]{2,1,0:T(8,128)S(1)}, f32[2,128,128]{2,1,0:T(8,128)S(1)}, u32[]{:S(2)}, u32[]{:S(2)}) collective-permute-start(f32[2,128,128]{2,1,0:T(8,128)S(1)} %get-tuple-element.72), channel_id=1, source_target_pairs={{0,2},{1,3},{2,0},{3,1},{4,6},{5,7},{6,4},{7,5},{8,10},{9,11},{10,... | collective-permute-start | bytes 393224 | tf_op jit(solution)/shard_map/ppermute | solution.py:168
  22.2 9.2 %collective-permute-start.11 = (f32[512,128]{1,0:T(8,128)S(1)}, f32[512,128]{1,0:T(8,128)S(1)}, u32[]{:S(2)}, u32[]{:S(2)}) collective-permute-start(f32[512,128]{1,0:T(8,128)S(1)} %get-tuple-element.82), channel_id=1, source_target_pairs={{0,4},{4,0},{1,5},{5,1},{2,6},{6,2},{3,7},{7,3},{8,12},{12,8},{9,1... | collective-permute-start | bytes 786440 | tf_op jit(solution)/shard_map/ppermute | solution.py:168
  27.5 14.7 %collective-permute-start.10 = (f32[2,512,128]{2,1,0:T(8,128)S(1)}, f32[2,512,128]{2,1,0:T(8,128)S(1)}, u32[]{:S(2)}, u32[]{:S(2)}) collective-permute-start(f32[2,512,128]{2,1,0:T(8,128)S(1)} %get-tuple-element.81), channel_id=1, source_target_pairs={{0,4},{4,0},{1,5},{5,1},{2,6},{6,2},{3,7},{7,3},{8,12},{12,8},{9,1... | collective-permute-start | bytes 1572872 | tf_op jit(solution)/shard_map/ppermute | solution.py:168
  27.8 7.2 %collective-permute-start.15 = (f32[128,128]{1,0:T(8,128)S(1)}, f32[128,128]{1,0:T(8,128)S(1)}, u32[]{:S(2)}, u32[]{:S(2)}) collective-permute-start(f32[128,128]{1,0:T(8,128)S(1)} %shard_map.85.refs_4_), channel_id=1, source_target_pairs={{0,2},{1,3},{2,0},{3,1},{4,6},{5,7},{6,4},{7,5},{8,10},{9,11},{10,... | collective-permute-start | bytes 196616 | tf_op jit(solution)/shard_map/ppermute | solution.py:516
  29.1 5.7 %collective-permute-start.17 = (f32[128,128]{1,0:T(8,128)S(1)}, f32[128,128]{1,0:T(8,128)S(1)}, u32[]{:S(2)}, u32[]{:S(2)}) collective-permute-start(f32[128,128]{1,0:T(8,128)S(1)} %get-tuple-element.87), channel_id=1, source_target_pairs={{0,1},{1,0},{2,3},{3,2},{4,5},{5,4},{6,7},{7,6},{8,9},{9,8},{10,11... | collective-permute-start | bytes 196616 | tf_op jit(solution)/shard_map/ppermute | solution.py:516
  31.9 5.8 %collective-permute-start.12 = (f32[128,128]{1,0:T(8,128)S(1)}, f32[128,128]{1,0:T(8,128)S(1)}, u32[]{:S(2)}, u32[]{:S(2)}) collective-permute-start(f32[128,128]{1,0:T(8,128)S(1)} %shard_map.89.refs_4_), channel_id=1, source_target_pairs={{0,2},{1,3},{2,0},{3,1},{4,6},{5,7},{6,4},{7,5},{8,10},{9,11},{10,... | collective-permute-start | bytes 196616 | tf_op jit(solution)/shard_map/ppermute | solution.py:516
  39.0 6.4 %collective-permute-start.23 = (f32[2,128,128]{2,1,0:T(8,128)S(1)}, f32[2,128,128]{2,1,0:T(8,128)S(1)}, u32[]{:S(2)}, u32[]{:S(2)}) collective-permute-start(f32[2,128,128]{2,1,0:T(8,128)S(1)} %get-tuple-element.89.refs_3_), channel_id=1, source_target_pairs={{0,2},{1,3},{2,0},{3,1},{4,6},{5,7},{6,4},{7,5},{8,10},{9,11},{10,... | collective-permute-start | bytes 393224 | tf_op jit(solution)/shard_map/ppermute | solution.py:516
  41.1 6.1 %collective-permute-start.21 = (f32[2,128,128]{2,1,0:T(8,128)S(1)}, f32[2,128,128]{2,1,0:T(8,128)S(1)}, u32[]{:S(2)}, u32[]{:S(2)}) collective-permute-start(f32[2,128,128]{2,1,0:T(8,128)S(1)} %get-tuple-element.94), channel_id=1, source_target_pairs={{0,3},{1,2},{2,1},{3,0},{4,7},{5,6},{6,5},{7,4},{8,11},{9,10},{10,... | collective-permute-start | bytes 393224 | tf_op jit(solution)/shard_map/ppermute | solution.py:516
  41.9 5.3 %collective-permute-start.22 = (f32[2,128,128]{2,1,0:T(8,128)S(1)}, f32[2,128,128]{2,1,0:T(8,128)S(1)}, u32[]{:S(2)}, u32[]{:S(2)}) collective-permute-start(f32[2,128,128]{2,1,0:T(8,128)S(1)} %get-tuple-element.95), channel_id=1, source_target_pairs={{0,1},{1,0},{2,3},{3,2},{4,5},{5,4},{6,7},{7,6},{8,9},{9,8},{10,11... | collective-permute-start | bytes 393224 | tf_op jit(solution)/shard_map/ppermute | solution.py:516
  42.6 8.3 %collective-permute-start.20 = (f32[2,128,128]{2,1,0:T(8,128)S(1)}, f32[2,128,128]{2,1,0:T(8,128)S(1)}, u32[]{:S(2)}, u32[]{:S(2)}) collective-permute-start(f32[2,128,128]{2,1,0:T(8,128)S(1)} %shard_map.94.refs_4_), channel_id=1, source_target_pairs={{0,2},{1,3},{2,0},{3,1},{4,6},{5,7},{6,4},{7,5},{8,10},{9,11},{10,... | collective-permute-start | bytes 393224 | tf_op jit(solution)/shard_map/ppermute | solution.py:516
  44.6 8.2 %collective-permute-start.18 = (f32[2,128,128]{2,1,0:T(8,128)S(1)}, f32[2,128,128]{2,1,0:T(8,128)S(1)}, u32[]{:S(2)}, u32[]{:S(2)}) collective-permute-start(f32[2,128,128]{2,1,0:T(8,128)S(1)} %get-tuple-element.91), channel_id=1, source_target_pairs={{0,3},{1,2},{2,1},{3,0},{4,7},{5,6},{6,5},{7,4},{8,11},{9,10},{10,... | collective-permute-start | bytes 393224 | tf_op jit(solution)/shard_map/ppermute | solution.py:516
  45.3 7.5 %collective-permute-start.19 = (f32[2,128,128]{2,1,0:T(8,128)S(1)}, f32[2,128,128]{2,1,0:T(8,128)S(1)}, u32[]{:S(2)}, u32[]{:S(2)}) collective-permute-start(f32[2,128,128]{2,1,0:T(8,128)S(1)} %get-tuple-element.92), channel_id=1, source_target_pairs={{0,1},{1,0},{2,3},{3,2},{4,5},{5,4},{6,7},{7,6},{8,9},{9,8},{10,11... | collective-permute-start | bytes 393224 | tf_op jit(solution)/shard_map/ppermute | solution.py:516
  47.9 17.0 %collective-permute-start.28 = (f32[2,512,128]{2,1,0:T(8,128)S(1)}, f32[2,512,128]{2,1,0:T(8,128)S(1)}, u32[]{:S(2)}, u32[]{:S(2)}) collective-permute-start(f32[2,512,128]{2,1,0:T(8,128)S(1)} %get-tuple-element.104), channel_id=1, source_target_pairs={{0,4},{4,0},{1,5},{5,1},{2,6},{6,2},{3,7},{7,3},{8,12},{12,8},{9,1... | collective-permute-start | bytes 1572872 | tf_op jit(solution)/shard_map/ppermute | solution.py:168
  54.1 6.3 %collective-permute-start.26 = (f32[2,128,128]{2,1,0:T(8,128)S(1)}, f32[2,128,128]{2,1,0:T(8,128)S(1)}, u32[]{:S(2)}, u32[]{:S(2)}) collective-permute-start(f32[2,128,128]{2,1,0:T(8,128)S(1)} %get-tuple-element.98.refs_3_), channel_id=1, source_target_pairs={{0,2},{1,3},{2,0},{3,1},{4,6},{5,7},{6,4},{7,5},{8,10},{9,11},{10,... | collective-permute-start | bytes 393224 | tf_op jit(solution)/shard_map/ppermute | solution.py:516
  56.4 6.3 %collective-permute-start.24 = (f32[2,128,128]{2,1,0:T(8,128)S(1)}, f32[2,128,128]{2,1,0:T(8,128)S(1)}, u32[]{:S(2)}, u32[]{:S(2)}) collective-permute-start(f32[2,128,128]{2,1,0:T(8,128)S(1)} %get-tuple-element.99), channel_id=1, source_target_pairs={{0,3},{1,2},{2,1},{3,0},{4,7},{5,6},{6,5},{7,4},{8,11},{9,10},{10,... | collective-permute-start | bytes 393224 | tf_op jit(solution)/shard_map/ppermute | solution.py:516
  57.0 5.7 %collective-permute-start.25 = (f32[2,128,128]{2,1,0:T(8,128)S(1)}, f32[2,128,128]{2,1,0:T(8,128)S(1)}, u32[]{:S(2)}, u32[]{:S(2)}) collective-permute-start(f32[2,128,128]{2,1,0:T(8,128)S(1)} %get-tuple-element.100), channel_id=1, source_target_pairs={{0,1},{1,0},{2,3},{3,2},{4,5},{5,4},{6,7},{7,6},{8,9},{9,8},{10,11... | collective-permute-start | bytes 393224 | tf_op jit(solution)/shard_map/ppermute | solution.py:516
  63.5 9.2 %collective-permute-start.32 = (f32[512,128]{1,0:T(8,128)S(1)}, f32[512,128]{1,0:T(8,128)S(1)}, u32[]{:S(2)}, u32[]{:S(2)}) collective-permute-start(f32[512,128]{1,0:T(8,128)S(1)} %get-tuple-element.109), channel_id=1, source_target_pairs={{0,4},{4,0},{1,5},{5,1},{2,6},{6,2},{3,7},{7,3},{8,12},{12,8},{9,1... | collective-permute-start | bytes 786440 | tf_op jit(solution)/shard_map/ppermute | solution.py:168
  65.2 5.5 %collective-permute-start.31 = (f32[2,128,128]{2,1,0:T(8,128)S(1)}, f32[2,128,128]{2,1,0:T(8,128)S(1)}, u32[]{:S(2)}, u32[]{:S(2)}) collective-permute-start(f32[2,128,128]{2,1,0:T(8,128)S(1)} %shard_map.103.refs_4_), channel_id=1, source_target_pairs={{0,2},{1,3},{2,0},{3,1},{4,6},{5,7},{6,4},{7,5},{8,10},{9,11},{10,... | collective-permute-start | bytes 393224 | tf_op jit(solution)/shard_map/ppermute | solution.py:516
  66.1 11.4 %collective-permute-start.27 = (f32[512,128]{1,0:T(8,128)S(1)}, f32[512,128]{1,0:T(8,128)S(1)}, u32[]{:S(2)}, u32[]{:S(2)}) collective-permute-start(f32[512,128]{1,0:T(8,128)S(1)} %get-tuple-element.103), channel_id=1, source_target_pairs={{0,4},{4,0},{1,5},{5,1},{2,6},{6,2},{3,7},{7,3},{8,12},{12,8},{9,1... | collective-permute-start | bytes 786440 | tf_op jit(solution)/shard_map/ppermute | solution.py:168
  68.0 7.3 %collective-permute-start.29 = (f32[2,128,128]{2,1,0:T(8,128)S(1)}, f32[2,128,128]{2,1,0:T(8,128)S(1)}, u32[]{:S(2)}, u32[]{:S(2)}) collective-permute-start(f32[2,128,128]{2,1,0:T(8,128)S(1)} %get-tuple-element.106), channel_id=1, source_target_pairs={{0,3},{1,2},{2,1},{3,0},{4,7},{5,6},{6,5},{7,4},{8,11},{9,10},{10,... | collective-permute-start | bytes 393224 | tf_op jit(solution)/shard_map/ppermute | solution.py:516
  68.0 8.3 %collective-permute-start.30 = (f32[2,128,128]{2,1,0:T(8,128)S(1)}, f32[2,128,128]{2,1,0:T(8,128)S(1)}, u32[]{:S(2)}, u32[]{:S(2)}) collective-permute-start(f32[2,128,128]{2,1,0:T(8,128)S(1)} %get-tuple-element.107), channel_id=1, source_target_pairs={{0,1},{1,0},{2,3},{3,2},{4,5},{5,4},{6,7},{7,6},{8,9},{9,8},{10,11... | collective-permute-start | bytes 393224 | tf_op jit(solution)/shard_map/ppermute | solution.py:516
  73.2 7.9 %collective-permute-start.36 = (f32[128,128]{1,0:T(8,128)S(1)}, f32[128,128]{1,0:T(8,128)S(1)}, u32[]{:S(2)}, u32[]{:S(2)}) collective-permute-start(f32[128,128]{1,0:T(8,128)S(1)} %shard_map.106.refs_4_), channel_id=1, source_target_pairs={{0,2},{1,3},{2,0},{3,1},{4,6},{5,7},{6,4},{7,5},{8,10},{9,11},{10,... | collective-permute-start | bytes 196616 | tf_op jit(solution)/shard_map/ppermute | solution.py:516
  75.2 5.8 %collective-permute-start.38 = (f32[128,128]{1,0:T(8,128)S(1)}, f32[128,128]{1,0:T(8,128)S(1)}, u32[]{:S(2)}, u32[]{:S(2)}) collective-permute-start(f32[128,128]{1,0:T(8,128)S(1)} %get-tuple-element.115), channel_id=1, source_target_pairs={{0,1},{1,0},{2,3},{3,2},{4,5},{5,4},{6,7},{7,6},{8,9},{9,8},{10,11... | collective-permute-start | bytes 196616 | tf_op jit(solution)/shard_map/ppermute | solution.py:516
  77.9 6.1 %collective-permute-start.33 = (f32[128,128]{1,0:T(8,128)S(1)}, f32[128,128]{1,0:T(8,128)S(1)}, u32[]{:S(2)}, u32[]{:S(2)}) collective-permute-start(f32[128,128]{1,0:T(8,128)S(1)} %shard_map.109.refs_4_), channel_id=1, source_target_pairs={{0,2},{1,3},{2,0},{3,1},{4,6},{5,7},{6,4},{7,5},{8,10},{9,11},{10,... | collective-permute-start | bytes 196616 | tf_op jit(solution)/shard_map/ppermute | solution.py:516
  84.5 7.5 %collective-permute-start.39 = (f32[256,128]{1,0:T(8,128)S(1)}, f32[256,128]{1,0:T(8,128)S(1)}, u32[]{:S(2)}, u32[]{:S(2)}) collective-permute-start(f32[256,128]{1,0:T(8,128)S(1)} %shard_map.112.refs_11_.refs_0_), channel_id=1, source_target_pairs={{0,8},{8,0},{16,24},{24,16},{1,9},{9,1},{17,25},{25,17},{2,10},{10... | collective-permute-start | bytes 393224 | tf_op jit(solution)/shard_map/ppermute | solution.py:574
  92.0 8.3 %collective-permute-start.43 = (f32[264,128]{1,0:T(8,128)S(1)}, f32[264,128]{1,0:T(8,128)S(1)}, u32[]{:S(2)}, u32[]{:S(2)}) collective-permute-start(f32[264,128]{1,0:T(8,128)S(1)} %shard_map.115.refs_0_.refs_2_), channel_id=1, source_target_pairs={{0,16},{8,24},{16,0},{24,8},{1,17},{9,25},{17,1},{25,9},{2,18},{10... | collective-permute-start | bytes 405512 | tf_op jit(solution)/shard_map/ppermute | solution.py:574
  (24 other events, 100.2 us)

commit v6 on v4

--- a/solution.py
+++ b/solution.py
@@ -159,7 +159,7 @@
 
 
 def turns(size):
-    return sorted(range(size), key=lambda d: (d == 1, d))
+    return sorted(range(size), key=lambda d: (d == 1, d > 0, -d))
 
 
 def send(blocks, axis, size):

time: 105 us -> 107 us (1.019)
  waiting for transfers between devices: 38.6 us -> 42.5 us
  starting transfers between devices: 35.8 us -> 33.8 us
    ppermute x21, waiting for transfers between devices: 16.7 us -> 19.7 us  [turn_block(): return lax.ppermute(value, 'lat', [(i, i ^ d) for i in range(lat)])]
    ppermute x21, starting transfers between devices: 15.5 us -> 13.8 us  [turn_block(): return lax.ppermute(value, 'lat', [(i, i ^ d) for i in range(lat)])]
    ppermute x3, waiting for transfers between devices: 10.9 us -> 12.3 us  [across(): return lax.ppermute(value, 'freq', [(i, i ^ d) for i in range(freqs)])]
where the time goes in v6:
time: 107 us; the launch traced here: 106 us
  waiting for transfers between devices  42.5 us (40%)
  starting transfers between devices  33.8 us (32%)
  Pallas kernels  27.7 us (26%)
  local copies, waits for them, and re-layouts  1.37 us (1%)
  between operations  1.1 us (1%)
    pallas_call x39, Pallas kernels, call(): pl.pallas_call(ordered, grid=(1,), out_shape=outs, in_specs=list(specs) +...  27.7 us
    ppermute x21, waiting for transfers between devices, turn_block(): return lax.ppermute(value, 'lat', [(i, i ^ d) for i in range(lat)])  19.7 us
    ppermute x18, starting transfers between devices, send(): got.append(lax.ppermute(block, axis, [(i, i ^ d) for i in range(size)]))  15.5 us
    ppermute x21, starting transfers between devices, turn_block(): return lax.ppermute(value, 'lat', [(i, i ^ d) for i in range(lat)])  13.8 us
    ppermute x3, waiting for transfers between devices, across(): return lax.ppermute(value, 'freq', [(i, i ^ d) for i in range(freqs)])  12.3 us
    ppermute x18, waiting for transfers between devices, send(): got.append(lax.ppermute(block, axis, [(i, i ^ d) for i in range(size)]))  10.5 us
    ppermute x3, starting transfers between devices, across(): return lax.ppermute(value, 'freq', [(i, i ^ d) for i in range(freqs)])  4.45 us
  transfers between devices with their start and end apart: 42, of which 17 were waited for; matrix products, arithmetic and copies ran while one was open for 0% of the time, Pallas kernels for 22%

profile of v6, /device:TPU:0, one launch (start us, length us, event | category | flops | bytes accessed | tf_op | source)
XLA Modules:
  0.0 106.4 jit_solution(1152742052307430263)
XLA Ops:
  0.7 3.4 %shard_map.77 = (f32[128,128]{1,0:T(8,128)}, f32[128,128]{1,0:T(8,128)}, f32[128,128]{1,0:T(8,128)}, f32[128,128]{1,0:T(8,128)}, f32[128,128]{1,0:T(8,128)}, /*i...) custom-call(f32[2,2,128,512]{3,2,1,0:T(8,128)} %bitcast.6, f32[2,128,512]{2,1,0:T(8,128)} %bitcast.13, ...), custom_call_target="tpu_custom_call" | custom-call | flops 805306368 | bytes 1048576 | tf_op jit(solution)/shard_map/pallas_call | solution.py:137
  4.1 2.5 %collective-permute-start.2 = (f32[128,128]{1,0:T(8,128)}, f32[128,128]{1,0:T(8,128)S(1)}, u32[]{:S(2)}, u32[]{:S(2)}) collective-permute-start(f32[128,128]{1,0:T(8,128)} %get-tuple-element.62), channel_id=1, source_target_pairs={{0,3},{1,2},{2,1},{3,0},{4,7},{5,6},{6,5},{7,4},{8,11},{9,10},{10,... | collective-permute-start | bytes 196616 | tf_op jit(solution)/shard_map/ppermute | solution.py:168
  7.3 1.7 %collective-permute-start.6 = (f32[128,128]{1,0:T(8,128)}, f32[128,128]{1,0:T(8,128)S(1)}, u32[]{:S(2)}, u32[]{:S(2)}) collective-permute-start(f32[128,128]{1,0:T(8,128)} %get-tuple-element.70), channel_id=1, source_target_pairs={{0,2},{1,3},{2,0},{3,1},{4,6},{5,7},{6,4},{7,5},{8,10},{9,11},{10,... | collective-permute-start | bytes 196616 | tf_op jit(solution)/shard_map/ppermute | solution.py:168
  13.2 1.8 %collective-permute-start.10 = (f32[512,128]{1,0:T(8,128)S(1)}, f32[512,128]{1,0:T(8,128)S(1)}, u32[]{:S(2)}, u32[]{:S(2)}) collective-permute-start(f32[512,128]{1,0:T(8,128)S(1)} %get-tuple-element.77), channel_id=1, source_target_pairs={{0,4},{4,0},{1,5},{5,1},{2,6},{6,2},{3,7},{7,3},{8,12},{12,8},{9,1... | collective-permute-start | bytes 786440 | tf_op jit(solution)/shard_map/ppermute | solution.py:168
  14.9 1.0 shard_map.82
  16.0 1.6 %collective-permute-start.3 = (f32[2,128,128]{2,1,0:T(8,128)S(1)}, f32[2,128,128]{2,1,0:T(8,128)S(1)}, u32[]{:S(2)}, u32[]{:S(2)}) collective-permute-start(f32[2,128,128]{2,1,0:T(8,128)S(1)} %get-tuple-element.66), channel_id=1, source_target_pairs={{0,2},{1,3},{2,0},{3,1},{4,6},{5,7},{6,4},{7,5},{8,10},{9,11},{10,... | collective-permute-start | bytes 393224 | tf_op jit(solution)/shard_map/ppermute | solution.py:168
  20.2 3.1 %collective-permute-done.5.refs_1_ = f32[2,128,128]{2,1,0:T(8,128)S(1)} collective-permute-done((f32[2,128,128]{2,1,0:T(8,128)S(1)}, f32[2,128,128]{2,1,0:T(8,128)S(1)}, u32[]{:S(2)}, u32[]{:S(2)}) %collective-permute-start.5) | collective-permute-done | bytes 131104 | tf_op jit(solution)/shard_map/ppermute | solution.py:168
  25.2 2.7 %collective-permute-done.11.refs_3_ = f32[512,128]{1,0:T(8,128)S(1)} collective-permute-done((f32[512,128]{1,0:T(8,128)S(1)}, f32[512,128]{1,0:T(8,128)S(1)}, u32[]{:S(2)}, u32[]{:S(2)}) %collective-permute-start.11) | collective-permute-done | bytes 262176 | tf_op jit(solution)/shard_map/ppermute | solution.py:168
  29.8 1.3 %collective-permute-start.12 = (f32[2,128,128]{2,1,0:T(8,128)S(1)}, f32[2,128,128]{2,1,0:T(8,128)S(1)}, u32[]{:S(2)}, u32[]{:S(2)}) collective-permute-start(f32[2,128,128]{2,1,0:T(8,128)S(1)} %get-tuple-element.79), channel_id=1, source_target_pairs={{0,2},{1,3},{2,0},{3,1},{4,6},{5,7},{6,4},{7,5},{8,10},{9,11},{10,... | collective-permute-start | bytes 393224 | tf_op jit(solution)/shard_map/ppermute | solution.py:531
  31.4 2.8 %collective-permute-done.14.refs_1_ = f32[2,128,128]{2,1,0:T(8,128)S(1)} collective-permute-done((f32[2,128,128]{2,1,0:T(8,128)S(1)}, f32[2,128,128]{2,1,0:T(8,128)S(1)}, u32[]{:S(2)}, u32[]{:S(2)}) %collective-permute-start.14) | collective-permute-done | bytes 131104 | tf_op jit(solution)/shard_map/ppermute | solution.py:531
  34.8 2.3 %collective-permute-done.12.refs_0_ = f32[2,128,128]{2,1,0:T(8,128)S(1)} collective-permute-done((f32[2,128,128]{2,1,0:T(8,128)S(1)}, f32[2,128,128]{2,1,0:T(8,128)S(1)}, u32[]{:S(2)}, u32[]{:S(2)}) %collective-permute-start.12) | collective-permute-done | bytes 131104 | tf_op jit(solution)/shard_map/ppermute | solution.py:531
  37.1 1.3 %shard_map.90 = (f32[2,128,128]{2,1,0:T(8,128)S(1)}, f32[2,128,512]{2,1,0:T(8,128)S(1)}) custom-call(f32[2,128,128]{2,1,0:T(8,128)S(1)} %collective-permute-done.12.refs_0_, f32[2,128,128]{2,1,0:T(8,128)S(1)} %collective-permute-done.13.refs_1_, f32[2,128,512]{2,1,0:T(8,128)S(1)} %shard_map.89.refs_2_.refs_7_, f32[2,2,128,512]{3,2,1,0:T(8,128)S(1)} %bitcast.8, ...), custom_call_target="tpu_custom_call" | custom-call | flops 805306368 | bytes 1310720 | tf_op jit(solution)/shard_map/pallas_call | solution.py:137
  39.9 1.1 %collective-permute-start.18 = (f32[2,128,128]{2,1,0:T(8,128)S(1)}, f32[2,128,128]{2,1,0:T(8,128)S(1)}, u32[]{:S(2)}, u32[]{:S(2)}) collective-permute-start(f32[2,128,128]{2,1,0:T(8,128)S(1)} %get-tuple-element.88), channel_id=1, source_target_pairs={{0,2},{1,3},{2,0},{3,1},{4,6},{5,7},{6,4},{7,5},{8,10},{9,11},{10,... | collective-permute-start | bytes 393224 | tf_op jit(solution)/shard_map/ppermute | solution.py:531
  43.4 1.3 %collective-permute-start.15 = (f32[2,128,128]{2,1,0:T(8,128)S(1)}, f32[2,128,128]{2,1,0:T(8,128)S(1)}, u32[]{:S(2)}, u32[]{:S(2)}) collective-permute-start(f32[2,128,128]{2,1,0:T(8,128)S(1)} %get-tuple-element.85), channel_id=1, source_target_pairs={{0,2},{1,3},{2,0},{3,1},{4,6},{5,7},{6,4},{7,5},{8,10},{9,11},{10,... | collective-permute-start | bytes 393224 | tf_op jit(solution)/shard_map/ppermute | solution.py:531
  45.3 2.0 %collective-permute-done.18.refs_0_ = f32[2,128,128]{2,1,0:T(8,128)S(1)} collective-permute-done((f32[2,128,128]{2,1,0:T(8,128)S(1)}, f32[2,128,128]{2,1,0:T(8,128)S(1)}, u32[]{:S(2)}, u32[]{:S(2)}) %collective-permute-start.18) | collective-permute-done | bytes 131104 | tf_op jit(solution)/shard_map/ppermute | solution.py:531
  50.3 2.4 %collective-permute-done.15.refs_0_ = f32[2,128,128]{2,1,0:T(8,128)S(1)} collective-permute-done((f32[2,128,128]{2,1,0:T(8,128)S(1)}, f32[2,128,128]{2,1,0:T(8,128)S(1)}, u32[]{:S(2)}, u32[]{:S(2)}) %collective-permute-start.15) | collective-permute-done | bytes 131104 | tf_op jit(solution)/shard_map/ppermute | solution.py:531
  52.7 1.3 %shard_map.97 = (f32[2,128,128]{2,1,0:T(8,128)S(1)}, f32[2,128,512]{2,1,0:T(8,128)S(1)}) custom-call(f32[2,128,128]{2,1,0:T(8,128)S(1)} %collective-permute-done.15.refs_0_, f32[2,128,128]{2,1,0:T(8,128)S(1)} %collective-permute-done.16.refs_1_, f32[2,128,512]{2,1,0:T(8,128)S(1)} %shard_map.96.refs_2_.refs_7_, f32[2,2,128,512]{3,2,1,0:T(8,128)S(1)} %bitcast.9, ...), custom_call_target="tpu_custom_call" | custom-call | flops 805306368 | bytes 1310720 | tf_op jit(solution)/shard_map/pallas_call | solution.py:137
  54.9 1.6 %collective-permute-start.21 = (f32[2,128,128]{2,1,0:T(8,128)S(1)}, f32[2,128,128]{2,1,0:T(8,128)S(1)}, u32[]{:S(2)}, u32[]{:S(2)}) collective-permute-start(f32[2,128,128]{2,1,0:T(8,128)S(1)} %get-tuple-element.93), channel_id=1, source_target_pairs={{0,2},{1,3},{2,0},{3,1},{4,6},{5,7},{6,4},{7,5},{8,10},{9,11},{10,... | collective-permute-start | bytes 393224 | tf_op jit(solution)/shard_map/ppermute | solution.py:531
  56.8 3.0 %collective-permute-done.23.refs_1_ = f32[2,128,128]{2,1,0:T(8,128)S(1)} collective-permute-done((f32[2,128,128]{2,1,0:T(8,128)S(1)}, f32[2,128,128]{2,1,0:T(8,128)S(1)}, u32[]{:S(2)}, u32[]{:S(2)}) %collective-permute-start.23) | collective-permute-done | bytes 131104 | tf_op jit(solution)/shard_map/ppermute | solution.py:531
  60.3 2.3 %collective-permute-done.21.refs_0_ = f32[2,128,128]{2,1,0:T(8,128)S(1)} collective-permute-done((f32[2,128,128]{2,1,0:T(8,128)S(1)}, f32[2,128,128]{2,1,0:T(8,128)S(1)}, u32[]{:S(2)}, u32[]{:S(2)}) %collective-permute-start.21) | collective-permute-done | bytes 131104 | tf_op jit(solution)/shard_map/ppermute | solution.py:531
  64.9 1.2 %collective-permute-start.24 = (f32[512,128]{1,0:T(8,128)S(1)}, f32[512,128]{1,0:T(8,128)S(1)}, u32[]{:S(2)}, u32[]{:S(2)}) collective-permute-start(f32[512,128]{1,0:T(8,128)S(1)} %get-tuple-element.97), channel_id=1, source_target_pairs={{0,4},{4,0},{1,5},{5,1},{2,6},{6,2},{3,7},{7,3},{8,12},{12,8},{9,1... | collective-permute-start | bytes 786440 | tf_op jit(solution)/shard_map/ppermute | solution.py:168
  66.9 1.4 %collective-permute-start.26 = (f32[2,128,128]{2,1,0:T(8,128)S(1)}, f32[2,128,128]{2,1,0:T(8,128)S(1)}, u32[]{:S(2)}, u32[]{:S(2)}) collective-permute-start(f32[2,128,128]{2,1,0:T(8,128)S(1)} %get-tuple-element.100), channel_id=1, source_target_pairs={{0,2},{1,3},{2,0},{3,1},{4,6},{5,7},{6,4},{7,5},{8,10},{9,11},{10,... | collective-permute-start | bytes 393224 | tf_op jit(solution)/shard_map/ppermute | solution.py:531
  68.5 2.1 %collective-permute-done.28.refs_1_ = f32[2,128,128]{2,1,0:T(8,128)S(1)} collective-permute-done((f32[2,128,128]{2,1,0:T(8,128)S(1)}, f32[2,128,128]{2,1,0:T(8,128)S(1)}, u32[]{:S(2)}, u32[]{:S(2)}) %collective-permute-start.28) | collective-permute-done | bytes 131104 | tf_op jit(solution)/shard_map/ppermute | solution.py:531
  71.2 1.5 %collective-permute-done.29.refs_1_ = f32[512,128]{1,0:T(8,128)S(1)} collective-permute-done((f32[512,128]{1,0:T(8,128)S(1)}, f32[512,128]{1,0:T(8,128)S(1)}, u32[]{:S(2)}, u32[]{:S(2)}) %collective-permute-start.29) | collective-permute-done | bytes 262176 | tf_op jit(solution)/shard_map/ppermute | solution.py:168
  74.6 1.4 %collective-permute-start.35 = (f32[128,128]{1,0:T(8,128)S(1)}, f32[128,128]{1,0:T(8,128)S(1)}, u32[]{:S(2)}, u32[]{:S(2)}) collective-permute-start(f32[128,128]{1,0:T(8,128)S(1)} %get-tuple-element.109), channel_id=1, source_target_pairs={{0,1},{1,0},{2,3},{3,2},{4,5},{5,4},{6,7},{7,6},{8,9},{9,8},{10,11... | collective-permute-start | bytes 196616 | tf_op jit(solution)/shard_map/ppermute | solution.py:531
  81.4 1.8 %collective-permute-done.31.refs_2_ = f32[128,128]{1,0:T(8,128)S(1)} collective-permute-done((f32[128,128]{1,0:T(8,128)S(1)}, f32[128,128]{1,0:T(8,128)S(1)}, u32[]{:S(2)}, u32[]{:S(2)}) %collective-permute-start.31) | collective-permute-done | bytes 65568 | tf_op jit(solution)/shard_map/ppermute | solution.py:531
  83.7 1.7 %collective-permute-start.36 = (f32[256,128]{1,0:T(8,128)S(1)}, f32[256,128]{1,0:T(8,128)S(1)}, u32[]{:S(2)}, u32[]{:S(2)}) collective-permute-start(f32[256,128]{1,0:T(8,128)S(1)} %shard_map.110.refs_11_.refs_0_), channel_id=1, source_target_pairs={{0,8},{8,0},{16,24},{24,16},{1,9},{9,1},{17,25},{25,17},{2,10},{10... | collective-permute-start | bytes 393224 | tf_op jit(solution)/shard_map/ppermute | solution.py:590
  86.3 1.2 %collective-permute-start.38 = (f32[8,128]{1,0:T(8,128)S(1)}, f32[8,128]{1,0:T(8,128)S(1)}, u32[]{:S(2)}, u32[]{:S(2)}) collective-permute-start(f32[8,128]{1,0:T(8,128)S(1)} %shard_map.112.refs_2_.refs_6_), channel_id=1, source_target_pairs={{0,2},{1,3},{2,0},{3,1},{4,6},{5,7},{6,4},{7,5},{8,10},{9,11},{10,... | collective-permute-start | bytes 12296 | tf_op jit(solution)/shard_map/ppermute | solution.py:168
  88.2 1.8 %collective-permute-done.38.refs_4_ = f32[8,128]{1,0:T(8,128)S(1)} collective-permute-done((f32[8,128]{1,0:T(8,128)S(1)}, f32[8,128]{1,0:T(8,128)S(1)}, u32[]{:S(2)}, u32[]{:S(2)}) %collective-permute-start.38) | collective-permute-done | bytes 4128 | tf_op jit(solution)/shard_map/ppermute | solution.py:168
  90.6 2.7 %collective-permute-start.40 = (f32[264,128]{1,0:T(8,128)S(1)}, f32[264,128]{1,0:T(8,128)S(1)}, u32[]{:S(2)}, u32[]{:S(2)}) collective-permute-start(f32[264,128]{1,0:T(8,128)S(1)} %shard_map.113.refs_0_.refs_2_), channel_id=1, source_target_pairs={{0,16},{8,24},{16,0},{24,8},{1,17},{9,25},{17,1},{25,9},{2,18},{10... | collective-permute-start | bytes 405512 | tf_op jit(solution)/shard_map/ppermute | solution.py:590
  93.3 6.8 %collective-permute-done.40.refs_1_ = f32[264,128]{1,0:T(8,128)S(1)} collective-permute-done((f32[264,128]{1,0:T(8,128)S(1)}, f32[264,128]{1,0:T(8,128)S(1)}, u32[]{:S(2)}, u32[]{:S(2)}) %collective-permute-start.40) | collective-permute-done | bytes 135200 | tf_op jit(solution)/shard_map/ppermute | solution.py:590
  100.2 5.5 %collective-permute-done.41.refs_1_ = f32[264,128]{1,0:T(8,128)S(1)} collective-permute-done((f32[264,128]{1,0:T(8,128)S(1)}, f32[264,128]{1,0:T(8,128)S(1)}, u32[]{:S(2)}, u32[]{:S(2)}) %collective-permute-start.41) | collective-permute-done | bytes 135200 | tf_op jit(solution)/shard_map/ppermute | solution.py:590
  (109 shorter events, 35.5 us)
Async XLA Ops:
  4.1 6.7 %collective-permute-start.2 = (f32[128,128]{1,0:T(8,128)}, f32[128,128]{1,0:T(8,128)S(1)}, u32[]{:S(2)}, u32[]{:S(2)}) collective-permute-start(f32[128,128]{1,0:T(8,128)} %get-tuple-element.62), channel_id=1, source_target_pairs={{0,3},{1,2},{2,1},{3,0},{4,7},{5,6},{6,5},{7,4},{8,11},{9,10},{10,... | collective-permute-start | bytes 196616 | tf_op jit(solution)/shard_map/ppermute | solution.py:168
  6.6 5.8 %collective-permute-start = (f32[128,128]{1,0:T(8,128)}, f32[128,128]{1,0:T(8,128)S(1)}, u32[]{:S(2)}, u32[]{:S(2)}) collective-permute-start(f32[128,128]{1,0:T(8,128)} %get-tuple-element.60), channel_id=1, source_target_pairs={{0,2},{1,3},{2,0},{3,1},{4,6},{5,7},{6,4},{7,5},{8,10},{9,11},{10,... | collective-permute-start | bytes 196616 | tf_op jit(solution)/shard_map/ppermute | solution.py:168
  7.3 10.9 %collective-permute-start.6 = (f32[128,128]{1,0:T(8,128)}, f32[128,128]{1,0:T(8,128)S(1)}, u32[]{:S(2)}, u32[]{:S(2)}) collective-permute-start(f32[128,128]{1,0:T(8,128)} %get-tuple-element.70), channel_id=1, source_target_pairs={{0,2},{1,3},{2,0},{3,1},{4,6},{5,7},{6,4},{7,5},{8,10},{9,11},{10,... | collective-permute-start | bytes 196616 | tf_op jit(solution)/shard_map/ppermute | solution.py:168
  9.0 9.9 %collective-permute-start.7 = (f32[128,128]{1,0:T(8,128)}, f32[128,128]{1,0:T(8,128)S(1)}, u32[]{:S(2)}, u32[]{:S(2)}) collective-permute-start(f32[128,128]{1,0:T(8,128)} %get-tuple-element.71), channel_id=1, source_target_pairs={{0,1},{1,0},{2,3},{3,2},{4,5},{5,4},{6,7},{7,6},{8,9},{9,8},{10,11... | collective-permute-start | bytes 196616 | tf_op jit(solution)/shard_map/ppermute | solution.py:168
  11.3 6.2 %collective-permute-start.8 = (f32[128,128]{1,0:T(8,128)S(1)}, f32[128,128]{1,0:T(8,128)S(1)}, u32[]{:S(2)}, u32[]{:S(2)}) collective-permute-start(f32[128,128]{1,0:T(8,128)S(1)} %copy-done.8), channel_id=1, source_target_pairs={{0,3},{1,2},{2,1},{3,0},{4,7},{5,6},{6,5},{7,4},{8,11},{9,10},{10,... | collective-permute-start | bytes 196616 | tf_op jit(solution)/shard_map/ppermute | solution.py:168
  13.2 12.0 %collective-permute-start.10 = (f32[512,128]{1,0:T(8,128)S(1)}, f32[512,128]{1,0:T(8,128)S(1)}, u32[]{:S(2)}, u32[]{:S(2)}) collective-permute-start(f32[512,128]{1,0:T(8,128)S(1)} %get-tuple-element.77), channel_id=1, source_target_pairs={{0,4},{4,0},{1,5},{5,1},{2,6},{6,2},{3,7},{7,3},{8,12},{12,8},{9,1... | collective-permute-start | bytes 786440 | tf_op jit(solution)/shard_map/ppermute | solution.py:168
  16.0 8.0 %collective-permute-start.3 = (f32[2,128,128]{2,1,0:T(8,128)S(1)}, f32[2,128,128]{2,1,0:T(8,128)S(1)}, u32[]{:S(2)}, u32[]{:S(2)}) collective-permute-start(f32[2,128,128]{2,1,0:T(8,128)S(1)} %get-tuple-element.66), channel_id=1, source_target_pairs={{0,2},{1,3},{2,0},{3,1},{4,6},{5,7},{6,4},{7,5},{8,10},{9,11},{10,... | collective-permute-start | bytes 393224 | tf_op jit(solution)/shard_map/ppermute | solution.py:168
  17.5 5.8 %collective-permute-start.5 = (f32[2,128,128]{2,1,0:T(8,128)S(1)}, f32[2,128,128]{2,1,0:T(8,128)S(1)}, u32[]{:S(2)}, u32[]{:S(2)}) collective-permute-start(f32[2,128,128]{2,1,0:T(8,128)S(1)} %get-tuple-element.69), channel_id=1, source_target_pairs={{0,3},{1,2},{2,1},{3,0},{4,7},{5,6},{6,5},{7,4},{8,11},{9,10},{10,... | collective-permute-start | bytes 393224 | tf_op jit(solution)/shard_map/ppermute | solution.py:168
  19.6 8.3 %collective-permute-start.11 = (f32[512,128]{1,0:T(8,128)S(1)}, f32[512,128]{1,0:T(8,128)S(1)}, u32[]{:S(2)}, u32[]{:S(2)}) collective-permute-start(f32[512,128]{1,0:T(8,128)S(1)} %get-tuple-element.78), channel_id=1, source_target_pairs={{0,4},{4,0},{1,5},{5,1},{2,6},{6,2},{3,7},{7,3},{8,12},{12,8},{9,1... | collective-permute-start | bytes 786440 | tf_op jit(solution)/shard_map/ppermute | solution.py:168
  24.6 16.6 %collective-permute-start.9 = (f32[2,512,128]{2,1,0:T(8,128)S(1)}, f32[2,512,128]{2,1,0:T(8,128)S(1)}, u32[]{:S(2)}, u32[]{:S(2)}) collective-permute-start(f32[2,512,128]{2,1,0:T(8,128)S(1)} %get-tuple-element.76), channel_id=1, source_target_pairs={{0,4},{4,0},{1,5},{5,1},{2,6},{6,2},{3,7},{7,3},{8,12},{12,8},{9,1... | collective-permute-start | bytes 1572872 | tf_op jit(solution)/shard_map/ppermute | solution.py:168
  28.5 5.8 %collective-permute-start.14 = (f32[2,128,128]{2,1,0:T(8,128)S(1)}, f32[2,128,128]{2,1,0:T(8,128)S(1)}, u32[]{:S(2)}, u32[]{:S(2)}) collective-permute-start(f32[2,128,128]{2,1,0:T(8,128)S(1)} %shard_map.87.refs_6_), channel_id=1, source_target_pairs={{0,3},{1,2},{2,1},{3,0},{4,7},{5,6},{6,5},{7,4},{8,11},{9,10},{10,... | collective-permute-start | bytes 393224 | tf_op jit(solution)/shard_map/ppermute | solution.py:531
  29.8 7.3 %collective-permute-start.12 = (f32[2,128,128]{2,1,0:T(8,128)S(1)}, f32[2,128,128]{2,1,0:T(8,128)S(1)}, u32[]{:S(2)}, u32[]{:S(2)}) collective-permute-start(f32[2,128,128]{2,1,0:T(8,128)S(1)} %get-tuple-element.79), channel_id=1, source_target_pairs={{0,2},{1,3},{2,0},{3,1},{4,6},{5,7},{6,4},{7,5},{8,10},{9,11},{10,... | collective-permute-start | bytes 393224 | tf_op jit(solution)/shard_map/ppermute | solution.py:531
  31.1 6.0 %collective-permute-start.13 = (f32[2,128,128]{2,1,0:T(8,128)S(1)}, f32[2,128,128]{2,1,0:T(8,128)S(1)}, u32[]{:S(2)}, u32[]{:S(2)}) collective-permute-start(f32[2,128,128]{2,1,0:T(8,128)S(1)} %get-tuple-element.80), channel_id=1, source_target_pairs={{0,1},{1,0},{2,3},{3,2},{4,5},{5,4},{6,7},{7,6},{8,9},{9,8},{10,11... | collective-permute-start | bytes 393224 | tf_op jit(solution)/shard_map/ppermute | solution.py:531
  38.4 6.2 %collective-permute-start.20 = (f32[2,128,128]{2,1,0:T(8,128)S(1)}, f32[2,128,128]{2,1,0:T(8,128)S(1)}, u32[]{:S(2)}, u32[]{:S(2)}) collective-permute-start(f32[2,128,128]{2,1,0:T(8,128)S(1)} %get-tuple-element.83.refs_3_), channel_id=1, source_target_pairs={{0,3},{1,2},{2,1},{3,0},{4,7},{5,6},{6,5},{7,4},{8,11},{9,10},{10,... | collective-permute-start | bytes 393224 | tf_op jit(solution)/shard_map/ppermute | solution.py:531
  39.9 7.4 %collective-permute-start.18 = (f32[2,128,128]{2,1,0:T(8,128)S(1)}, f32[2,128,128]{2,1,0:T(8,128)S(1)}, u32[]{:S(2)}, u32[]{:S(2)}) collective-permute-start(f32[2,128,128]{2,1,0:T(8,128)S(1)} %get-tuple-element.88), channel_id=1, source_target_pairs={{0,2},{1,3},{2,0},{3,1},{4,6},{5,7},{6,4},{7,5},{8,10},{9,11},{10,... | collective-permute-start | bytes 393224 | tf_op jit(solution)/shard_map/ppermute | solution.py:531
  41.0 6.3 %collective-permute-start.19 = (f32[2,128,128]{2,1,0:T(8,128)S(1)}, f32[2,128,128]{2,1,0:T(8,128)S(1)}, u32[]{:S(2)}, u32[]{:S(2)}) collective-permute-start(f32[2,128,128]{2,1,0:T(8,128)S(1)} %get-tuple-element.89), channel_id=1, source_target_pairs={{0,1},{1,0},{2,3},{3,2},{4,5},{5,4},{6,7},{7,6},{8,9},{9,8},{10,11... | collective-permute-start | bytes 393224 | tf_op jit(solution)/shard_map/ppermute | solution.py:531
  41.6 8.1 %collective-permute-start.17 = (f32[2,128,128]{2,1,0:T(8,128)S(1)}, f32[2,128,128]{2,1,0:T(8,128)S(1)}, u32[]{:S(2)}, u32[]{:S(2)}) collective-permute-start(f32[2,128,128]{2,1,0:T(8,128)S(1)} %shard_map.92.refs_4_), channel_id=1, source_target_pairs={{0,3},{1,2},{2,1},{3,0},{4,7},{5,6},{6,5},{7,4},{8,11},{9,10},{10,... | collective-permute-start | bytes 393224 | tf_op jit(solution)/shard_map/ppermute | solution.py:531
  43.4 9.3 %collective-permute-start.15 = (f32[2,128,128]{2,1,0:T(8,128)S(1)}, f32[2,128,128]{2,1,0:T(8,128)S(1)}, u32[]{:S(2)}, u32[]{:S(2)}) collective-permute-start(f32[2,128,128]{2,1,0:T(8,128)S(1)} %get-tuple-element.85), channel_id=1, source_target_pairs={{0,2},{1,3},{2,0},{3,1},{4,6},{5,7},{6,4},{7,5},{8,10},{9,11},{10,... | collective-permute-start | bytes 393224 | tf_op jit(solution)/shard_map/ppermute | solution.py:531
  44.7 8.0 %collective-permute-start.16 = (f32[2,128,128]{2,1,0:T(8,128)S(1)}, f32[2,128,128]{2,1,0:T(8,128)S(1)}, u32[]{:S(2)}, u32[]{:S(2)}) collective-permute-start(f32[2,128,128]{2,1,0:T(8,128)S(1)} %get-tuple-element.86), channel_id=1, source_target_pairs={{0,1},{1,0},{2,3},{3,2},{4,5},{5,4},{6,7},{7,6},{8,9},{9,8},{10,11... | collective-permute-start | bytes 393224 | tf_op jit(solution)/shard_map/ppermute | solution.py:531
  48.0 16.4 %collective-permute-start.25 = (f32[2,512,128]{2,1,0:T(8,128)S(1)}, f32[2,512,128]{2,1,0:T(8,128)S(1)}, u32[]{:S(2)}, u32[]{:S(2)}) collective-permute-start(f32[2,512,128]{2,1,0:T(8,128)S(1)} %get-tuple-element.98), channel_id=1, source_target_pairs={{0,4},{4,0},{1,5},{5,1},{2,6},{6,2},{3,7},{7,3},{8,12},{12,8},{9,1... | collective-permute-start | bytes 1572872 | tf_op jit(solution)/shard_map/ppermute | solution.py:168
  54.0 5.8 %collective-permute-start.23 = (f32[2,128,128]{2,1,0:T(8,128)S(1)}, f32[2,128,128]{2,1,0:T(8,128)S(1)}, u32[]{:S(2)}, u32[]{:S(2)}) collective-permute-start(f32[2,128,128]{2,1,0:T(8,128)S(1)} %get-tuple-element.92.refs_3_), channel_id=1, source_target_pairs={{0,3},{1,2},{2,1},{3,0},{4,7},{5,6},{6,5},{7,4},{8,11},{9,10},{10,... | collective-permute-start | bytes 393224 | tf_op jit(solution)/shard_map/ppermute | solution.py:531
  54.9 7.8 %collective-permute-start.21 = (f32[2,128,128]{2,1,0:T(8,128)S(1)}, f32[2,128,128]{2,1,0:T(8,128)S(1)}, u32[]{:S(2)}, u32[]{:S(2)}) collective-permute-start(f32[2,128,128]{2,1,0:T(8,128)S(1)} %get-tuple-element.93), channel_id=1, source_target_pairs={{0,2},{1,3},{2,0},{3,1},{4,6},{5,7},{6,4},{7,5},{8,10},{9,11},{10,... | collective-permute-start | bytes 393224 | tf_op jit(solution)/shard_map/ppermute | solution.py:531
  56.4 6.2 %collective-permute-start.22 = (f32[2,128,128]{2,1,0:T(8,128)S(1)}, f32[2,128,128]{2,1,0:T(8,128)S(1)}, u32[]{:S(2)}, u32[]{:S(2)}) collective-permute-start(f32[2,128,128]{2,1,0:T(8,128)S(1)} %get-tuple-element.94), channel_id=1, source_target_pairs={{0,1},{1,0},{2,3},{3,2},{4,5},{5,4},{6,7},{7,6},{8,9},{9,8},{10,11... | collective-permute-start | bytes 393224 | tf_op jit(solution)/shard_map/ppermute | solution.py:531
  63.5 9.2 %collective-permute-start.29 = (f32[512,128]{1,0:T(8,128)S(1)}, f32[512,128]{1,0:T(8,128)S(1)}, u32[]{:S(2)}, u32[]{:S(2)}) collective-permute-start(f32[512,128]{1,0:T(8,128)S(1)} %get-tuple-element.103), channel_id=1, source_target_pairs={{0,4},{4,0},{1,5},{5,1},{2,6},{6,2},{3,7},{7,3},{8,12},{12,8},{9,1... | collective-permute-start | bytes 786440 | tf_op jit(solution)/shard_map/ppermute | solution.py:168
  64.8 5.8 %collective-permute-start.28 = (f32[2,128,128]{2,1,0:T(8,128)S(1)}, f32[2,128,128]{2,1,0:T(8,128)S(1)}, u32[]{:S(2)}, u32[]{:S(2)}) collective-permute-start(f32[2,128,128]{2,1,0:T(8,128)S(1)} %shard_map.101.refs_4_), channel_id=1, source_target_pairs={{0,3},{1,2},{2,1},{3,0},{4,7},{5,6},{6,5},{7,4},{8,11},{9,10},{10,... | collective-permute-start | bytes 393224 | tf_op jit(solution)/shard_map/ppermute | solution.py:531
  64.9 12.5 %collective-permute-start.24 = (f32[512,128]{1,0:T(8,128)S(1)}, f32[512,128]{1,0:T(8,128)S(1)}, u32[]{:S(2)}, u32[]{:S(2)}) collective-permute-start(f32[512,128]{1,0:T(8,128)S(1)} %get-tuple-element.97), channel_id=1, source_target_pairs={{0,4},{4,0},{1,5},{5,1},{2,6},{6,2},{3,7},{7,3},{8,12},{12,8},{9,1... | collective-permute-start | bytes 786440 | tf_op jit(solution)/shard_map/ppermute | solution.py:168
  66.9 7.6 %collective-permute-start.26 = (f32[2,128,128]{2,1,0:T(8,128)S(1)}, f32[2,128,128]{2,1,0:T(8,128)S(1)}, u32[]{:S(2)}, u32[]{:S(2)}) collective-permute-start(f32[2,128,128]{2,1,0:T(8,128)S(1)} %get-tuple-element.100), channel_id=1, source_target_pairs={{0,2},{1,3},{2,0},{3,1},{4,6},{5,7},{6,4},{7,5},{8,10},{9,11},{10,... | collective-permute-start | bytes 393224 | tf_op jit(solution)/shard_map/ppermute | solution.py:531
  68.3 7.7 %collective-permute-start.27 = (f32[2,128,128]{2,1,0:T(8,128)S(1)}, f32[2,128,128]{2,1,0:T(8,128)S(1)}, u32[]{:S(2)}, u32[]{:S(2)}) collective-permute-start(f32[2,128,128]{2,1,0:T(8,128)S(1)} %get-tuple-element.101), channel_id=1, source_target_pairs={{0,1},{1,0},{2,3},{3,2},{4,5},{5,4},{6,7},{7,6},{8,9},{9,8},{10,11... | collective-permute-start | bytes 393224 | tf_op jit(solution)/shard_map/ppermute | solution.py:531
  73.1 7.5 %collective-permute-start.33 = (f32[128,128]{1,0:T(8,128)S(1)}, f32[128,128]{1,0:T(8,128)S(1)}, u32[]{:S(2)}, u32[]{:S(2)}) collective-permute-start(f32[128,128]{1,0:T(8,128)S(1)} %shard_map.104.refs_4_), channel_id=1, source_target_pairs={{0,3},{1,2},{2,1},{3,0},{4,7},{5,6},{6,5},{7,4},{8,11},{9,10},{10,... | collective-permute-start | bytes 196616 | tf_op jit(solution)/shard_map/ppermute | solution.py:531
  74.6 6.1 %collective-permute-start.35 = (f32[128,128]{1,0:T(8,128)S(1)}, f32[128,128]{1,0:T(8,128)S(1)}, u32[]{:S(2)}, u32[]{:S(2)}) collective-permute-start(f32[128,128]{1,0:T(8,128)S(1)} %get-tuple-element.109), channel_id=1, source_target_pairs={{0,1},{1,0},{2,3},{3,2},{4,5},{5,4},{6,7},{7,6},{8,9},{9,8},{10,11... | collective-permute-start | bytes 196616 | tf_op jit(solution)/shard_map/ppermute | solution.py:531
  83.7 6.9 %collective-permute-start.36 = (f32[256,128]{1,0:T(8,128)S(1)}, f32[256,128]{1,0:T(8,128)S(1)}, u32[]{:S(2)}, u32[]{:S(2)}) collective-permute-start(f32[256,128]{1,0:T(8,128)S(1)} %shard_map.110.refs_11_.refs_0_), channel_id=1, source_target_pairs={{0,8},{8,0},{16,24},{24,16},{1,9},{9,1},{17,25},{25,17},{2,10},{10... | collective-permute-start | bytes 393224 | tf_op jit(solution)/shard_map/ppermute | solution.py:590
  90.6 9.5 %collective-permute-start.40 = (f32[264,128]{1,0:T(8,128)S(1)}, f32[264,128]{1,0:T(8,128)S(1)}, u32[]{:S(2)}, u32[]{:S(2)}) collective-permute-start(f32[264,128]{1,0:T(8,128)S(1)} %shard_map.113.refs_0_.refs_2_), channel_id=1, source_target_pairs={{0,16},{8,24},{16,0},{24,8},{1,17},{9,25},{17,1},{25,9},{2,18},{10... | collective-permute-start | bytes 405512 | tf_op jit(solution)/shard_map/ppermute | solution.py:590
  (19 other events, 76.8 us)
